TPU v7x, 128 devices: a whole 4x4x4 slice. The times are simulated.
128 devices in a mesh: dp: 4 (over z_lo, core), row: 8 (over y, z_hi), col: 4 (over x).
Axes of the slice: x: 4, y: 4, z: 4 (z_hi: 2, z_lo: 2; z = z_hi * 2 + z_lo), core: 2. Of those that a mesh axis runs over, the one named last changes fastest.
Arguments:
- tokens: bfloat16 [16384, 1536], P(('dp', 'row'), 'col'), may hold values from -6 to 6
- positions: int32 [16384], P(('dp', 'col')), may hold values from 0 to 6142, as said below
- attn_gain: float32 [1536], P('col'), may hold values from 0.1 to 1.9
- qkv_weight: bfloat16 [1536, 3072], P('col', 'row'), may hold values from -0.15625 to 0.15625
- output_weight: bfloat16 [1536, 1536], P('row', 'col'), may hold values from -1.25 to 1.25
- ffn_gain: float32 [1536], P('col'), may hold values from 0.1 to 1.9
- gate_weight: bfloat16 [1536, 4096], P('col', 'row'), may hold values from -0.15625 to 0.15625
- up_weight: bfloat16 [1536, 4096], P('col', 'row'), may hold values from -0.15625 to 0.15625
- down_weight: bfloat16 [4096, 1536], P('row', 'col'), may hold values from -0.09375 to 0.09375
- cotangent: bfloat16 [16384, 1536], P(('dp', 'row'), 'col'), may hold values from -6 to 6
Outputs:
- mixed: float32 [16384, 1536], P(('dp', 'row'), 'col')
- tokens_grad: float32 [16384, 1536], P(('dp', 'row'), 'col')
- attn_dgain: float32 [1536], P('col')
- qkv_grad: float32 [1536, 3072], P('col', 'row')
- output_grad: float32 [1536, 1536], P('row', 'col')
- ffn_dgain: float32 [1536], P('col')
- gate_grad: float32 [1536, 4096], P('col', 'row')
- up_grad: float32 [1536, 4096], P('col', 'row')
- down_grad: float32 [4096, 1536], P('row', 'col')
Inputs may be any that keep to these rules, and one draw needn't show every extreme that they name: Within each sequence of 1024 tokens the positions rise by one or two from each token to the next, and a sequence's first position is at most 4096.
All inputs are finite; a program needn't handle non-finite values.
Results may differ from a plain program's by a relative error of at most 0.02.
Values may be sent and summed in bfloat16 or wider, within the bound.
A program may use at most 192 MiB of HBM per device.

v0:
```python
import math

import jax
import jax.numpy as jnp
from jax import lax
from jax.sharding import Mesh
from jax.sharding import PartitionSpec as P

D = 1536
H = 16
KVH = 8
HD = 96
LEN = 1024
ROW = ("row_0", "row_1")
DP_ROW = ("dp", "row_0", "row_1")


epsilon = 1e-05
rope_base = 100000.0
masked_score = -1e30


def gather_axes(x, axes, dim):
    for axis in reversed(axes):
        x = lax.all_gather(x, axis, axis=dim, tiled=True)
    return x


def rope_tables(places, head_size):
    half_size = head_size // 2
    frequency = rope_base ** (-(jnp.arange(half_size, dtype=jnp.float32) * 2.0 / head_size))
    angles = places.astype(jnp.float32)[:, None] * frequency[None, :]
    return (jnp.cos(angles), jnp.sin(angles))


def rotate(vectors, cosine, sine):
    half_size = vectors.shape[-1] // 2
    first_half = vectors[..., :half_size]
    second_half = vectors[..., half_size:]
    return jnp.concatenate(
        [first_half * cosine - second_half * sine, second_half * cosine + first_half * sine],
        axis=-1,
    )


def unrotate(grads, cosine, sine):
    half_size = grads.shape[-1] // 2
    first_half = grads[..., :half_size]
    second_half = grads[..., half_size:]
    return jnp.concatenate(
        [first_half * cosine + second_half * sine, second_half * cosine - first_half * sine],
        axis=-1,
    )


def column_total(values):
    return lax.psum(values, "col")


def norm_forward(source, gain):
    total = column_total(jnp.sum(source * source, axis=1))
    inverse = lax.rsqrt(total / D + epsilon)
    return (source * inverse[:, None] * gain[None, :], inverse)


def norm_backward(d_normed, source, inverse, gain):
    scaled = d_normed * gain[None, :]
    inner = column_total(jnp.sum(scaled * source, axis=1))
    d_source = (
        inverse[:, None] * scaled - source * (inverse * inverse * inverse * inner / D)[:, None]
    )
    d_gain = jnp.sum(d_normed * source * inverse[:, None], axis=0)
    return (d_source, d_gain)


def gather_rows(values):
    return lax.all_gather(values, ROW, axis=0, tiled=True)


def out_project(values, weight):
    gathered = lax.all_gather(values, "col", axis=0, tiled=True)
    term = jnp.dot(gathered, weight, preferred_element_type=jnp.float32)
    return (gathered, lax.psum_scatter(term, ROW, scatter_dimension=0, tiled=True))


def back_out(grads, weight, kept):
    gathered = gather_axes(grads, ROW, 0)
    d_weight = jnp.einsum("tk,tn->kn", kept, gathered, preferred_element_type=jnp.float32)
    term = jnp.einsum("tn,kn->tk", gathered, weight, preferred_element_type=jnp.float32)
    return (d_weight, lax.psum_scatter(term, "col", scatter_dimension=0, tiled=True))


def back_in(grads, weight, kept):
    gathered = lax.all_gather(grads, "col", axis=0, tiled=True)
    d_weight = jnp.einsum("tn,tk->nk", kept, gathered, preferred_element_type=jnp.float32)
    term = jnp.einsum("tk,nk->tn", gathered, weight, preferred_element_type=jnp.float32)
    return (
        d_weight,
        lax.psum_scatter(term.astype(jnp.bfloat16), ROW, scatter_dimension=0, tiled=True).astype(
            jnp.float32
        ),
    )


def block_scores(query_block, key_seq, start):
    scale = 1.0 / math.sqrt(query_block.shape[-1])
    raw = (
        jnp.einsum("qhgd,khd->hgqk", query_block, key_seq, preferred_element_type=jnp.float32)
        * scale
    )
    rows_index = start + jnp.arange(query_block.shape[0], dtype=jnp.int32)
    cols_index = jnp.arange(key_seq.shape[0], dtype=jnp.int32)
    allowed = cols_index[None, :] <= rows_index[:, None]
    return jnp.where(allowed[None, None], raw, masked_score)


def rope_shaped(places, seq_count):
    cosine, sine = rope_tables(places, HD)
    return (cosine.reshape(seq_count, LEN, 1, 1, -1), sine.reshape(seq_count, LEN, 1, 1, -1))


def attention_forward(projected, places):
    count = projected.shape[0]
    seq_count = count // LEN
    group = H // KVH
    shaped = projected.reshape(seq_count, LEN, -1, group + 2, HD)
    cosine, sine = rope_shaped(places, seq_count)
    queries = rotate(shaped[..., :group, :], cosine, sine).astype(jnp.bfloat16)
    keys = rotate(shaped[..., group, :], cosine[..., 0, :], sine[..., 0, :]).astype(jnp.bfloat16)
    values = shaped[..., group + 1, :].astype(jnp.bfloat16)
    block = min(512, LEN)
    blocks = LEN // block
    starts = jnp.arange(blocks, dtype=jnp.int32) * block

    def one_sequence(inputs):
        query_seq, key_seq, value_seq = inputs
        query_blocks = query_seq.reshape(
            blocks, block, query_seq.shape[1], query_seq.shape[2], query_seq.shape[3]
        )

        def one_block(pair):
            query_block, start = pair
            scores = block_scores(query_block, key_seq, start)
            top = jnp.max(scores, axis=-1, keepdims=True)
            exponent = jnp.exp(scores - top)
            totals = jnp.sum(exponent, axis=-1, keepdims=True)
            probs = exponent / totals
            attended = jnp.einsum(
                "hgqk,khd->qhgd",
                probs.astype(jnp.bfloat16),
                value_seq,
                preferred_element_type=jnp.float32,
            )
            return (attended, (top + jnp.log(totals))[..., 0])

        attended, logsum = lax.map(one_block, (query_blocks, starts))
        return (
            attended.reshape(LEN, attended.shape[2], attended.shape[3], attended.shape[4]),
            logsum,
        )

    attended, logsum = lax.map(one_sequence, (queries, keys, values))
    return (attended.reshape(count, -1), logsum, (queries, keys, values))


def attention_backward(d_attended, kept, logsum, places):
    queries, keys, values = kept
    seq_count = queries.shape[0]
    count = seq_count * LEN
    block = min(512, LEN)
    blocks = LEN // block
    starts = jnp.arange(blocks, dtype=jnp.int32) * block
    d_shaped = d_attended.reshape(queries.shape)

    def one_sequence(inputs):
        query_seq, key_seq, value_seq, grad_seq, logsum_seq = inputs
        query_blocks = query_seq.reshape(
            blocks, block, query_seq.shape[1], query_seq.shape[2], query_seq.shape[3]
        )
        grad_blocks = grad_seq.reshape(
            blocks, block, grad_seq.shape[1], grad_seq.shape[2], grad_seq.shape[3]
        )
        scale = 1.0 / math.sqrt(query_seq.shape[-1])

        def one_block(carry, pieces):
            key_total, value_total = carry
            query_block, grad_block, logsum_block, start = pieces
            scores = block_scores(query_block, key_seq, start)
            probs = jnp.exp(scores - logsum_block[..., None])
            d_probs = jnp.einsum(
                "qhgd,khd->hgqk", grad_block, value_seq, preferred_element_type=jnp.float32
            )
            inner = jnp.sum(probs * d_probs, axis=-1, keepdims=True)
            d_scores = (probs * (d_probs - inner) * scale).astype(jnp.bfloat16)
            d_query = jnp.einsum(
                "hgqk,khd->qhgd", d_scores, key_seq, preferred_element_type=jnp.float32
            )
            key_total = key_total + jnp.einsum(
                "hgqk,qhgd->khd", d_scores, query_block, preferred_element_type=jnp.float32
            )
            value_total = value_total + jnp.einsum(
                "hgqk,qhgd->khd",
                probs.astype(jnp.bfloat16),
                grad_block,
                preferred_element_type=jnp.float32,
            )
            return ((key_total, value_total), d_query)

        empty = jnp.zeros(key_seq.shape, jnp.float32)
        totals, d_queries = lax.scan(
            one_block, (empty, empty), (query_blocks, grad_blocks, logsum_seq, starts)
        )
        return (d_queries.reshape(query_seq.shape), totals[0], totals[1])

    d_queries, d_keys, d_values = lax.map(one_sequence, (queries, keys, values, d_shaped, logsum))
    cosine, sine = rope_shaped(places, seq_count)
    d_queries = unrotate(d_queries, cosine, sine)
    d_keys = unrotate(d_keys, cosine[..., 0, :], sine[..., 0, :])
    joined = jnp.concatenate([d_queries, d_keys[..., None, :], d_values[..., None, :]], axis=3)
    return joined.reshape(count, -1).astype(jnp.bfloat16)


def per_device(
    tokens,
    positions,
    attn_gain,
    qkv_weight,
    output_weight,
    ffn_gain,
    gate_weight,
    up_weight,
    down_weight,
    cotangent,
):
    source = tokens.astype(jnp.float32)
    normed, inverse_attn = norm_forward(source, attn_gain)
    attn_rows = gather_rows(normed.astype(jnp.bfloat16))
    projected = lax.psum_scatter(
        jnp.dot(attn_rows, qkv_weight, preferred_element_type=jnp.float32),
        "col",
        scatter_dimension=0,
        tiled=True,
    )
    attended, logsum, kept = attention_forward(projected, positions)
    attended_all, attn_branch = out_project(attended.astype(jnp.bfloat16), output_weight)
    middle = source + attn_branch
    normed_ffn, inverse_ffn = norm_forward(middle, ffn_gain)
    ffn_rows = gather_rows(normed_ffn.astype(jnp.bfloat16))
    gate_full, up_full = (
        lax.all_gather(gate_weight, "col", axis=0, tiled=True),
        lax.all_gather(up_weight, "col", axis=0, tiled=True),
    )
    local_rows = lax.all_to_all(ffn_rows, "col", split_axis=0, concat_axis=1, tiled=True)
    gate = jnp.dot(local_rows, gate_full, preferred_element_type=jnp.float32)
    up_values = jnp.dot(local_rows, up_full, preferred_element_type=jnp.float32)
    sigma = jax.nn.sigmoid(gate)
    silu_gate = gate * sigma
    hidden = (silu_gate * up_values).astype(jnp.bfloat16)
    hidden_all, ffn_branch = out_project(hidden, down_weight)
    mixed = middle + ffn_branch
    down_part, d_hidden = back_out(cotangent, down_weight, hidden_all)
    d_gate = d_hidden * up_values * sigma * (1.0 + gate * (1.0 - sigma))
    d_up = d_hidden * silu_gate
    stacked_grads = jnp.concatenate([d_gate, d_up], axis=1).astype(jnp.bfloat16)
    stacked_weights = jnp.concatenate([gate_weight, up_weight], axis=1)
    gateup_part, d_normed_ffn = back_in(stacked_grads, stacked_weights, ffn_rows)
    hidden_width = gate_weight.shape[1]
    d_middle_norm, ffn_gain_part = norm_backward(d_normed_ffn, middle, inverse_ffn, ffn_gain)
    d_middle = cotangent.astype(jnp.float32) + d_middle_norm
    output_part, d_attended = back_out(d_middle.astype(jnp.bfloat16), output_weight, attended_all)
    d_projected = attention_backward(d_attended.astype(jnp.bfloat16), kept, logsum, positions)
    qkv_part, d_normed = back_in(d_projected, qkv_weight, attn_rows)
    d_source_norm, attn_gain_part = norm_backward(d_normed, source, inverse_attn, attn_gain)
    tokens_grad = d_middle + d_source_norm
    qkv_grad, output_grad, gate_grad, up_grad, down_grad = (
        lax.psum(qkv_part.astype(jnp.bfloat16), "dp").astype(jnp.float32),
        lax.psum(output_part.astype(jnp.bfloat16), "dp").astype(jnp.float32),
        lax.psum(gateup_part[:, :hidden_width].astype(jnp.bfloat16), "dp").astype(jnp.float32),
        lax.psum(gateup_part[:, hidden_width:].astype(jnp.bfloat16), "dp").astype(jnp.float32),
        lax.psum(down_part.astype(jnp.bfloat16), "dp").astype(jnp.float32),
    )
    attn_dgain, ffn_dgain = lax.psum((attn_gain_part, ffn_gain_part), DP_ROW)
    return (
        mixed,
        tokens_grad,
        attn_dgain,
        qkv_grad,
        output_grad,
        ffn_dgain,
        gate_grad,
        up_grad,
        down_grad,
    )


def solution(mesh):
    finer = Mesh(
        mesh.devices.reshape(mesh.shape["dp"], 4, 2, mesh.shape["col"]),
        ("dp", "row_0", "row_1", "col"),
    )
    in_specs = (
        P(DP_ROW, "col"),
        P(("dp", "col")),
        P("col"),
        P("col", ROW),
        P(ROW, "col"),
        P("col"),
        P("col", ROW),
        P("col", ROW),
        P(ROW, "col"),
        P(DP_ROW, "col"),
    )
    out_specs = (
        P(DP_ROW, "col"),
        P(DP_ROW, "col"),
        P("col"),
        P("col", ROW),
        P(ROW, "col"),
        P("col"),
        P("col", ROW),
        P("col", ROW),
        P(ROW, "col"),
    )
    return jax.shard_map(
        per_device, mesh=finer, in_specs=in_specs, out_specs=out_specs, check_vma=False
    )
```

profile of v0, /device:TPU:25, one launch (start us, length us, event | category | flops | bytes accessed | tf_op | source)
XLA Modules:
  0.0 1183.7 jit_solution(18271114523280630852)
XLA Ops:
  9.3 8.5 psum.77
  18.3 1.9 fusion.69
  20.3 63.0 %all-gather.11.cloned.1.call-done = bf16[4096,384]{1,0:T(8,128)(2,1)} async-done(((bf16[512,384]{1,0:T(8,128)(2,1)}), bf16[4096,384]{1,0:T(8,128)(2,1)}) %all-gather.11.cloned.1.call-update) | async-done | bytes 3145744 | tf_op jit(solution)/shard_map/all_gather | solution.py:77
  83.3 6.6 fusion.102
  91.4 63.2 %reduce-scatter.8.cloned.1.call-done = f32[1024,384]{1,0:T(8,128)} async-done(((f32[4096,384]{1,0:T(8,128)}), f32[1024,384]{1,0:T(8,128)}) %reduce-scatter.8.cloned.1.call-update) | async-done | bytes 1572880 | tf_op jit(solution)/shard_map/reduce_scatter | solution.py:238
  154.6 1.9 copy.25
  158.4 12.4 %while.47 = (s32[]{:T(128)}, bf16[2,512,1,2,96]{1,4,3,2,0:T(8,128)(2,1)}, f32[2,1,2,512]{3,2,1,0:T(2,128)S(1)}, s32[2]{0:T(128)S(1)}, bf16[2,512,1,2,96]{1,4,3,2...) while((s32[]{:T(128)}, ...), condition=%wide.region_6.7_spmd, body=%wide.region_3.6_spmd.sunk | while | flops 415759872 | bytes 18845864 | solution.py:156
  162.3 1.5 fusion.157
  168.5 1.5 fusion.157
  173.1 26.3 %all-gather.13.cloned.1.call-done = bf16[4096,192]{0,1:T(8,128)(2,1)} async-done(((bf16[1024,192]{0,1:T(8,128)(2,1)}), bf16[4096,192]{0,1:T(8,128)(2,1)}) %all-gather.13.cloned.1.call-update) | async-done | bytes 1572880 | tf_op jit(solution)/shard_map/all_gather | solution.py:81
  199.4 5.4 fusion.103
  205.8 13.8 %all_gather.42 = bf16[1024,384]{1,0:T(8,128)(2,1)} all-gather(bf16[512,384]{1,0:T(8,128)(2,1)S(1)} %copy-done.18), channel_id=1, replica_groups=mesh['dp'=4,'row_0'=4,'row_1'=2,'col'=4] {'row_1'}, dimensions={0}, use_global_device_ids=true | all-gather | bytes 1179648 | tf_op jit(solution)/shard_map/all_gather | solution.py:25
  219.6 108.6 %reduce-scatter.10.cloned.1.call-done = f32[512,384]{1,0:T(8,128)} async-done(((f32[4096,384]{1,0:T(8,128)}), f32[512,384]{1,0:T(8,128)}) %reduce-scatter.10.cloned.1.call-update) | async-done | bytes 786448 | tf_op jit(solution)/shard_map/reduce_scatter | solution.py:83
  329.5 8.4 psum.78
  340.4 7.5 fusion.106
  348.0 51.8 %all-gather.15.cloned.1.call-done = bf16[4096,384]{1,0:T(8,128)(2,1)} async-done(((bf16[512,384]{1,0:T(8,128)(2,1)}), bf16[4096,384]{1,0:T(8,128)(2,1)}) %all-gather.15.cloned.1.call-update) | async-done | bytes 3145744 | tf_op jit(solution)/shard_map/all_gather | solution.py:77
  399.8 4.7 copy.28
  404.4 4.6 all-to-all-start
  409.1 32.3 %all-gather.19.cloned.1.call-done = bf16[1536,512]{1,0:T(8,128)(2,1)} async-done(((bf16[384,512]{1,0:T(8,128)(2,1)}), bf16[1536,512]{1,0:T(8,128)(2,1)}) %all-gather.19.cloned.1.call-update) | async-done | bytes 1572880 | tf_op jit(solution)/shard_map/all_gather | solution.py:251
  441.4 15.6 %all-to-all-done = bf16[4,1024,384]{1,2,0:T(8,128)(2,1)} async-done(((bf16[4,1024,384]{1,2,0:T(8,128)(2,1)}), bf16[4,1024,384]{1,2,0:T(8,128)(2,1)}, u32[]{:S(2)}, u32[]{:S(2)}) %all-to-all-start) | async-done | bytes 3145760 | tf_op jit(solution)/shard_map/all_to_all | solution.py:253
  457.1 5.5 fusion.104
  462.6 10.1 all-gather.17.cloned.1.call-done
  472.7 80.8 %reduce-scatter.14.cloned.1.call-done = f32[1024,512]{0,1:T(8,128)} async-done(((f32[4096,512]{0,1:T(8,128)}), f32[1024,512]{0,1:T(8,128)}) %reduce-scatter.14.cloned.1.call-update) | async-done | bytes 2097168 | tf_op jit(solution)/shard_map/reduce_scatter | solution.py:90
  553.5 7.3 multiply_convert_fusion.1
  560.8 1.5 pad_maximum_fusion
  562.3 82.7 %all-gather.25.cloned.1.call-done = bf16[4096,1024]{0,1:T(8,128)(2,1)} async-done(((bf16[1024,1024]{0,1:T(8,128)(2,1)}), bf16[4096,1024]{0,1:T(8,128)(2,1)}) %all-gather.25.cloned.1.call-update) | async-done | bytes 8388624 | tf_op jit(solution)/shard_map/all_gather | solution.py:94
  645.0 9.6 convolution_convert_fusion.1
  654.7 79.5 %reduce-scatter.16.cloned.1.call-done = bf16[512,384]{1,0:T(8,128)(2,1)} async-done(((bf16[4096,384]{1,0:T(8,128)(2,1)}), bf16[512,384]{1,0:T(8,128)(2,1)}) %reduce-scatter.16.cloned.1.call-update) | async-done | bytes 393232 | tf_op jit(solution)/shard_map/reduce_scatter | solution.py:99
  734.2 1.9 fusion.66
  736.0 8.6 psum.79
  745.9 8.9 all_gather.45
  754.9 38.9 %all-gather.27.cloned.1.call-done = bf16[4096,384]{1,0:T(8,128)(2,1)} async-done(((bf16[1024,384]{1,0:T(8,128)(2,1)}), bf16[4096,384]{1,0:T(8,128)(2,1)}) %all-gather.27.cloned.1.call-update) | async-done | bytes 3145744 | tf_op jit(solution)/shard_map/all_gather | solution.py:25
  793.8 4.8 fusion.107
  799.4 39.8 %reduce-scatter.18.cloned.1.call-done = f32[1024,192]{0,1:T(8,128)} async-done(((f32[4096,192]{0,1:T(8,128)}), f32[1024,192]{0,1:T(8,128)}) %reduce-scatter.18.cloned.1.call-update) | async-done | bytes 786448 | tf_op jit(solution)/shard_map/reduce_scatter | solution.py:90
  840.7 43.4 %while.48 = (s32[]{:T(128)}, f32[1024,1,96]{0,2,1:T(8,128)}, f32[1024,1,96]{0,2,1:T(8,128)}, f32[2,512,1,2,96]{1,0,4,3,2:T(2,128)}, bf16[2,512,1,2,96]{1,4,3,2,0...) while((s32[]{:T(128)}, f32[1024,1,96]{0,2,1:T(8,128)}, ...), condition=%wide.region_18.19_spmd.clone, body=%wide.region_16.18_spmd.clone.sunk | while | flops 1024327168 | bytes 64718232 | solution.py:210
  843.1 1.6 fusion.167
  844.8 1.5 fusion.168
  847.4 8.1 dynamic_update_slice.32
  855.6 2.1 fusion.169
  857.7 4.5 fusion.170
  864.7 1.6 fusion.167
  866.4 1.5 fusion.168
  869.1 8.1 dynamic_update_slice.32
  877.1 2.3 fusion.169
  879.5 4.5 fusion.170
  884.0 2.7 broadcast_in_dim.81
  886.7 2.0 fusion.89
  892.4 5.4 convolution_convert_fusion.3
  897.8 6.2 convolution_convert_fusion.2
  904.9 1.6 convolution_convert_fusion.5
  906.6 24.8 %all-gather.29.cloned.1.call-done = bf16[4096,384]{0,1:T(8,128)(2,1)} async-done(((bf16[1024,384]{0,1:T(8,128)(2,1)}), bf16[4096,384]{0,1:T(8,128)(2,1)}) %all-gather.29.cloned.1.call-update) | async-done | bytes 3145744 | tf_op jit(solution)/shard_map/all_gather | solution.py:94
  931.4 5.5 convolution_convert_fusion.4
  937.0 4.7 convolution_convert_fusion
  941.8 7.2 fusion.105
  949.2 38.8 %all-reduce.4.cloned.1.call-done = (bf16[384,384]{1,0:T(8,128)(2,1)}, bf16[192,384]{1,0:T(8,128)(2,1)}, bf16[384,512]{1,0:T(8,128)(2,1)}, bf16[384,512]{1,0:T(8,128)(2,1)}, bf16[512,384]{1,0:T(8,128)(2,1)}) async-done(((bf16[384,384]{1,0:T(8,128)(2,1)}, bf16[192,384]{1,0:T(8,128)(2,1)}, bf16[384,512]{1,0:T(8,128)(2,1)}, bf16[384,512]{1,0:T(8,128)(2,1)}, bf16[512,384]{1,0:T(8,128)(2,1)}), ...) | async-done | bytes 1622032 | tf_op jit(solution)/shard_map/psum | solution.py:276
  988.0 2.0 convert_element_type.136
  990.0 2.0 convert_element_type.137
  992.0 1.9 convert_element_type.139
  995.5 74.9 %reduce-scatter.20.cloned.1.call-done = bf16[512,384]{1,0:T(8,128)(2,1)} async-done(((bf16[4096,384]{1,0:T(8,128)(2,1)}), bf16[512,384]{1,0:T(8,128)(2,1)}) %reduce-scatter.20.cloned.1.call-update) | async-done | bytes 393232 | tf_op jit(solution)/shard_map/reduce_scatter | solution.py:99
  1070.4 1.4 fusion.72
  1071.8 63.9 %all-reduce = (f32[384]{0:T(512)}, f32[384]{0:T(512)}) all-reduce(f32[384]{0:T(512)S(1)} %get-tuple-element.219, f32[384]{0:T(512)S(1)} %copy-done.36), channel_id=1, replica_groups=mesh['dp'=4,'row_0'=4,'row_1'=2,'col'=4] {'dp','row_0','row_1'}, use_global_device_ids=true, to_apply=%region_23.24 | all-reduce | flops 768 | bytes 6144 | tf_op jit(solution)/shard_map/psum | solution.py:282
  1135.7 8.3 psum.80
  1144.1 28.9 %reduce-scatter.12.cloned.1.call-done = f32[512,384]{1,0:T(8,128)} async-done(((f32[4096,384]{1,0:T(8,128)}), f32[512,384]{1,0:T(8,128)}) %reduce-scatter.12.cloned.1.call-update) | async-done | bytes 786448 | tf_op jit(solution)/shard_map/reduce_scatter | solution.py:83
  1173.0 2.8 fusion.61
  (202 shorter events, 38.8 us)
Async XLA Ops:
  8.0 332.4 %copy-start = (bf16[512,384]{1,0:T(8,128)(2,1)S(1)}, bf16[512,384]{1,0:T(8,128)(2,1)}, u32[]{:S(2)}) copy-start(bf16[512,384]{1,0:T(8,128)(2,1)} %param.22) | copy-start | bytes 1179652
  8.0 75.2 %all-gather.11.cloned.1.call-start = ((), (), s32[]{:S(2)}) async-start(), calls=%async_computation.8 | async-start | bytes 3538944 | tf_op jit(solution)/shard_map/all_gather | solution.py:77
  17.7 72.2 %copy-start.34 = (f32[512]{0:T(512)}, f32[512]{0:T(512)S(1)}, u32[]{:S(2)}) copy-start(f32[512]{0:T(512)S(1)} %psum.77) | copy-start | bytes 6148
  20.3 134.3 %reduce-scatter.8.cloned.1.call-start = ((), (), s32[]{:S(2)}) async-start(), calls=%async_computation.9 | async-start | bytes 7864320 | tf_op jit(solution)/shard_map/reduce_scatter | solution.py:238
  89.9 109.4 %all-gather.13.cloned.1.call-start = ((), (), s32[]{:S(2)}) async-start(), calls=%async_computation.10 | async-start | bytes 1966080 | tf_op jit(solution)/shard_map/all_gather | solution.py:81
  90.6 66.9 %copy-start.37 = (f32[48]{0:T(128)}, f32[48]{0:T(128)S(1)}, u32[]{:S(2)}) copy-start(f32[48]{0:T(128)S(1)} %negate_power_fusion) | copy-start | bytes 580
  91.4 65.4 %copy-start.22 = (f32[1024,48]{0,1:T(8,128)}, f32[1024,48]{0,1:T(8,128)S(1)}, u32[]{:S(2)}) copy-start(f32[1024,48]{0,1:T(8,128)S(1)} %get-tuple-element.283) | copy-start | bytes 589828
  91.4 65.4 %copy-start.23 = (f32[1024,48]{0,1:T(8,128)}, f32[1024,48]{0,1:T(8,128)S(1)}, u32[]{:S(2)}) copy-start(f32[1024,48]{0,1:T(8,128)S(1)} %get-tuple-element.284) | copy-start | bytes 589828
  158.4 41.0 %copy-start.24 = (bf16[192,384]{1,0:T(8,128)(2,1)S(1)}, bf16[192,384]{1,0:T(8,128)(2,1)}, u32[]{:S(2)}) copy-start(bf16[192,384]{1,0:T(8,128)(2,1)} %param.18) | copy-start | bytes 442372
  161.1 1.2 copy-start.26
  167.3 1.2 copy-start.26
  173.0 155.1 %reduce-scatter.10.cloned.1.call-start = ((), (), s32[]{:S(2)}) async-start(), calls=%async_computation.11 | async-start | bytes 7077888 | tf_op jit(solution)/shard_map/reduce_scatter | solution.py:83
  204.8 123.4 %copy-start.10 = (bf16[512,384]{1,0:T(8,128)(2,1)S(1)}, bf16[512,384]{1,0:T(8,128)(2,1)}, u32[]{:S(2)}) copy-start(bf16[512,384]{1,0:T(8,128)(2,1)} %param.14) | copy-start | bytes 1179652
  204.8 133.1 %copy-start.30 = (f32[384]{0:T(512)S(1)}, f32[384]{0:T(512)}, u32[]{:S(2)}) copy-start(f32[384]{0:T(512)} %param.19) | copy-start | bytes 4612
  204.8 135.6 %all-gather.23.cloned.1.call-start = ((), (), s32[]{:S(2)}) async-start(), calls=%async_computation.17 | async-start | bytes 3932160 | tf_op jit(solution)/shard_map/all_gather | solution.py:25
  219.6 180.2 %all-gather.15.cloned.1.call-start = ((), (), s32[]{:S(2)}) async-start(), calls=%async_computation.12 | async-start | bytes 3538944 | tf_op jit(solution)/shard_map/all_gather | solution.py:77
  329.5 415.1 %copy-start.4 = (f32[512,384]{1,0:T(8,128)}, f32[512,384]{1,0:T(8,128)S(1)}, u32[]{:S(2)}) copy-start(f32[512,384]{1,0:T(8,128)S(1)} %get-tuple-element.263) | copy-start | bytes 2359300
  338.8 102.6 %all-gather.19.cloned.1.call-start = ((), (), s32[]{:S(2)}) async-start(), calls=%async_computation.14 | async-start | bytes 1966080 | tf_op jit(solution)/shard_map/all_gather | solution.py:251
  339.4 133.3 %all-gather.17.cloned.1.call-start = ((), (), s32[]{:S(2)}) async-start(), calls=%async_computation.13 | async-start | bytes 1966080 | tf_op jit(solution)/shard_map/all_gather | solution.py:250
  340.1 213.4 %reduce-scatter.14.cloned.1.call-start = ((), (), s32[]{:S(2)}) async-start(), calls=%async_computation.18 | async-start | bytes 10485760 | tf_op jit(solution)/shard_map/reduce_scatter | solution.py:90
  404.4 52.7 %all-to-all-start = ((bf16[4,1024,384]{1,2,0:T(8,128)(2,1)}), bf16[4,1024,384]{1,2,0:T(8,128)(2,1)}, u32[]{:S(2)}, u32[]{:S(2)}) async-start(bf16[4,1024,384]{1,2,0:T(8,128)(2,1)} %copy.28), calls=%async_computation.2 | async-start | bytes 6291456 | tf_op jit(solution)/shard_map/all_to_all | solution.py:253
  409.1 235.9 %all-gather.25.cloned.1.call-start = ((), (), s32[]{:S(2)}) async-start(), calls=%async_computation.19 | async-start | bytes 10485760 | tf_op jit(solution)/shard_map/all_gather | solution.py:94
  560.8 84.2 %copy-start.25 = (bf16[384,512]{1,0:T(8,128)(2,1)S(1)}, bf16[384,512]{1,0:T(8,128)(2,1)}, u32[]{:S(2)}) copy-start(bf16[384,512]{1,0:T(8,128)(2,1)} %param.21) | copy-start | bytes 1179652
  562.3 171.9 %reduce-scatter.16.cloned.1.call-start = ((), (), s32[]{:S(2)}) async-start(), calls=%async_computation.20 | async-start | bytes 3538944 | tf_op jit(solution)/shard_map/reduce_scatter | solution.py:99
  654.6 139.2 %all-gather.27.cloned.1.call-start = ((), (), s32[]{:S(2)}) async-start(), calls=%async_computation.21 | async-start | bytes 3932160 | tf_op jit(solution)/shard_map/all_gather | solution.py:25
  754.8 84.3 %reduce-scatter.18.cloned.1.call-start = ((), (), s32[]{:S(2)}) async-start(), calls=%async_computation.22 | async-start | bytes 3932160 | tf_op jit(solution)/shard_map/reduce_scatter | solution.py:90
  798.6 93.8 %all-gather.21.cloned.1.call-start = ((), (), s32[]{:S(2)}) async-start(), calls=%async_computation.15 | async-start | bytes 5242880 | tf_op jit(solution)/shard_map/all_gather | solution.py:81
  799.3 132.1 %all-gather.29.cloned.1.call-start = ((), (), s32[]{:S(2)}) async-start(), calls=%async_computation.23 | async-start | bytes 3932160 | tf_op jit(solution)/shard_map/all_gather | solution.py:94
  840.7 4.0 copy-start.12
  840.7 4.0 copy-start.15
  840.7 4.0 copy-start.7
  840.7 5.5 copy-start.2
  841.5 3.3 copy-start.1
  857.7 4.6 copy-start.3
  857.7 4.6 copy-start.8
  857.7 4.6 copy-start.13
  857.7 4.6 copy-start.16
  862.3 4.0 copy-start.12
  862.3 4.0 copy-start.15
  862.3 4.0 copy-start.7
  862.3 5.5 copy-start.2
  863.1 3.3 copy-start.1
  879.5 4.5 copy-start.3
  879.5 4.5 copy-start.8
  879.5 4.5 copy-start.13
  879.5 4.6 copy-start.16
  886.7 5.7 copy-start.17
  892.1 95.9 %all-reduce.4.cloned.1.call-start = ((), (), s32[]{:S(2)}) async-start(), calls=%async_computation.25 | async-start | bytes 3244032 | tf_op jit(solution)/shard_map/psum | solution.py:276
  892.4 5.4 copy-start.21
  897.8 7.1 copy-start.6
  897.8 7.1 copy-start.9
  931.4 5.6 copy-start.14
  936.9 133.5 %reduce-scatter.20.cloned.1.call-start = ((), (), s32[]{:S(2)}) async-start(), calls=%async_computation.24 | async-start | bytes 3538944 | tf_op jit(solution)/shard_map/reduce_scatter | solution.py:99
  941.8 231.2 %reduce-scatter.12.cloned.1.call-start = ((), (), s32[]{:S(2)}) async-start(), calls=%async_computation.16 | async-start | bytes 7077888 | tf_op jit(solution)/shard_map/reduce_scatter | solution.py:83
  949.1 121.3 %copy-start.11 = (bf16[512,384]{1,0:T(8,128)(2,1)S(1)}, bf16[512,384]{1,0:T(8,128)(2,1)}, u32[]{:S(2)}) copy-start(bf16[512,384]{1,0:T(8,128)(2,1)} %param.14) | copy-start | bytes 1179652
  949.1 121.3 %copy-start.32 = (f32[512]{0:T(512)S(1)}, f32[512]{0:T(512)}, u32[]{:S(2)}) copy-start(f32[512]{0:T(512)} %copy-done.31) | copy-start | bytes 6148
  949.1 121.3 %copy-start.33 = (f32[384]{0:T(512)S(1)}, f32[384]{0:T(512)}, u32[]{:S(2)}) copy-start(f32[384]{0:T(512)} %param.16) | copy-start | bytes 4612
  949.1 122.7 %copy-start.36 = (f32[384]{0:T(512)S(1)}, f32[384]{0:T(512)}, u32[]{:S(2)}) copy-start(f32[384]{0:T(512)} %get-tuple-element.217) | copy-start | bytes 4612
  949.1 194.9 %copy-start.35 = (f32[512]{0:T(512)S(1)}, f32[512]{0:T(512)}, u32[]{:S(2)}) copy-start(f32[512]{0:T(512)} %copy-done.34) | copy-start | bytes 6148
  949.2 223.9 %copy-start.5 = (f32[512,384]{1,0:T(8,128)S(1)}, f32[512,384]{1,0:T(8,128)}, u32[]{:S(2)}) copy-start(f32[512,384]{1,0:T(8,128)} %copy-done.4) | copy-start | bytes 2359300
  949.2 223.8 %copy-start.19 = (bf16[512,384]{1,0:T(8,128)(2,1)S(1)}, bf16[512,384]{1,0:T(8,128)(2,1)}, u32[]{:S(2)}) copy-start(bf16[512,384]{1,0:T(8,128)(2,1)} %param.23) | copy-start | bytes 1179652
  949.2 223.8 %copy-start.20 = (bf16[512,384]{1,0:T(8,128)(2,1)S(1)}, bf16[512,384]{1,0:T(8,128)(2,1)}, u32[]{:S(2)}) copy-start(bf16[512,384]{1,0:T(8,128)(2,1)} %reduce-scatter.16.cloned.1.call-done) | copy-start | bytes 1179652
  988.0 5.9 copy-start.28
  988.0 6.8 copy-start.29
  (5 other events, 3.8 us)
Sparse Core Ops, SparseCore 0:
  20.4 62.8 all-gather.10
  90.1 64.4 reduce-scatter.7
  173.2 26.1 all-gather.12
  204.9 123.2 reduce-scatter.9
  654.7 79.3 reduce-scatter.15
  798.7 40.4 reduce-scatter.17
  840.8 47.9 all-gather.20
  892.2 39.1 all-gather.28
Sparse Core Ops, SparseCore 1:
  219.7 49.5 all-gather.22
  338.9 60.8 all-gather.14
  401.4 40.0 all-gather.18
  443.2 29.4 all-gather.16
  475.4 78.1 reduce-scatter.13
  562.4 82.6 all-gather.24
  754.9 38.8 all-gather.26
  937.0 50.9 all-reduce.3
  992.2 78.1 reduce-scatter.19
  1074.4 98.6 reduce-scatter.11
where the time goes:
time: 1200 us; the launch traced here: 1180 us
  waiting for transfers between devices  862 us (72%)
  blocking collectives  120 us (10%)
  matrix products  103 us (9%)
  other arithmetic  39.6 us (3%)
  local copies, waits for them, and re-layouts  36.3 us (3%)
  between operations  16.6 us (1%)
    reduce_scatter x2, waiting for transfers between devices, back_in(): lax.psum_scatter(term.astype(jnp.bfloat16), ROW, scatter_dimension=0, til...  154 us
    reduce_scatter x2, waiting for transfers between devices, out_project(): lax.psum_scatter(term, ROW, scatter_dimension=0, tiled=True)  138 us
    reduce_scatter x2, waiting for transfers between devices, back_out(): lax.psum_scatter(term, 'col', scatter_dimension=0, tiled=True)  121 us
    all_gather x2, waiting for transfers between devices, gather_rows(): return lax.all_gather(values, ROW, axis=0, tiled=True)  115 us
    all_gather x2, waiting for transfers between devices, back_in(): gathered = lax.all_gather(grads, 'col', axis=0, tiled=True)  107 us
    psum x1, blocking collectives, per_device(): attn_dgain, ffn_dgain = lax.psum((attn_gain_part, ffn_gain_part), DP_ROW)  63.9 us
    reduce_scatter x1, waiting for transfers between devices, per_device(): lax.psum_scatter(jnp.dot(attn_rows, qkv_weight, preferred_element_type=jn...  63.2 us
    all_gather x2, waiting for transfers between devices, gather_axes(): x = lax.all_gather(x, axis, axis=dim, tiled=True)  38.9 us
  transfers between devices with their start and end apart: 19, of which 17 were waited for; matrix products, arithmetic and copies ran while one was open for 9% of the time, Pallas kernels for 0%

commit v1 on v0

v1 whole, which is shorter than its diff:
```python
import math

import jax
import jax.numpy as jnp
from jax import lax
from jax.sharding import Mesh
from jax.sharding import PartitionSpec as P

D = 1536
H = 16
KVH = 8
HD = 96
LEN = 1024
GROUP = H // KVH
AXES = ("zl", "core", "y", "zh", "x")
DP_ROW = ("zl", "core", "y", "zh")
bf16 = jnp.bfloat16
f32 = jnp.float32

epsilon = 1e-05
rope_base = 100000.0
masked_score = -1e30
SIZES = {"zl": 2, "core": 2, "y": 4, "zh": 2, "x": 4}


def fetch(values, axis, step):
    n = SIZES[axis]
    return lax.ppermute(values, axis, [((i + step) % n, i) for i in range(n)])


def fetch_z(values, flip):
    flip = (flip & 1) * 2 + flip // 2
    return lax.ppermute(values, ("zl", "zh"), [(i ^ flip, i) for i in range(4)])


def send_xy(values):
    return lax.ppermute(values, ("y", "x"), [(y * 4 + x, x * 4 + y) for y in range(4) for x in range(4)])


def gather_ring(values, axis):
    return [values] + [fetch(values, axis, k) for k in range(1, SIZES[axis])]


def gather_z(values):
    return [values] + [fetch_z(values, k) for k in range(1, 4)]


def scatter_ring(blocks, axis):
    total = blocks[0].astype(f32)
    for k in range(1, 4):
        total = total + fetch(blocks[k].astype(bf16), axis, -k).astype(f32)
    return total


def scatter_z(blocks):
    total = blocks[0].astype(f32)
    for k in range(1, 4):
        total = total + fetch_z(blocks[k].astype(bf16), k).astype(f32)
    return total


def rolled(stack, start):
    return lax.dynamic_slice_in_dim(jnp.concatenate([stack, stack], 0), start, 4, axis=0)


def ordered(flag, own, other):
    return jnp.where(flag == 0, own, other), jnp.where(flag == 0, other, own)


def dot(a, b, dims):
    return lax.dot_general(a, b, (dims, ((), ())), preferred_element_type=f32)


def rope_tables(places):
    half_size = HD // 2
    frequency = rope_base ** (-(jnp.arange(half_size, dtype=f32) * 2.0 / HD))
    angles = places.astype(f32)[:, None] * frequency[None, :]
    return jnp.cos(angles), jnp.sin(angles)


def rotate(vectors, cosine, sine):
    half_size = vectors.shape[-1] // 2
    a, b = vectors[..., :half_size], vectors[..., half_size:]
    return jnp.concatenate([a * cosine - b * sine, b * cosine + a * sine], axis=-1)


def block_scores(query_block, key_seq, start):
    raw = jnp.einsum("qhd,kd->hqk", query_block, key_seq, preferred_element_type=f32)
    raw = raw * (1.0 / math.sqrt(HD))
    rows = start + jnp.arange(query_block.shape[0], dtype=jnp.int32)
    cols = jnp.arange(key_seq.shape[0], dtype=jnp.int32)
    return jnp.where((cols[None, :] <= rows[:, None])[None], raw, masked_score)


def attention_forward(q, k, v):
    outs, logs = [], []
    for start in (0, 512):
        keys, values = k[: start + 512], v[: start + 512]
        scores = block_scores(q[start : start + 512], keys, start)
        top = jnp.max(scores, axis=-1, keepdims=True)
        exponent = jnp.exp(scores - top)
        totals = jnp.sum(exponent, axis=-1, keepdims=True)
        probs = (exponent / totals).astype(bf16)
        outs.append(jnp.einsum("hqk,kd->qhd", probs, values, preferred_element_type=f32))
        logs.append((top + jnp.log(totals))[..., 0])
    return jnp.concatenate(outs, 0).astype(bf16), logs


def attention_backward(q, k, v, grad, logs):
    scale = 1.0 / math.sqrt(HD)
    dqs = []
    dk = jnp.zeros((LEN, HD), f32)
    dv = jnp.zeros((LEN, HD), f32)
    for i, start in enumerate((0, 512)):
        n = start + 512
        qb, gb = q[start:n], grad[start:n]
        scores = block_scores(qb, k[:n], start)
        probs = jnp.exp(scores - logs[i][..., None])
        dpr = jnp.einsum("qhd,kd->hqk", gb, v[:n], preferred_element_type=f32)
        inner = jnp.sum(probs * dpr, axis=-1, keepdims=True)
        ds = (probs * (dpr - inner) * scale).astype(bf16)
        dqs.append(jnp.einsum("hqk,kd->qhd", ds, k[:n], preferred_element_type=f32))
        dk = dk.at[:n].add(jnp.einsum("hqk,qhd->kd", ds, qb, preferred_element_type=f32))
        dv = dv.at[:n].add(jnp.einsum("hqk,qhd->kd", probs.astype(bf16), gb, preferred_element_type=f32))
    return jnp.concatenate(dqs, 0), dk, dv


def per_device(
    tokens,
    positions,
    attn_gain,
    qkv_weight,
    output_weight,
    ffn_gain,
    gate_weight,
    up_weight,
    down_weight,
    cotangent,
):
    ix, iy = lax.axis_index("x"), lax.axis_index("y")
    zl, zh, core = lax.axis_index("zl"), lax.axis_index("zh"), lax.axis_index("core")
    quarter = zl * 2 + core

    x_full = jnp.concatenate(gather_ring(tokens, "x"), 1).astype(f32)
    gains = gather_ring(jnp.stack([attn_gain, ffn_gain]), "x")
    gains = jnp.concatenate(gains, 1)
    gain_a, gain_f = gains[0], gains[1]
    places = rolled(jnp.stack(gather_ring(positions, "x")), (iy - ix + 4) % 4)[0]
    places = lax.dynamic_slice_in_dim(places, zh * 512, 512)

    qo = jnp.concatenate([qkv_weight.T, output_weight], 0)
    qo = lax.dynamic_slice_in_dim(qo, quarter * 144, 144, axis=0)
    qo = send_xy(qo)
    qo = rolled(jnp.stack(gather_ring(qo, "y")), (ix - iy + 4) % 4)
    qo = jnp.concatenate([qo[0], qo[1], qo[2], qo[3]], 1)
    zs = gather_z(qo)
    own = jnp.concatenate(ordered(zl, zs[0], zs[1]), 0).reshape(2, 144, D)
    far = jnp.concatenate(ordered(zl, zs[2], zs[3]), 0).reshape(2, 144, D)
    pair = jnp.stack([own, far])
    pair = jnp.stack(ordered(core, pair, fetch(pair, "core", 1)), 2)
    heads = pair.reshape(2, 576, D)
    w_qkv = heads[:, :384].reshape(768, D)
    w_out = heads[:, 384:].reshape(384, D)

    def hidden_rows(w):
        blocks = lax.dynamic_slice_in_dim(w.reshape(4, 4, 32, 384), quarter, 1, axis=1)[:, 0]
        return rolled(blocks, ix)

    mine = jnp.stack([hidden_rows(gate_weight.T), hidden_rows(up_weight.T), hidden_rows(down_weight)], 1)
    ffn = jnp.concatenate([mine[0]] + [fetch(mine[4 - k], "x", k) for k in range(1, 4)], 2)
    half_a = jnp.concatenate(gather_z(jnp.concatenate(gather_ring(ffn[:, :16], "y"), 1)), 1)
    half_b = jnp.concatenate(gather_ring(jnp.concatenate(gather_z(ffn[:, 16:]), 1), "y"), 1)
    ffn = jnp.concatenate([half_a, half_b], 1)
    ffn = jnp.concatenate([ffn, fetch(ffn, "core", 1)], 1)
    w_gate, w_up, w_down = ffn[0], ffn[1], ffn[2]

    rinv1 = lax.rsqrt(jnp.mean(x_full * x_full, axis=1) + epsilon)
    a1 = (x_full * rinv1[:, None] * gain_a[None, :]).astype(bf16)
    proj = dot(a1, w_qkv, ((1,), (1,))).reshape(512, 2, 4, HD)
    cosine, sine = rope_tables(places)
    cosine, sine = cosine[:, None, None], sine[:, None, None]
    rot = rotate(proj[:, :, :3], cosine, sine)
    qkv = jnp.concatenate([rot, proj[:, :, 3:]], 2).astype(bf16)
    first, second = ordered(zh, qkv[:, 0], fetch(qkv[:, 1], "zh", 1))
    seq = jnp.concatenate([first, second], 0)
    att, logs = attention_forward(seq[:, :2], seq[:, 2], seq[:, 3])
    lower, upper = att[:512], att[512:]
    stay, go = ordered(zh, lower, upper)
    att_pair = jnp.concatenate([stay.reshape(512, 192), fetch(go.reshape(512, 192), "zh", 1)], 1)
    branch = dot(att_pair, w_out, ((1,), (0,)))
    middle = tokens.astype(f32) + scatter_ring([branch[:, 384 * k : 384 * k + 384] for k in range(4)], "x")

    m_full = jnp.concatenate(gather_ring(middle.astype(bf16), "x"), 1).astype(f32)
    rinv2 = lax.rsqrt(jnp.mean(m_full * m_full, axis=1) + epsilon)
    a2 = (m_full * rinv2[:, None] * gain_f[None, :]).astype(bf16)
    cot = jnp.concatenate(gather_ring(cotangent, "x"), 1)
    gate = dot(a2, w_gate, ((1,), (1,)))
    up = dot(a2, w_up, ((1,), (1,)))
    dh = dot(cot, w_down, ((1,), (1,)))
    sg = jax.nn.sigmoid(gate)
    silu = gate * sg
    hidden = (silu * up).astype(bf16)
    dgate = (dh * up * sg * (1.0 + gate * (1.0 - sg))).astype(bf16)
    dup = (dh * silu).astype(bf16)
    da2 = dot(dgate, w_gate, ((1,), (0,))) + dot(dup, w_up, ((1,), (0,)))
    da2 = scatter_ring([da2[:, 384 * k : 384 * k + 384] for k in range(4)], "x")
    inner2 = jnp.sum(dgate.astype(f32) * gate + dup.astype(f32) * up, axis=1).reshape(4, 128)
    inner2 = sum(gather_ring(inner2, "x")).reshape(512) / rinv2
    gain_f_own, gain_a_own = ffn_gain[None, :], attn_gain[None, :]
    ffn_dgain = jnp.sum(da2 * middle * rinv2[:, None], axis=0)
    dmiddle = (
        cotangent.astype(f32)
        + rinv2[:, None] * gain_f_own * da2
        - middle * (rinv2 * rinv2 * rinv2 * inner2 / D)[:, None]
    )
    dz = jnp.concatenate(gather_ring(dmiddle.astype(bf16), "x"), 1)
    datt = dot(dz, w_out, ((1,), (1,))).astype(bf16)
    down = dot(hidden, w_down, ((1,), (0,)))
    mixed = middle + scatter_ring([down[:, 384 * k : 384 * k + 384] for k in range(4)], "x")
    g_ffn = jnp.stack([dot(dgate, a2, ((0,), (0,))), dot(dup, a2, ((0,), (0,))), dot(hidden, cot, ((0,), (0,)))])

    def reduce_hidden(g):
        keep = g[:, :512] + fetch(g[:, 512:].astype(bf16), "core", 1).astype(f32)
        a, b = keep[:, :256], keep[:, 256:]
        a = scatter_z([a[:, 64 * k : 64 * k + 64] for k in range(4)])
        a = scatter_ring([a[:, 16 * k : 16 * k + 16] for k in range(4)], "y")
        b = scatter_ring([b[:, 64 * k : 64 * k + 64] for k in range(4)], "y")
        b = scatter_z([b[:, 16 * k : 16 * k + 16] for k in range(4)])
        part = jnp.concatenate([a, b], 1).astype(bf16)
        back = [part[:, :, :384]] + [fetch(part[:, :, 384 * k : 384 * k + 384], "x", -k) for k in range(1, 4)]
        blocks = rolled(jnp.stack([back[0], back[3], back[2], back[1]]), (4 - ix) % 4)
        quarters = jnp.stack(ordered(core, blocks, fetch(blocks, "core", 1)), 2)
        quarters = jnp.stack(ordered(zl, quarters, fetch(quarters, "zl", 1)), 2)
        return quarters.transpose(1, 0, 2, 3, 4, 5).reshape(3, 512, 384).astype(f32)

    g_gate, g_up, g_down = reduce_hidden(g_ffn)

    own_half, far_half = datt[:, :192], datt[:, 192:]
    g_lo, g_hi = ordered(zh, own_half, fetch(far_half, "zh", 1))
    g_seq = jnp.concatenate([g_lo, g_hi], 0).reshape(LEN, GROUP, HD)
    dq, dk, dv = attention_backward(seq[:, :2], seq[:, 2], seq[:, 3], g_seq, logs)
    dqkv = jnp.concatenate([dq, dk[:, None], dv[:, None]], 1).astype(bf16)
    stay, go = ordered(zh, dqkv[:512], dqkv[512:])
    dpair = jnp.stack([stay, fetch(go, "zh", 1)], 1).astype(f32)
    inner1 = jnp.sum(dpair * qkv.astype(f32), axis=(1, 2, 3)).reshape(4, 128)
    inner1 = sum(gather_ring(inner1, "x")).reshape(512) / rinv1
    turned = rotate(dpair[:, :, :3], cosine, -sine)
    dproj = jnp.concatenate([turned, dpair[:, :, 3:]], 2).astype(bf16).reshape(512, 768)
    da1 = dot(dproj, w_qkv, ((1,), (0,)))
    da1 = scatter_ring([da1[:, 384 * k : 384 * k + 384] for k in range(4)], "x")
    x_own = tokens.astype(f32)
    attn_dgain = jnp.sum(da1 * x_own * rinv1[:, None], axis=0)
    tokens_grad = (
        dmiddle
        + rinv1[:, None] * gain_a_own * da1
        - x_own * (rinv1 * rinv1 * rinv1 * inner1 / D)[:, None]
    )

    gw_qkv = dot(dproj, a1, ((0,), (0,))).reshape(2, 384, D)
    gw_out = dot(att_pair, dz, ((0,), (0,))).reshape(2, 192, D)
    g = jnp.concatenate([gw_qkv, gw_out], 1).reshape(2, 2, 2, 144, D)
    keep, give = ordered(core, g[:, :, 0], g[:, :, 1])
    g = keep + fetch(give.astype(bf16), "core", 1).astype(f32)
    g_own, g_far = ordered(zl, g[:, 0], g[:, 1])
    g = scatter_z([g_own[0], g_far[0], g_own[1], g_far[1]])
    cols = jnp.stack([g[:, 384 * k : 384 * k + 384] for k in range(4)])
    cols = rolled(cols, (iy - ix + 4) % 4)
    g = scatter_ring([cols[k] for k in range(4)], "y").astype(bf16)
    g = send_xy(g)
    g = jnp.stack(ordered(core, g, fetch(g, "core", 1)))
    g = jnp.stack(ordered(zl, g, fetch(g, "zl", 1))).reshape(576, 384).astype(f32)
    qkv_grad, output_grad = g[:384].T, g[384:]

    attn_dgain, ffn_dgain = lax.psum((attn_dgain, ffn_dgain), DP_ROW)
    return (
        mixed,
        tokens_grad,
        attn_dgain,
        qkv_grad,
        output_grad,
        ffn_dgain,
        g_gate.T,
        g_up.T,
        g_down,
    )


def solution(mesh):
    finer = Mesh(mesh.devices.reshape(2, 2, 4, 2, 4), AXES)
    row = ("y", "zh")
    in_specs = (
        P(DP_ROW, "x"),
        P(("zl", "core", "x")),
        P("x"),
        P("x", row),
        P(row, "x"),
        P("x"),
        P("x", row),
        P("x", row),
        P(row, "x"),
        P(DP_ROW, "x"),
    )
    out_specs = (
        P(DP_ROW, "x"),
        P(DP_ROW, "x"),
        P("x"),
        P("x", row),
        P(row, "x"),
        P("x"),
        P("x", row),
        P("x", row),
        P(row, "x"),
    )
    return jax.shard_map(per_device, mesh=finer, in_specs=in_specs, out_specs=out_specs, check_vma=False)
```

time: 1200 us -> 594 us (0.49)
  the two profiles are of different devices: /device:TPU:25 before, /device:TPU:1 now
where the time goes in v1:
time: 594 us; the launch traced here: 585 us
  starting transfers between devices  194 us (33%)
  waiting for transfers between devices  194 us (33%)
  blocking collectives  67.6 us (11%)
  matrix products  59.3 us (10%)
  other arithmetic  41.4 us (7%)
  local copies, waits for them, and re-layouts  25.2 us (4%)
    ppermute x72, starting transfers between devices, fetch(): return lax.ppermute(values, axis, [((i + step) % n, i) for i in range(n)])  168 us
    ppermute x72, waiting for transfers between devices, fetch(): return lax.ppermute(values, axis, [((i + step) % n, i) for i in range(n)])  137 us
    psum x1, blocking collectives, per_device(): attn_dgain, ffn_dgain = lax.psum((attn_dgain, ffn_dgain), DP_ROW)  67.6 us
    ppermute x18, waiting for transfers between devices, fetch_z(): return lax.ppermute(values, ('zl', 'zh'), [(i ^ flip, i) for i in range(4)])  57.5 us
    dot_general x15, matrix products, dot(): return lax.dot_general(a, b, (dims, ((), ())), preferred_element_type=f32)  24.9 us
    ppermute x18, starting transfers between devices, fetch_z(): return lax.ppermute(values, ('zl', 'zh'), [(i ^ flip, i) for i in range(4)])  23.6 us
    another operation x6, other arithmetic  15 us
    dot_general x2, matrix products, attention_backward(): jnp.einsum('hqk,qhd->kd', ds, qb, preferred_element_type=f32)  12.5 us
  transfers between devices with their start and end apart: 92, of which 40 were waited for; matrix products, arithmetic and copies ran while one was open for 12% of the time, Pallas kernels for 0%

profile of v1, /device:TPU:1, one launch (start us, length us, event | category | flops | bytes accessed | tf_op | source)
XLA Modules:
  0.0 584.8 jit_solution(13672932920831743802)
XLA Ops:
  4.2 2.5 collective-permute-start.4
  20.5 5.1 collective-permute-done.15
  31.3 4.5 collective-permute-start.28
  35.7 7.5 %collective-permute-start.7 = (bf16[144,384]{1,0:T(8,128)(2,1)S(1)}, bf16[144,384]{1,0:T(8,128)(2,1)S(1)}, u32[]{:S(2)}, u32[]{:S(2)}) collective-permute-start(bf16[144,384]{1,0:T(8,128)(2,1)S(1)} %collective-permute-done.6), channel_id=1, source_target_pairs={{8,0},{16,8},{24,16},{0,24},{9,1},{17,9},{25,17},{1,25},{10,2},{18... | collective-permute-start | bytes 331784 | tf_op jit(solution)/shard_map/ppermute | solution.py:28
  47.7 3.0 collective-permute-done.8
  52.3 3.7 collective-permute-done.9
  59.0 2.5 collective-permute-done.29
  61.5 3.6 collective-permute-start.11
  70.4 5.9 %collective-permute-done.10 = bf16[144,1536]{1,0:T(8,128)(2,1)S(1)} collective-permute-done((bf16[144,1536]{1,0:T(8,128)(2,1)S(1)}, bf16[144,1536]{1,0:T(8,128)(2,1)S(1)}, u32[]{:S(2)}, u32[]{:S(2)}) %collective-permute-start.10) | collective-permute-done | bytes 442400 | tf_op jit(solution)/shard_map/ppermute | solution.py:33
  76.9 23.0 %collective-permute-start.13 = (bf16[2,2,144,1536]{3,2,1,0:T(8,128)(2,1)S(1)}, bf16[2,2,144,1536]{3,2,1,0:T(8,128)(2,1)S(1)}, u32[]{:S(2)}, u32[]{:S(2)}) collective-permute-start(bf16[2,2,144,1536]{3,2,1,0:T(8,128)(2,1)S(1)} %pad_maximum_fusion.3), channel_id=1, source_target_pairs={{32,0},{0,32},{33,1},{1,33},{34,2},{2,34},{35,3},{3,35},{36,4},{4,... | collective-permute-start | bytes 5308424 | tf_op jit(solution)/shard_map/ppermute | solution.py:28
  101.2 3.1 collective-permute-start.35
  106.5 5.5 collective-permute-done.35
  112.0 4.8 collective-permute-done.36
  119.6 11.1 %collective-permute-done.37 = bf16[3,64,1536]{2,1,0:T(8,128)(2,1)S(1)} collective-permute-done((bf16[3,64,1536]{2,1,0:T(8,128)(2,1)S(1)}, bf16[3,64,1536]{2,1,0:T(8,128)(2,1)S(1)}, u32[]{:S(2)}, u32[]{:S(2)}) %collective-permute-start.37) | collective-permute-done | bytes 589856 | tf_op jit(solution)/shard_map/ppermute | solution.py:28
  134.2 10.1 %collective-permute-done.39 = bf16[3,64,1536]{2,1,0:T(8,128)(2,1)S(1)} collective-permute-done((bf16[3,64,1536]{2,1,0:T(8,128)(2,1)S(1)}, bf16[3,64,1536]{2,1,0:T(8,128)(2,1)S(1)}, u32[]{:S(2)}, u32[]{:S(2)}) %collective-permute-start.39) | collective-permute-done | bytes 589856 | tf_op jit(solution)/shard_map/ppermute | solution.py:28
  144.4 5.3 collective-permute-start.40
  157.1 3.8 collective-permute-done.18
  164.5 2.7 collective-permute-start.44
  171.3 4.8 collective-permute-start.46
  177.6 3.1 collective-permute-done.44
  180.6 7.3 %collective-permute-start.23 = (bf16[512,384]{1,0:T(8,128)(2,1)S(1)}, bf16[512,384]{1,0:T(8,128)(2,1)S(1)}, u32[]{:S(2)}, u32[]{:S(2)}) collective-permute-start(bf16[512,384]{1,0:T(8,128)(2,1)S(1)} %get-tuple-element.115), channel_id=1, source_target_pairs={{2,0},{3,1},{0,2},{1,3},{6,4},{7,5},{4,6},{5,7},{10,8},{11,9},{8,1... | collective-permute-start | bytes 1179656 | tf_op jit(solution)/shard_map/ppermute | solution.py:28
  188.0 3.5 collective-permute-start.22
  192.4 14.0 %collective-permute-done.24 = bf16[512,384]{1,0:T(8,128)(2,1)S(1)} collective-permute-done((bf16[512,384]{1,0:T(8,128)(2,1)S(1)}, bf16[512,384]{1,0:T(8,128)(2,1)S(1)}, u32[]{:S(2)}, u32[]{:S(2)}) %collective-permute-start.24) | collective-permute-done | bytes 393248 | tf_op jit(solution)/shard_map/ppermute | solution.py:28
  206.3 2.4 collective-permute-done.23
  213.2 2.9 add_reduce_fusion
  216.2 3.5 collective-permute-start.51
  229.2 2.5 collective-permute-start.43
  232.9 3.2 collective-permute-start.41
  238.2 6.6 %collective-permute-done.43 = bf16[512,384]{1,0:T(8,128)(2,1)S(1)} collective-permute-done((bf16[512,384]{1,0:T(8,128)(2,1)S(1)}, bf16[512,384]{1,0:T(8,128)(2,1)S(1)}, u32[]{:S(2)}, u32[]{:S(2)}) %collective-permute-start.43) | collective-permute-done | bytes 393248 | tf_op jit(solution)/shard_map/ppermute | solution.py:28
  246.4 8.7 %collective-permute-done.41 = bf16[512,384]{1,0:T(8,128)(2,1)S(1)} collective-permute-done((bf16[512,384]{1,0:T(8,128)(2,1)S(1)}, bf16[512,384]{1,0:T(8,128)(2,1)S(1)}, u32[]{:S(2)}, u32[]{:S(2)}) %collective-permute-start.41) | collective-permute-done | bytes 393248 | tf_op jit(solution)/shard_map/ppermute | solution.py:28
  260.2 7.5 %collective-permute-done.55 = bf16[512,384]{1,0:T(8,128)(2,1)S(1)} collective-permute-done((bf16[512,384]{1,0:T(8,128)(2,1)S(1)}, bf16[512,384]{1,0:T(8,128)(2,1)S(1)}, u32[]{:S(2)}, u32[]{:S(2)}) %collective-permute-start.55) | collective-permute-done | bytes 393248 | tf_op jit(solution)/shard_map/ppermute | solution.py:28
  267.7 4.3 collective-permute-done.54
  274.2 5.0 collective-permute-done.56
  282.3 4.0 fusion.53
  286.3 4.0 fusion.52
  290.4 2.8 fusion.165
  294.9 8.4 %fusion.54 = bf16[512,2,96]{0,2,1:T(8,128)(2,1)S(1)} fusion(bf16[1024,96,1]{0,1,2:T(8,128)(2,1)S(1)} %copy-done.54, f32[1024,512,2]{1,0,2:T(8,128)} %fusion.165, f32[2,512,1024]{1,2,0:T(8,128)} %copy-done.4, f32[2,512]{1,0:T(2,128)S(1)} %log_add_fusion), kind=kOutput, calls=%fused_computation.106 | convolution fusion | flops 208766976 | bytes 8785920 | tf_op jit(solution)/shard_map/hqk,kd->qhd/dot_general | solution.py:122
  303.3 8.4 %fusion.93 = bf16[1024,1,96]{0,2,1:T(8,128)(2,1)S(1)} fusion(f32[512,96]{0,1:T(8,128)S(1)} %copy-done.72, bf16[512,4,96]{0,2,1:T(8,128)(2,1)S(1)} %copy-done.20, f32[1024,512,2]{1,0,2:T(8,128)} %fusion.165, f32[2,512,1024]{1,2,0:T(8,128)} %copy-done.4, f32[2,512]{1,0:T(2,128)S(1)} %log_add_fusion), kind=kOutput, calls=%fused_computation.206 | convolution fusion | flops 208865280 | bytes 17375232 | tf_op jit(solution)/shard_map/hqk,qhd->kd/dot_general | solution.py:123
  314.1 6.0 %collective-permute-done.57 = bf16[512,4,96]{0,2,1:T(8,128)(2,1)S(1)} collective-permute-done((bf16[512,4,96]{0,2,1:T(8,128)(2,1)S(1)}, bf16[512,4,96]{0,2,1:T(8,128)(2,1)S(1)}, u32[]{:S(2)}, u32[]{:S(2)}) %collective-permute-start.57) | collective-permute-done | bytes 393248 | tf_op jit(solution)/shard_map/ppermute | solution.py:28
  325.2 13.3 %collective-permute-start.64 = (bf16[2,2,144,1536]{3,2,1,0:T(8,128)(2,1)}, bf16[2,2,144,1536]{3,2,1,0:T(8,128)(2,1)}, u32[]{:S(2)}, u32[]{:S(2)}) collective-permute-start(bf16[2,2,144,1536]{3,2,1,0:T(8,128)(2,1)} %fusion.32), channel_id=1, source_target_pairs={{32,0},{0,32},{33,1},{1,33},{34,2},{2,34},{35,3},{3,35},{36,4},{4,... | collective-permute-start | bytes 5308424 | tf_op jit(solution)/shard_map/ppermute | solution.py:28
  345.9 3.2 slice.796
  350.8 7.5 %fusion.7 = f32[2,2,144,1536]{3,2,1,0:T(8,128)S(1)} fusion(bf16[2,2,144,1536]{3,2,1,0:T(8,128)(2,1)} %collective-permute-done.64, f32[2,2,2,144,1536]{4,3,2,1,0:T(8,128)} %bitcast.394, pred[]{:T(512)S(6)} %eq.12), kind=kLoop, calls=%fused_computation.26 | loop fusion | flops 2654208 | bytes 12386305 | tf_op jit(solution)/shard_map/add | solution.py:263
  362.3 16.9 %collective-permute-done.67 = bf16[144,1536]{1,0:T(8,128)(2,1)S(1)} collective-permute-done((bf16[144,1536]{1,0:T(8,128)(2,1)S(1)}, bf16[144,1536]{1,0:T(8,128)(2,1)S(1)}, u32[]{:S(2)}, u32[]{:S(2)}) %collective-permute-start.67) | collective-permute-done | bytes 442400 | tf_op jit(solution)/shard_map/ppermute | solution.py:33
  382.5 3.8 collective-permute-start.69
  387.3 12.1 %fusion.146 = (bf16[3,512,1536]{2,1,0:T(8,128)(2,1)}, f32[3,512,1536]{2,1,0:T(8,128)}) fusion(bf16[3,512,1536]{2,1,0:T(8,128)(2,1)} %collective-permute-done.74, f32[3,1024,1536]{2,1,0:T(8,128)} %copy-done.2), kind=kLoop, calls=%fused_computation.349 | loop fusion | flops 7077888 | bytes 28311552 | tf_op jit(solution)/shard_map/convert.15
  399.3 3.9 fusion.149
  410.6 2.5 collective-permute-start.63
  413.1 2.7 collective-permute-start.62
  415.9 4.4 collective-permute-start.72
  421.8 2.7 collective-permute-start.76
  424.6 2.4 collective-permute-start.83
  429.9 8.4 %collective-permute-done.76 = bf16[3,64,1536]{2,1,0:T(8,128)(2,1)S(1)} collective-permute-done((bf16[3,64,1536]{2,1,0:T(8,128)(2,1)S(1)}, bf16[3,64,1536]{2,1,0:T(8,128)(2,1)S(1)}, u32[]{:S(2)}, u32[]{:S(2)}) %collective-permute-start.76) | collective-permute-done | bytes 589856 | tf_op jit(solution)/shard_map/ppermute | solution.py:33
  438.3 4.5 collective-permute-start.60
  442.8 7.1 %collective-permute-done.75 = bf16[3,64,1536]{2,1,0:T(8,128)(2,1)S(1)} collective-permute-done((bf16[3,64,1536]{2,1,0:T(8,128)(2,1)S(1)}, bf16[3,64,1536]{2,1,0:T(8,128)(2,1)S(1)}, u32[]{:S(2)}, u32[]{:S(2)}) %collective-permute-start.75) | collective-permute-done | bytes 589856 | tf_op jit(solution)/shard_map/ppermute | solution.py:33
  449.9 4.4 collective-permute-start.59
  456.4 2.5 fusion.142
  462.3 5.8 collective-permute-done.86
  474.6 3.1 collective-permute-done.78
  479.2 3.2 collective-permute-done.87
  484.1 3.0 collective-permute-done.88
  488.7 2.9 collective-permute-done.89
  491.8 4.3 collective-permute-start.90
  497.5 67.6 %all-reduce.2 = (f32[384]{0:T(512)}, f32[384]{0:T(512)}) all-reduce(f32[384]{0:T(512)S(1)} %get-tuple-element.120, f32[384]{0:T(512)S(1)} %get-tuple-element.119), channel_id=1, replica_groups=mesh['zl'=2,'core'=2,'y'=4,'zh'=2,'x'=4] {'zl','core','y','zh'}, use_global_device_ids=true, to_apply=%region_11.12 | all-reduce | flops 768 | bytes 6144 | tf_op jit(solution)/shard_map/psum | solution.py:274
  567.6 13.0 %collective-permute-done.91 = bf16[4,3,2,32,384]{4,3,1,0,2:T(8,128)(2,1)S(1)} collective-permute-done((bf16[4,3,2,32,384]{4,3,1,0,2:T(8,128)(2,1)S(1)}, bf16[4,3,2,32,384]{4,3,1,0,2:T(8,128)(2,1)S(1)}, u32[]{:S(2)}, u32[]{:S(2)}) %collective-permute-start.91) | collective-permute-done | bytes 589856 | tf_op jit(solution)/shard_map/ppermute | solution.py:28
  (447 shorter events, 156.0 us)
Async XLA Ops:
  2.1 13.1 %collective-permute-start.5 = (f32[2,384]{1,0:T(2,128)S(1)}, f32[2,384]{1,0:T(2,128)S(1)}, u32[]{:S(2)}, u32[]{:S(2)}) collective-permute-start(f32[2,384]{1,0:T(2,128)S(1)} %pad_maximum_fusion.27), channel_id=1, source_target_pairs={{3,0},{0,1},{1,2},{2,3},{7,4},{4,5},{5,6},{6,7},{11,8},{8,9},{9,10... | collective-permute-start | bytes 9224 | tf_op jit(solution)/shard_map/ppermute | solution.py:28
  4.2 12.6 %collective-permute-start.4 = (f32[2,384]{1,0:T(2,128)S(1)}, f32[2,384]{1,0:T(2,128)S(1)}, u32[]{:S(2)}, u32[]{:S(2)}) collective-permute-start(f32[2,384]{1,0:T(2,128)S(1)} %pad_maximum_fusion.27), channel_id=1, source_target_pairs={{2,0},{3,1},{0,2},{1,3},{6,4},{7,5},{4,6},{5,7},{10,8},{11,9},{8,1... | collective-permute-start | bytes 9224 | tf_op jit(solution)/shard_map/ppermute | solution.py:28
  6.7 12.5 %collective-permute-start.3 = (f32[2,384]{1,0:T(2,128)S(1)}, f32[2,384]{1,0:T(2,128)S(1)}, u32[]{:S(2)}, u32[]{:S(2)}) collective-permute-start(f32[2,384]{1,0:T(2,128)S(1)} %pad_maximum_fusion.27), channel_id=1, source_target_pairs={{1,0},{2,1},{3,2},{0,3},{5,4},{6,5},{7,6},{4,7},{9,8},{10,9},{11,1... | collective-permute-start | bytes 9224 | tf_op jit(solution)/shard_map/ppermute | solution.py:28
  7.8 58.2 %collective-permute-start.2 = (bf16[512,384]{1,0:T(8,128)(2,1)}, bf16[512,384]{1,0:T(8,128)(2,1)S(1)}, u32[]{:S(2)}, u32[]{:S(2)}) collective-permute-start(bf16[512,384]{1,0:T(8,128)(2,1)} %param.22), channel_id=1, source_target_pairs={{3,0},{0,1},{1,2},{2,3},{7,4},{4,5},{5,6},{6,7},{11,8},{8,9},{9,10... | collective-permute-start | bytes 1179656 | tf_op jit(solution)/shard_map/ppermute | solution.py:28
  8.1 59.0 %collective-permute-start.1 = (bf16[512,384]{1,0:T(8,128)(2,1)}, bf16[512,384]{1,0:T(8,128)(2,1)S(1)}, u32[]{:S(2)}, u32[]{:S(2)}) collective-permute-start(bf16[512,384]{1,0:T(8,128)(2,1)} %param.22), channel_id=1, source_target_pairs={{2,0},{3,1},{0,2},{1,3},{6,4},{7,5},{4,6},{5,7},{10,8},{11,9},{8,1... | collective-permute-start | bytes 1179656 | tf_op jit(solution)/shard_map/ppermute | solution.py:28
  19.2 10.0 %collective-permute-start.27 = (bf16[3,32,384]{2,1,0:T(8,128)(2,1)S(1)}, bf16[3,32,384]{2,1,0:T(8,128)(2,1)S(1)}, u32[]{:S(2)}, u32[]{:S(2)}) collective-permute-start(bf16[3,32,384]{2,1,0:T(8,128)(2,1)S(1)} %get-tuple-element.209), channel_id=1, source_target_pairs={{3,0},{0,1},{1,2},{2,3},{7,4},{4,5},{5,6},{6,7},{11,8},{8,9},{9,10... | collective-permute-start | bytes 221192 | tf_op jit(solution)/shard_map/ppermute | solution.py:28
  29.2 38.6 %collective-permute-start = (bf16[512,384]{1,0:T(8,128)(2,1)S(1)}, bf16[512,384]{1,0:T(8,128)(2,1)S(1)}, u32[]{:S(2)}, u32[]{:S(2)}) collective-permute-start(bf16[512,384]{1,0:T(8,128)(2,1)S(1)} %copy-done.8), channel_id=1, source_target_pairs={{1,0},{2,1},{3,2},{0,3},{5,4},{6,5},{7,6},{4,7},{9,8},{10,9},{11,1... | collective-permute-start | bytes 1179656 | tf_op jit(solution)/shard_map/ppermute | solution.py:28
  31.3 26.3 %collective-permute-start.28 = (bf16[3,16,1536]{2,1,0:T(8,128)(2,1)S(1)}, bf16[3,16,1536]{2,1,0:T(8,128)(2,1)S(1)}, u32[]{:S(2)}, u32[]{:S(2)}) collective-permute-start(bf16[3,16,1536]{2,1,0:T(8,128)(2,1)S(1)} %get-tuple-element.206), channel_id=1, source_target_pairs={{8,0},{16,8},{24,16},{0,24},{9,1},{17,9},{25,17},{1,25},{10,2},{18... | collective-permute-start | bytes 442376 | tf_op jit(solution)/shard_map/ppermute | solution.py:28
  35.7 9.8 %collective-permute-start.7 = (bf16[144,384]{1,0:T(8,128)(2,1)S(1)}, bf16[144,384]{1,0:T(8,128)(2,1)S(1)}, u32[]{:S(2)}, u32[]{:S(2)}) collective-permute-start(bf16[144,384]{1,0:T(8,128)(2,1)S(1)} %collective-permute-done.6), channel_id=1, source_target_pairs={{8,0},{16,8},{24,16},{0,24},{9,1},{17,9},{25,17},{1,25},{10,2},{18... | collective-permute-start | bytes 331784 | tf_op jit(solution)/shard_map/ppermute | solution.py:28
  61.5 15.0 %collective-permute-start.11 = (bf16[144,1536]{1,0:T(8,128)(2,1)S(1)}, bf16[144,1536]{1,0:T(8,128)(2,1)S(1)}, u32[]{:S(2)}, u32[]{:S(2)}) collective-permute-start(bf16[144,1536]{1,0:T(8,128)(2,1)S(1)} %pad_maximum_fusion.14), channel_id=1, source_target_pairs={{4,0},{0,4},{68,64},{64,68},{5,1},{1,5},{69,65},{65,69},{6,2},{2,6... | collective-permute-start | bytes 1327112 | tf_op jit(solution)/shard_map/ppermute | solution.py:33
  65.1 11.2 %collective-permute-start.10 = (bf16[144,1536]{1,0:T(8,128)(2,1)S(1)}, bf16[144,1536]{1,0:T(8,128)(2,1)S(1)}, u32[]{:S(2)}, u32[]{:S(2)}) collective-permute-start(bf16[144,1536]{1,0:T(8,128)(2,1)S(1)} %pad_maximum_fusion.14), channel_id=1, source_target_pairs={{64,0},{68,4},{0,64},{4,68},{65,1},{69,5},{1,65},{5,69},{66,2},{70... | collective-permute-start | bytes 1327112 | tf_op jit(solution)/shard_map/ppermute | solution.py:33
  66.0 10.4 %collective-permute-start.12 = (bf16[144,1536]{1,0:T(8,128)(2,1)S(1)}, bf16[144,1536]{1,0:T(8,128)(2,1)S(1)}, u32[]{:S(2)}, u32[]{:S(2)}) collective-permute-start(bf16[144,1536]{1,0:T(8,128)(2,1)S(1)} %pad_maximum_fusion.14), channel_id=1, source_target_pairs={{68,0},{64,4},{4,64},{0,68},{69,1},{65,5},{5,65},{1,69},{70,2},{66... | collective-permute-start | bytes 1327112 | tf_op jit(solution)/shard_map/ppermute | solution.py:33
  67.1 32.8 %collective-permute-start.31 = (bf16[3,64,1536]{2,1,0:T(8,128)(2,1)S(1)}, bf16[3,64,1536]{2,1,0:T(8,128)(2,1)S(1)}, u32[]{:S(2)}, u32[]{:S(2)}) collective-permute-start(bf16[3,64,1536]{2,1,0:T(8,128)(2,1)S(1)} %pad_maximum_fusion.11), channel_id=1, source_target_pairs={{64,0},{68,4},{0,64},{4,68},{65,1},{69,5},{1,65},{5,69},{66,2},{70... | collective-permute-start | bytes 1769480 | tf_op jit(solution)/shard_map/ppermute | solution.py:33
  67.9 32.1 %collective-permute-start.32 = (bf16[3,64,1536]{2,1,0:T(8,128)(2,1)S(1)}, bf16[3,64,1536]{2,1,0:T(8,128)(2,1)S(1)}, u32[]{:S(2)}, u32[]{:S(2)}) collective-permute-start(bf16[3,64,1536]{2,1,0:T(8,128)(2,1)S(1)} %pad_maximum_fusion.11), channel_id=1, source_target_pairs={{4,0},{0,4},{68,64},{64,68},{5,1},{1,5},{69,65},{65,69},{6,2},{2,6... | collective-permute-start | bytes 1769480 | tf_op jit(solution)/shard_map/ppermute | solution.py:33
  76.3 24.0 %collective-permute-start.33 = (bf16[3,64,1536]{2,1,0:T(8,128)(2,1)S(1)}, bf16[3,64,1536]{2,1,0:T(8,128)(2,1)S(1)}, u32[]{:S(2)}, u32[]{:S(2)}) collective-permute-start(bf16[3,64,1536]{2,1,0:T(8,128)(2,1)S(1)} %pad_maximum_fusion.11), channel_id=1, source_target_pairs={{68,0},{64,4},{4,64},{0,68},{69,1},{65,5},{5,65},{1,69},{70,2},{66... | collective-permute-start | bytes 1769480 | tf_op jit(solution)/shard_map/ppermute | solution.py:33
  76.9 54.0 %collective-permute-start.13 = (bf16[2,2,144,1536]{3,2,1,0:T(8,128)(2,1)S(1)}, bf16[2,2,144,1536]{3,2,1,0:T(8,128)(2,1)S(1)}, u32[]{:S(2)}, u32[]{:S(2)}) collective-permute-start(bf16[2,2,144,1536]{3,2,1,0:T(8,128)(2,1)S(1)} %pad_maximum_fusion.3), channel_id=1, source_target_pairs={{32,0},{0,32},{33,1},{1,33},{34,2},{2,34},{35,3},{3,35},{36,4},{4,... | collective-permute-start | bytes 5308424 | tf_op jit(solution)/shard_map/ppermute | solution.py:28
  101.2 10.7 %collective-permute-start.35 = (bf16[3,16,1536]{2,1,0:T(8,128)(2,1)S(1)}, bf16[3,16,1536]{2,1,0:T(8,128)(2,1)S(1)}, u32[]{:S(2)}, u32[]{:S(2)}) collective-permute-start(bf16[3,16,1536]{2,1,0:T(8,128)(2,1)S(1)} %get-tuple-element.203), channel_id=1, source_target_pairs={{4,0},{0,4},{68,64},{64,68},{5,1},{1,5},{69,65},{65,69},{6,2},{2,6... | collective-permute-start | bytes 442376 | tf_op jit(solution)/shard_map/ppermute | solution.py:33
  104.3 12.4 %collective-permute-start.36 = (bf16[3,16,1536]{2,1,0:T(8,128)(2,1)S(1)}, bf16[3,16,1536]{2,1,0:T(8,128)(2,1)S(1)}, u32[]{:S(2)}, u32[]{:S(2)}) collective-permute-start(bf16[3,16,1536]{2,1,0:T(8,128)(2,1)S(1)} %get-tuple-element.203), channel_id=1, source_target_pairs={{68,0},{64,4},{4,64},{0,68},{69,1},{65,5},{5,65},{1,69},{70,2},{66... | collective-permute-start | bytes 442376 | tf_op jit(solution)/shard_map/ppermute | solution.py:33
  116.8 14.0 %collective-permute-start.37 = (bf16[3,64,1536]{2,1,0:T(8,128)(2,1)S(1)}, bf16[3,64,1536]{2,1,0:T(8,128)(2,1)S(1)}, u32[]{:S(2)}, u32[]{:S(2)}) collective-permute-start(bf16[3,64,1536]{2,1,0:T(8,128)(2,1)S(1)} %pad_maximum_fusion.12), channel_id=1, source_target_pairs={{8,0},{16,8},{24,16},{0,24},{9,1},{17,9},{25,17},{1,25},{10,2},{18... | collective-permute-start | bytes 1769480 | tf_op jit(solution)/shard_map/ppermute | solution.py:28
  118.9 15.2 %collective-permute-start.38 = (bf16[3,64,1536]{2,1,0:T(8,128)(2,1)S(1)}, bf16[3,64,1536]{2,1,0:T(8,128)(2,1)S(1)}, u32[]{:S(2)}, u32[]{:S(2)}) collective-permute-start(bf16[3,64,1536]{2,1,0:T(8,128)(2,1)S(1)} %pad_maximum_fusion.12), channel_id=1, source_target_pairs={{16,0},{24,8},{0,16},{8,24},{17,1},{25,9},{1,17},{9,25},{18,2},{26... | collective-permute-start | bytes 1769480 | tf_op jit(solution)/shard_map/ppermute | solution.py:28
  118.9 25.4 %collective-permute-start.39 = (bf16[3,64,1536]{2,1,0:T(8,128)(2,1)S(1)}, bf16[3,64,1536]{2,1,0:T(8,128)(2,1)S(1)}, u32[]{:S(2)}, u32[]{:S(2)}) collective-permute-start(bf16[3,64,1536]{2,1,0:T(8,128)(2,1)S(1)} %pad_maximum_fusion.12), channel_id=1, source_target_pairs={{24,0},{0,8},{8,16},{16,24},{25,1},{1,9},{9,17},{17,25},{26,2},{2,... | collective-permute-start | bytes 1769480 | tf_op jit(solution)/shard_map/ppermute | solution.py:28
  133.9 15.8 %collective-permute-start.17 = (bf16[512,4,96]{0,2,1:T(8,128)(2,1)S(1)}, bf16[512,4,96]{0,2,1:T(8,128)(2,1)S(1)}, u32[]{:S(2)}, u32[]{:S(2)}) collective-permute-start(bf16[512,4,96]{0,2,1:T(8,128)(2,1)S(1)} %slice_bitcast_fusion.13), channel_id=1, source_target_pairs={{4,0},{0,4},{5,1},{1,5},{6,2},{2,6},{7,3},{3,7},{12,8},{8,12},{13,... | collective-permute-start | bytes 1179656 | tf_op jit(solution)/shard_map/ppermute | solution.py:28
  144.4 64.8 %collective-permute-start.40 = (bf16[3,512,1536]{2,1,0:T(8,128)(2,1)S(1)}, bf16[3,512,1536]{2,1,0:T(8,128)(2,1)S(1)}, u32[]{:S(2)}, u32[]{:S(2)}) collective-permute-start(bf16[3,512,1536]{2,1,0:T(8,128)(2,1)S(1)} %get-tuple-element.179), channel_id=1, source_target_pairs={{32,0},{0,32},{33,1},{1,33},{34,2},{2,34},{35,3},{3,35},{36,4},{4,... | collective-permute-start | bytes 14155784 | tf_op jit(solution)/shard_map/ppermute | solution.py:28
  164.5 11.5 %collective-permute-start.19 = (bf16[512,384]{1,0:T(8,128)(2,1)S(1)}, bf16[512,384]{1,0:T(8,128)(2,1)S(1)}, u32[]{:S(2)}, u32[]{:S(2)}) collective-permute-start(bf16[512,384]{1,0:T(8,128)(2,1)S(1)} %get-tuple-element.147), channel_id=1, source_target_pairs={{3,0},{0,1},{1,2},{2,3},{7,4},{4,5},{5,6},{6,7},{11,8},{8,9},{9,10... | collective-permute-start | bytes 1179656 | tf_op jit(solution)/shard_map/ppermute | solution.py:28
  164.5 16.1 %collective-permute-start.44 = (bf16[512,384]{1,0:T(8,128)(2,1)S(1)}, bf16[512,384]{1,0:T(8,128)(2,1)S(1)}, u32[]{:S(2)}, u32[]{:S(2)}) collective-permute-start(bf16[512,384]{1,0:T(8,128)(2,1)S(1)} %copy-done.21), channel_id=1, source_target_pairs={{1,0},{2,1},{3,2},{0,3},{5,4},{6,5},{7,6},{4,7},{9,8},{10,9},{11,1... | collective-permute-start | bytes 1179656 | tf_op jit(solution)/shard_map/ppermute | solution.py:28
  169.0 19.0 %collective-permute-start.45 = (bf16[512,384]{1,0:T(8,128)(2,1)S(1)}, bf16[512,384]{1,0:T(8,128)(2,1)S(1)}, u32[]{:S(2)}, u32[]{:S(2)}) collective-permute-start(bf16[512,384]{1,0:T(8,128)(2,1)S(1)} %copy-done.21), channel_id=1, source_target_pairs={{2,0},{3,1},{0,2},{1,3},{6,4},{7,5},{4,6},{5,7},{10,8},{11,9},{8,1... | collective-permute-start | bytes 1179656 | tf_op jit(solution)/shard_map/ppermute | solution.py:28
  171.3 21.0 %collective-permute-start.46 = (bf16[512,384]{1,0:T(8,128)(2,1)S(1)}, bf16[512,384]{1,0:T(8,128)(2,1)S(1)}, u32[]{:S(2)}, u32[]{:S(2)}) collective-permute-start(bf16[512,384]{1,0:T(8,128)(2,1)S(1)} %copy-done.21), channel_id=1, source_target_pairs={{3,0},{0,1},{1,2},{2,3},{7,4},{4,5},{5,6},{6,7},{11,8},{8,9},{9,10... | collective-permute-start | bytes 1179656 | tf_op jit(solution)/shard_map/ppermute | solution.py:28
  176.3 30.0 %collective-permute-start.24 = (bf16[512,384]{1,0:T(8,128)(2,1)S(1)}, bf16[512,384]{1,0:T(8,128)(2,1)S(1)}, u32[]{:S(2)}, u32[]{:S(2)}) collective-permute-start(bf16[512,384]{1,0:T(8,128)(2,1)S(1)} %get-tuple-element.115), channel_id=1, source_target_pairs={{3,0},{0,1},{1,2},{2,3},{7,4},{4,5},{5,6},{6,7},{11,8},{8,9},{9,10... | collective-permute-start | bytes 1179656 | tf_op jit(solution)/shard_map/ppermute | solution.py:28
  180.6 28.1 %collective-permute-start.23 = (bf16[512,384]{1,0:T(8,128)(2,1)S(1)}, bf16[512,384]{1,0:T(8,128)(2,1)S(1)}, u32[]{:S(2)}, u32[]{:S(2)}) collective-permute-start(bf16[512,384]{1,0:T(8,128)(2,1)S(1)} %get-tuple-element.115), channel_id=1, source_target_pairs={{2,0},{3,1},{0,2},{1,3},{6,4},{7,5},{4,6},{5,7},{10,8},{11,9},{8,1... | collective-permute-start | bytes 1179656 | tf_op jit(solution)/shard_map/ppermute | solution.py:28
  188.0 20.8 %collective-permute-start.22 = (bf16[512,384]{1,0:T(8,128)(2,1)S(1)}, bf16[512,384]{1,0:T(8,128)(2,1)S(1)}, u32[]{:S(2)}, u32[]{:S(2)}) collective-permute-start(bf16[512,384]{1,0:T(8,128)(2,1)S(1)} %get-tuple-element.115), channel_id=1, source_target_pairs={{1,0},{2,1},{3,2},{0,3},{5,4},{6,5},{7,6},{4,7},{9,8},{10,9},{11,1... | collective-permute-start | bytes 1179656 | tf_op jit(solution)/shard_map/ppermute | solution.py:28
  216.1 12.8 %collective-permute-start.52 = (f32[4,128]{1,0:T(4,128)S(1)}, f32[4,128]{1,0:T(4,128)S(1)}, u32[]{:S(2)}, u32[]{:S(2)}) collective-permute-start(f32[4,128]{1,0:T(4,128)S(1)} %bitcast.434), channel_id=1, source_target_pairs={{3,0},{0,1},{1,2},{2,3},{7,4},{4,5},{5,6},{6,7},{11,8},{8,9},{9,10... | collective-permute-start | bytes 6152 | tf_op jit(solution)/shard_map/ppermute | solution.py:28
  216.2 13.0 %collective-permute-start.51 = (f32[4,128]{1,0:T(4,128)S(1)}, f32[4,128]{1,0:T(4,128)S(1)}, u32[]{:S(2)}, u32[]{:S(2)}) collective-permute-start(f32[4,128]{1,0:T(4,128)S(1)} %bitcast.435), channel_id=1, source_target_pairs={{2,0},{3,1},{0,2},{1,3},{6,4},{7,5},{4,6},{5,7},{10,8},{11,9},{8,1... | collective-permute-start | bytes 6152 | tf_op jit(solution)/shard_map/ppermute | solution.py:28
  219.7 12.0 %collective-permute-start.50 = (f32[4,128]{1,0:T(4,128)S(1)}, f32[4,128]{1,0:T(4,128)S(1)}, u32[]{:S(2)}, u32[]{:S(2)}) collective-permute-start(f32[4,128]{1,0:T(4,128)S(1)} %bitcast.436), channel_id=1, source_target_pairs={{1,0},{2,1},{3,2},{0,3},{5,4},{6,5},{7,6},{4,7},{9,8},{10,9},{11,1... | collective-permute-start | bytes 6152 | tf_op jit(solution)/shard_map/ppermute | solution.py:28
  225.6 10.5 %collective-permute-start.48 = (bf16[512,384]{1,0:T(8,128)(2,1)S(1)}, bf16[512,384]{1,0:T(8,128)(2,1)S(1)}, u32[]{:S(2)}, u32[]{:S(2)}) collective-permute-start(bf16[512,384]{1,0:T(8,128)(2,1)S(1)} %get-tuple-element.143), channel_id=1, source_target_pairs={{2,0},{3,1},{0,2},{1,3},{6,4},{7,5},{4,6},{5,7},{10,8},{11,9},{8,1... | collective-permute-start | bytes 1179656 | tf_op jit(solution)/shard_map/ppermute | solution.py:28
  228.9 9.3 %collective-permute-start.47 = (bf16[512,384]{1,0:T(8,128)(2,1)S(1)}, bf16[512,384]{1,0:T(8,128)(2,1)S(1)}, u32[]{:S(2)}, u32[]{:S(2)}) collective-permute-start(bf16[512,384]{1,0:T(8,128)(2,1)S(1)} %get-tuple-element.141), channel_id=1, source_target_pairs={{3,0},{0,1},{1,2},{2,3},{7,4},{4,5},{5,6},{6,7},{11,8},{8,9},{9,10... | collective-permute-start | bytes 1179656 | tf_op jit(solution)/shard_map/ppermute | solution.py:28
  229.2 15.5 %collective-permute-start.43 = (bf16[512,384]{1,0:T(8,128)(2,1)S(1)}, bf16[512,384]{1,0:T(8,128)(2,1)S(1)}, u32[]{:S(2)}, u32[]{:S(2)}) collective-permute-start(bf16[512,384]{1,0:T(8,128)(2,1)S(1)} %get-tuple-element.145), channel_id=1, source_target_pairs={{1,0},{2,1},{3,2},{0,3},{5,4},{6,5},{7,6},{4,7},{9,8},{10,9},{11,1... | collective-permute-start | bytes 1179656 | tf_op jit(solution)/shard_map/ppermute | solution.py:28
  231.7 14.7 %collective-permute-start.42 = (bf16[512,384]{1,0:T(8,128)(2,1)S(1)}, bf16[512,384]{1,0:T(8,128)(2,1)S(1)}, u32[]{:S(2)}, u32[]{:S(2)}) collective-permute-start(bf16[512,384]{1,0:T(8,128)(2,1)S(1)} %get-tuple-element.146), channel_id=1, source_target_pairs={{2,0},{3,1},{0,2},{1,3},{6,4},{7,5},{4,6},{5,7},{10,8},{11,9},{8,1... | collective-permute-start | bytes 1179656 | tf_op jit(solution)/shard_map/ppermute | solution.py:28
  232.9 22.3 %collective-permute-start.41 = (bf16[512,384]{1,0:T(8,128)(2,1)S(1)}, bf16[512,384]{1,0:T(8,128)(2,1)S(1)}, u32[]{:S(2)}, u32[]{:S(2)}) collective-permute-start(bf16[512,384]{1,0:T(8,128)(2,1)S(1)} %get-tuple-element.144), channel_id=1, source_target_pairs={{3,0},{0,1},{1,2},{2,3},{7,4},{4,5},{5,6},{6,7},{11,8},{8,9},{9,10... | collective-permute-start | bytes 1179656 | tf_op jit(solution)/shard_map/ppermute | solution.py:28
  257.0 10.7 %collective-permute-start.55 = (bf16[512,384]{1,0:T(8,128)(2,1)S(1)}, bf16[512,384]{1,0:T(8,128)(2,1)S(1)}, u32[]{:S(2)}, u32[]{:S(2)}) collective-permute-start(bf16[512,384]{1,0:T(8,128)(2,1)S(1)} %get-tuple-element.110), channel_id=1, source_target_pairs={{3,0},{0,1},{1,2},{2,3},{7,4},{4,5},{5,6},{6,7},{11,8},{8,9},{9,10... | collective-permute-start | bytes 1179656 | tf_op jit(solution)/shard_map/ppermute | solution.py:28
  257.0 15.0 %collective-permute-start.54 = (bf16[512,384]{1,0:T(8,128)(2,1)S(1)}, bf16[512,384]{1,0:T(8,128)(2,1)S(1)}, u32[]{:S(2)}, u32[]{:S(2)}) collective-permute-start(bf16[512,384]{1,0:T(8,128)(2,1)S(1)} %get-tuple-element.110), channel_id=1, source_target_pairs={{2,0},{3,1},{0,2},{1,3},{6,4},{7,5},{4,6},{5,7},{10,8},{11,9},{8,1... | collective-permute-start | bytes 1179656 | tf_op jit(solution)/shard_map/ppermute | solution.py:28
  258.6 13.4 %collective-permute-start.53 = (bf16[512,384]{1,0:T(8,128)(2,1)S(1)}, bf16[512,384]{1,0:T(8,128)(2,1)S(1)}, u32[]{:S(2)}, u32[]{:S(2)}) collective-permute-start(bf16[512,384]{1,0:T(8,128)(2,1)S(1)} %get-tuple-element.110), channel_id=1, source_target_pairs={{1,0},{2,1},{3,2},{0,3},{5,4},{6,5},{7,6},{4,7},{9,8},{10,9},{11,1... | collective-permute-start | bytes 1179656 | tf_op jit(solution)/shard_map/ppermute | solution.py:28
  325.2 25.6 %collective-permute-start.64 = (bf16[2,2,144,1536]{3,2,1,0:T(8,128)(2,1)}, bf16[2,2,144,1536]{3,2,1,0:T(8,128)(2,1)}, u32[]{:S(2)}, u32[]{:S(2)}) collective-permute-start(bf16[2,2,144,1536]{3,2,1,0:T(8,128)(2,1)} %fusion.32), channel_id=1, source_target_pairs={{32,0},{0,32},{33,1},{1,33},{34,2},{2,34},{35,3},{3,35},{36,4},{4,... | collective-permute-start | bytes 5308424 | tf_op jit(solution)/shard_map/ppermute | solution.py:28
  349.1 38.2 %collective-permute-start.74 = (bf16[3,512,1536]{2,1,0:T(8,128)(2,1)}, bf16[3,512,1536]{2,1,0:T(8,128)(2,1)}, u32[]{:S(2)}, u32[]{:S(2)}) collective-permute-start(bf16[3,512,1536]{2,1,0:T(8,128)(2,1)} %slice.796), channel_id=1, source_target_pairs={{32,0},{0,32},{33,1},{1,33},{34,2},{2,34},{35,3},{3,35},{36,4},{4,... | collective-permute-start | bytes 14155784 | tf_op jit(solution)/shard_map/ppermute | solution.py:28
  358.6 20.6 %collective-permute-start.67 = (bf16[144,1536]{1,0:T(8,128)(2,1)S(1)}, bf16[144,1536]{1,0:T(8,128)(2,1)S(1)}, u32[]{:S(2)}, u32[]{:S(2)}) collective-permute-start(bf16[144,1536]{1,0:T(8,128)(2,1)S(1)} %get-tuple-element.155), channel_id=1, source_target_pairs={{68,0},{64,4},{4,64},{0,68},{69,1},{65,5},{5,65},{1,69},{70,2},{66... | collective-permute-start | bytes 1327112 | tf_op jit(solution)/shard_map/ppermute | solution.py:33
  360.9 18.3 %collective-permute-start.66 = (bf16[144,1536]{1,0:T(8,128)(2,1)S(1)}, bf16[144,1536]{1,0:T(8,128)(2,1)S(1)}, u32[]{:S(2)}, u32[]{:S(2)}) collective-permute-start(bf16[144,1536]{1,0:T(8,128)(2,1)S(1)} %fusion.80), channel_id=1, source_target_pairs={{4,0},{0,4},{68,64},{64,68},{5,1},{1,5},{69,65},{65,69},{6,2},{2,6... | collective-permute-start | bytes 1327112 | tf_op jit(solution)/shard_map/ppermute | solution.py:33
  361.0 18.9 %collective-permute-start.65 = (bf16[144,1536]{1,0:T(8,128)(2,1)S(1)}, bf16[144,1536]{1,0:T(8,128)(2,1)S(1)}, u32[]{:S(2)}, u32[]{:S(2)}) collective-permute-start(bf16[144,1536]{1,0:T(8,128)(2,1)S(1)} %get-tuple-element.154), channel_id=1, source_target_pairs={{64,0},{68,4},{0,64},{4,68},{65,1},{69,5},{1,65},{5,69},{66,2},{70... | collective-permute-start | bytes 1327112 | tf_op jit(solution)/shard_map/ppermute | solution.py:33
  381.7 23.4 %collective-permute-start.70 = (bf16[144,384]{1,0:T(8,128)(2,1)}, bf16[144,384]{1,0:T(8,128)(2,1)}, u32[]{:S(2)}, u32[]{:S(2)}) collective-permute-start(bf16[144,384]{1,0:T(8,128)(2,1)} %get-tuple-element.194), channel_id=1, source_target_pairs={{8,0},{16,8},{24,16},{0,24},{9,1},{17,9},{25,17},{1,25},{10,2},{18... | collective-permute-start | bytes 331784 | tf_op jit(solution)/shard_map/ppermute | solution.py:28
  382.5 22.7 %collective-permute-start.69 = (bf16[144,384]{1,0:T(8,128)(2,1)}, bf16[144,384]{1,0:T(8,128)(2,1)}, u32[]{:S(2)}, u32[]{:S(2)}) collective-permute-start(bf16[144,384]{1,0:T(8,128)(2,1)} %get-tuple-element.195), channel_id=1, source_target_pairs={{16,0},{24,8},{0,16},{8,24},{17,1},{25,9},{1,17},{9,25},{18,2},{26... | collective-permute-start | bytes 331784 | tf_op jit(solution)/shard_map/ppermute | solution.py:28
  386.3 18.9 %collective-permute-start.68 = (bf16[144,384]{1,0:T(8,128)(2,1)}, bf16[144,384]{1,0:T(8,128)(2,1)}, u32[]{:S(2)}, u32[]{:S(2)}) collective-permute-start(bf16[144,384]{1,0:T(8,128)(2,1)} %get-tuple-element.193), channel_id=1, source_target_pairs={{24,0},{0,8},{8,16},{16,24},{25,1},{1,9},{9,17},{17,25},{26,2},{2,... | collective-permute-start | bytes 331784 | tf_op jit(solution)/shard_map/ppermute | solution.py:28
  403.3 25.3 %collective-permute-start.77 = (bf16[3,64,1536]{2,1,0:T(8,128)(2,1)}, bf16[3,64,1536]{2,1,0:T(8,128)(2,1)}, u32[]{:S(2)}, u32[]{:S(2)}) collective-permute-start(bf16[3,64,1536]{2,1,0:T(8,128)(2,1)} %get-tuple-element.126), channel_id=1, source_target_pairs={{68,0},{64,4},{4,64},{0,68},{69,1},{65,5},{5,65},{1,69},{70,2},{66... | collective-permute-start | bytes 1769480 | tf_op jit(solution)/shard_map/ppermute | solution.py:33
  410.6 11.2 %collective-permute-start.63 = (f32[4,128]{1,0:T(4,128)S(1)}, f32[4,128]{1,0:T(4,128)S(1)}, u32[]{:S(2)}, u32[]{:S(2)}) collective-permute-start(f32[4,128]{1,0:T(4,128)S(1)} %bitcast.431), channel_id=1, source_target_pairs={{3,0},{0,1},{1,2},{2,3},{7,4},{4,5},{5,6},{6,7},{11,8},{8,9},{9,10... | collective-permute-start | bytes 6152 | tf_op jit(solution)/shard_map/ppermute | solution.py:28
  413.1 11.4 %collective-permute-start.62 = (f32[4,128]{1,0:T(4,128)S(1)}, f32[4,128]{1,0:T(4,128)S(1)}, u32[]{:S(2)}, u32[]{:S(2)}) collective-permute-start(f32[4,128]{1,0:T(4,128)S(1)} %bitcast.432), channel_id=1, source_target_pairs={{2,0},{3,1},{0,2},{1,3},{6,4},{7,5},{4,6},{5,7},{10,8},{11,9},{8,1... | collective-permute-start | bytes 6152 | tf_op jit(solution)/shard_map/ppermute | solution.py:28
  415.9 11.1 %collective-permute-start.72 = (bf16[144,384]{1,0:T(8,128)(2,1)}, bf16[144,384]{1,0:T(8,128)(2,1)S(1)}, u32[]{:S(2)}, u32[]{:S(2)}) collective-permute-start(bf16[144,384]{1,0:T(8,128)(2,1)} %collective-permute-done.71), channel_id=1, source_target_pairs={{32,0},{0,32},{33,1},{1,33},{34,2},{2,34},{35,3},{3,35},{36,4},{4,... | collective-permute-start | bytes 331784 | tf_op jit(solution)/shard_map/ppermute | solution.py:28
  421.8 16.5 %collective-permute-start.76 = (bf16[3,64,1536]{2,1,0:T(8,128)(2,1)S(1)}, bf16[3,64,1536]{2,1,0:T(8,128)(2,1)S(1)}, u32[]{:S(2)}, u32[]{:S(2)}) collective-permute-start(bf16[3,64,1536]{2,1,0:T(8,128)(2,1)S(1)} %copy-done.31), channel_id=1, source_target_pairs={{4,0},{0,4},{68,64},{64,68},{5,1},{1,5},{69,65},{65,69},{6,2},{2,6... | collective-permute-start | bytes 1769480 | tf_op jit(solution)/shard_map/ppermute | solution.py:33
  424.5 25.4 %collective-permute-start.75 = (bf16[3,64,1536]{2,1,0:T(8,128)(2,1)S(1)}, bf16[3,64,1536]{2,1,0:T(8,128)(2,1)S(1)}, u32[]{:S(2)}, u32[]{:S(2)}) collective-permute-start(bf16[3,64,1536]{2,1,0:T(8,128)(2,1)S(1)} %copy-done.30), channel_id=1, source_target_pairs={{64,0},{68,4},{0,64},{4,68},{65,1},{69,5},{1,65},{5,69},{66,2},{70... | collective-permute-start | bytes 1769480 | tf_op jit(solution)/shard_map/ppermute | solution.py:33
  424.6 29.8 %collective-permute-start.83 = (bf16[3,64,1536]{2,1,0:T(8,128)(2,1)S(1)}, bf16[3,64,1536]{2,1,0:T(8,128)(2,1)S(1)}, u32[]{:S(2)}, u32[]{:S(2)}) collective-permute-start(bf16[3,64,1536]{2,1,0:T(8,128)(2,1)S(1)} %copy-done.29), channel_id=1, source_target_pairs={{8,0},{16,8},{24,16},{0,24},{9,1},{17,9},{25,17},{1,25},{10,2},{18... | collective-permute-start | bytes 1769480 | tf_op jit(solution)/shard_map/ppermute | solution.py:28
  427.0 27.3 %collective-permute-start.82 = (bf16[3,64,1536]{2,1,0:T(8,128)(2,1)S(1)}, bf16[3,64,1536]{2,1,0:T(8,128)(2,1)S(1)}, u32[]{:S(2)}, u32[]{:S(2)}) collective-permute-start(bf16[3,64,1536]{2,1,0:T(8,128)(2,1)S(1)} %copy-done.28), channel_id=1, source_target_pairs={{16,0},{24,8},{0,16},{8,24},{17,1},{25,9},{1,17},{9,25},{18,2},{26... | collective-permute-start | bytes 1769480 | tf_op jit(solution)/shard_map/ppermute | solution.py:28
  428.6 27.8 %collective-permute-start.81 = (bf16[3,64,1536]{2,1,0:T(8,128)(2,1)S(1)}, bf16[3,64,1536]{2,1,0:T(8,128)(2,1)S(1)}, u32[]{:S(2)}, u32[]{:S(2)}) collective-permute-start(bf16[3,64,1536]{2,1,0:T(8,128)(2,1)S(1)} %copy-done.27), channel_id=1, source_target_pairs={{24,0},{0,8},{8,16},{16,24},{25,1},{1,9},{9,17},{17,25},{26,2},{2,... | collective-permute-start | bytes 1769480 | tf_op jit(solution)/shard_map/ppermute | solution.py:28
  438.3 57.8 %collective-permute-start.60 = (bf16[512,384]{1,0:T(8,128)(2,1)S(1)}, bf16[512,384]{1,0:T(8,128)(2,1)S(1)}, u32[]{:S(2)}, u32[]{:S(2)}) collective-permute-start(bf16[512,384]{1,0:T(8,128)(2,1)S(1)} %get-tuple-element.139), channel_id=1, source_target_pairs={{1,0},{2,1},{3,2},{0,3},{5,4},{6,5},{7,6},{4,7},{9,8},{10,9},{11,1... | collective-permute-start | bytes 1179656 | tf_op jit(solution)/shard_map/ppermute | solution.py:28
  449.9 46.2 %collective-permute-start.59 = (bf16[512,384]{1,0:T(8,128)(2,1)S(1)}, bf16[512,384]{1,0:T(8,128)(2,1)S(1)}, u32[]{:S(2)}, u32[]{:S(2)}) collective-permute-start(bf16[512,384]{1,0:T(8,128)(2,1)S(1)} %get-tuple-element.140), channel_id=1, source_target_pairs={{2,0},{3,1},{0,2},{1,3},{6,4},{7,5},{4,6},{5,7},{10,8},{11,9},{8,1... | collective-permute-start | bytes 1179656 | tf_op jit(solution)/shard_map/ppermute | solution.py:28
  472.2 24.0 %collective-permute-start.58 = (bf16[512,384]{1,0:T(8,128)(2,1)S(1)}, bf16[512,384]{1,0:T(8,128)(2,1)S(1)}, u32[]{:S(2)}, u32[]{:S(2)}) collective-permute-start(bf16[512,384]{1,0:T(8,128)(2,1)S(1)} %get-tuple-element.138), channel_id=1, source_target_pairs={{3,0},{0,1},{1,2},{2,3},{7,4},{4,5},{5,6},{6,7},{11,8},{8,9},{9,10... | collective-permute-start | bytes 1179656 | tf_op jit(solution)/shard_map/ppermute | solution.py:28
  474.6 90.6 %collective-permute-start.73 = (bf16[2,144,384]{2,1,0:T(8,128)(2,1)S(1)}, bf16[2,144,384]{2,1,0:T(8,128)(2,1)S(1)}, u32[]{:S(2)}, u32[]{:S(2)}) collective-permute-start(bf16[2,144,384]{2,1,0:T(8,128)(2,1)S(1)} %pad_maximum_fusion.23), channel_id=1, source_target_pairs={{64,0},{0,64},{65,1},{1,65},{66,2},{2,66},{67,3},{3,67},{68,4},{4,... | collective-permute-start | bytes 663560 | tf_op jit(solution)/shard_map/ppermute | solution.py:28
  491.8 73.4 %collective-permute-start.90 = (bf16[4,3,32,384]{3,2,1,0:T(8,128)(2,1)S(1)}, bf16[4,3,32,384]{3,2,1,0:T(8,128)(2,1)S(1)}, u32[]{:S(2)}, u32[]{:S(2)}) collective-permute-start(bf16[4,3,32,384]{3,2,1,0:T(8,128)(2,1)S(1)} %constant_dynamic-slice_fusion), channel_id=1, source_target_pairs={{32,0},{0,32},{33,1},{1,33},{34,2},{2,34},{35,3},{3,35},{36,4},{4,... | collective-permute-start | bytes 884744 | tf_op jit(solution)/shard_map/ppermute | solution.py:28
  565.4 15.3 %collective-permute-start.91 = (bf16[4,3,2,32,384]{4,3,1,0,2:T(8,128)(2,1)S(1)}, bf16[4,3,2,32,384]{4,3,1,0,2:T(8,128)(2,1)S(1)}, u32[]{:S(2)}, u32[]{:S(2)}) collective-permute-start(bf16[4,3,2,32,384]{4,3,1,0,2:T(8,128)(2,1)S(1)} %pad_maximum_fusion.13), channel_id=1, source_target_pairs={{64,0},{0,64},{65,1},{1,65},{66,2},{2,66},{67,3},{3,67},{68,4},{4,... | collective-permute-start | bytes 1769480 | tf_op jit(solution)/shard_map/ppermute | solution.py:28
  (101 other events, 1045.3 us)

commit v2 on v1

v2 whole, which is shorter than its diff:
```python
import functools
import math

import jax
import jax.numpy as jnp
import numpy as np
from jax import lax
from jax.experimental import pallas as pl
from jax.experimental.pallas import tpu as pltpu
from jax.sharding import Mesh
from jax.sharding import PartitionSpec as P

D = 1536
HD = 96
AXES = ("zl", "core", "y", "zh", "x")
DP_ROW = ("zl", "core", "y", "zh")
bf16 = jnp.bfloat16
f32 = jnp.float32
i32 = jnp.int32
MESH = pl.DeviceIdType.MESH
VM = pl.BlockSpec(memory_space=pltpu.VMEM)
ANY = pl.BlockSpec(memory_space=pl.ANY)

epsilon = 1e-05
rope_base = 100000.0
masked_score = -1e30
score_scale = math.log2(math.e) / math.sqrt(HD)
H0, H1 = pl.ds(0, 256), pl.ds(256, 256)


def dot(a, b):
    return lax.dot_general(a, b, (((1,), (0,)), ((), ())), preferred_element_type=f32)


def dot_t(a, b):
    return lax.dot_general(a, b, (((1,), (1,)), ((), ())), preferred_element_type=f32)


def lanes(index, width):
    return pl.ds(pl.multiple_of(index * width, 128), width)


class Place:
    def __init__(self):
        self.x, self.y = lax.axis_index("x"), lax.axis_index("y")
        self.zl, self.zh, self.core = lax.axis_index("zl"), lax.axis_index("zh"), lax.axis_index("core")
        self.quarter = self.zl * 2 + self.core
        self.ahead, self.behind, self.across = [(self.x + k) % 4 for k in (1, 3, 2)]
        self.right, self.left, self.far = {"x": self.ahead}, {"x": self.behind}, {"x": self.across}
        self.ys = [{"y": (self.y + k) % 4} for k in (1, 3, 2)]
        self.zs = [{"zl": 1 - self.zl}, {"zl": 1 - self.zl, "zh": 1 - self.zh}, {"zh": 1 - self.zh}]
        self.twin = {"core": 1 - self.core}
        self.mirror = {"x": self.y, "y": self.x}

    def enter(self):
        barrier = pltpu.get_barrier_semaphore()
        peers = [self.right, self.left, self.far, *self.ys, *self.zs, self.twin]
        for peer in peers:
            pl.semaphore_signal(barrier, inc=1, device_id=peer, device_id_type=MESH)

        @pl.when(self.x != self.y)
        def _():
            pl.semaphore_signal(barrier, inc=1, device_id=self.mirror, device_id_type=MESH)
            pl.semaphore_wait(barrier, len(peers) + 1)

        @pl.when(self.x == self.y)
        def _():
            pl.semaphore_wait(barrier, len(peers))


class Links:
    def __init__(self, send, recv, local):
        self.send, self.recv, self.local, self.count, self.local_count = send, recv, local, 0, 0
        self.open = []

    def make(self, src, dst, device):
        i = self.count
        self.count += 1
        return pltpu.make_async_remote_copy(
            src, dst, self.send.at[i], self.recv.at[i], device_id=device, device_id_type=MESH
        )

    def start(self, src, dst, device):
        copy = self.make(src, dst, device)
        copy.start()
        self.open.append(copy)
        return copy

    def spread(self, ref, devices):
        return [self.start(ref, ref, device) for device in devices]

    def keep(self, src, dst):
        copy = pltpu.make_async_copy(src, dst, self.local.at[self.local_count])
        self.local_count += 1
        copy.start()
        return copy

    def close(self):
        for copy in self.open:
            copy.wait_send()
        self.open = []


def arrive(copies):
    for copy in copies:
        copy.wait_recv()


class RingGather:
    def __init__(self, links, here, src, buf):
        cols = lanes(here.x, 384)
        self.links, self.here, self.buf = links, here, buf
        self.first = [
            links.start(src(H0), buf.at[H0, cols], here.right),
            links.start(src(H1), buf.at[H1, cols], here.left),
        ]
        self.second = [
            links.start(src(H1), buf.at[H1, cols], here.right),
            links.start(src(H0), buf.at[H0, cols], here.left),
        ]

    def forward(self):
        here, buf = self.here, self.buf
        self.first[0].wait_recv()
        a = buf.at[H0, lanes(here.behind, 384)]
        self.third = [self.links.start(a, a, here.right)]
        self.first[1].wait_recv()
        b = buf.at[H1, lanes(here.ahead, 384)]
        self.third += [self.links.start(b, b, here.left)]

    def finish(self):
        arrive(self.second)
        arrive(self.third)


class RingScatter:
    def __init__(self, links, here, part, slots):
        self.links, self.here, self.part, self.slots = links, here, part, slots

    def send_far(self):
        h, p, s = self.here, self.part, self.slots
        self.r0 = self.links.start(p.at[h.across, H0], s.at[0], h.right)
        self.l0 = self.links.start(p.at[h.across, H1], s.at[1], h.left)

    def send_near(self):
        h, p, s = self.here, self.part, self.slots
        self.r1 = self.links.start(p.at[h.ahead, H1], s.at[2], h.right)
        self.l1 = self.links.start(p.at[h.behind, H0], s.at[3], h.left)

    def forward(self):
        h, p, s = self.here, self.part, self.slots
        self.r0.wait_recv()
        p[h.ahead, H0] = (p[h.ahead, H0].astype(f32) + s[0].astype(f32)).astype(bf16)
        self.r2 = self.links.start(p.at[h.ahead, H0], s.at[4], h.right)
        self.l0.wait_recv()
        p[h.behind, H1] = (p[h.behind, H1].astype(f32) + s[1].astype(f32)).astype(bf16)
        self.l2 = self.links.start(p.at[h.behind, H1], s.at[5], h.left)

    def finish(self):
        arrive([self.r1, self.l1, self.r2, self.l2])

    def received(self, half):
        s = self.slots
        pair = (4, 3) if half == 0 else (2, 5)
        return s[pair[0]].astype(f32) + s[pair[1]].astype(f32)


def sine_cosine(angle):
    turns = jnp.floor(angle * (1.0 / (2.0 * math.pi)) + 0.5)
    r = angle - turns * 6.28125
    r = r - turns * 0.0019350051879882812
    r = r - turns * 3.0199159819185874e-07
    t = r * 0.5
    t2 = t * t
    s = 1.0 / 6227020800.0
    for c in (-1.0 / 39916800, 1.0 / 362880, -1.0 / 5040, 1.0 / 120, -1.0 / 6, 1.0):
        s = s * t2 + c
    s = s * t
    c_ = 1.0 / 479001600.0
    for c in (-1.0 / 3628800, 1.0 / 40320, -1.0 / 720, 1.0 / 24, -0.5, 1.0):
        c_ = c_ * t2 + c
    return 2.0 * s * c_, 1.0 - 2.0 * s * s


def turn(head, cosine, sine):
    return head * cosine + pltpu.roll(head, 64, 1) * sine


def forward_kernel(
    tokens, pos, gains, qkvw, ow, gw, uw, dw, cot, freq, perm, permo,
    a1, stats, qkv, kvr, att, cosb, sinb, middle, mf, cotf, gn, wqkv, wo, wg, wu, wd,
    xf, posb, wpad, acc, top, tot, packed, part, slots, send, recv, local,
):
    here = Place()
    links = Links(send, recv, local)
    x, y, zl, zh, core, quarter = here.x, here.y, here.zl, here.zh, here.core, here.quarter
    hid = zh * 4 + y
    here.enter()

    own_qkv = wqkv.at[zh, x, zl, core]
    own_o = wo.at[zh, zl, core, :, lanes(x, 384)]
    src_qkv, src_o = qkvw.at[pl.ds(quarter * 96, 96)], ow.at[pl.ds(quarter * 48, 48)]
    mirror = [links.make(src_qkv, own_qkv, here.mirror), links.make(src_o, own_o, here.mirror)]
    stay = [pltpu.make_async_copy(src_qkv, own_qkv, local.at[0]), pltpu.make_async_copy(src_o, own_o, local.at[1])]
    links.local_count = 2

    @pl.when(x != y)
    def _():
        for copy in mirror:
            copy.start()

    @pl.when(x == y)
    def _():
        for copy in stay:
            copy.start()

    ring_x = RingGather(links, here, lambda half: tokens.at[half], xf)
    kept = [links.keep(tokens, xf.at[:, lanes(x, 384)])]
    small = []
    for peer in (here.right, here.left, here.far):
        small += [links.start(pos, posb.at[x], peer), links.start(gains, gn.at[:, lanes(x, 384)], peer)]
    kept += [links.keep(pos, posb.at[x]), links.keep(gains, gn.at[:, lanes(x, 384)])]

    def hidden_slices(ref_g, ref_u, ref_d, target):
        rows = pl.ds(quarter * 96, 96)
        return [
            (ref_g.at[rows, lanes(target, 128)], wg.at[x, zl, core, :, lanes(hid, 128)]),
            (ref_u.at[rows, lanes(target, 128)], wu.at[x, zl, core, :, lanes(hid, 128)]),
            (ref_d.at[pl.ds(target * 128 + quarter * 32, 32)], wd.at[zh, y, zl, core, :, lanes(x, 384)]),
        ]

    swaps = []
    for peer, target in ((here.right, here.ahead), (here.left, here.behind), (here.far, here.across)):
        swaps += [links.start(src, dst, peer) for src, dst in hidden_slices(gw, uw, dw, target)]
    swap_kept = [links.keep(src, dst) for src, dst in hidden_slices(gw, uw, dw, x)]

    @pl.when(x != y)
    def _():
        for copy in mirror:
            copy.wait()

    @pl.when(x == y)
    def _():
        for copy in stay:
            copy.wait()

    a, b, oa, ob = pl.ds(0, 48), pl.ds(48, 48), pl.ds(0, 32), pl.ds(32, 16)
    y_cols = lanes(y, 384)
    head_a = links.spread(wqkv.at[zh, y, zl, core, a], here.ys)
    head_b = links.spread(wqkv.at[zh, y, zl, core, b], here.zs)
    head_a += links.spread(wo.at[zh, zl, core, oa, y_cols], here.ys)
    head_b += links.spread(wo.at[zh, zl, core, ob, y_cols], here.zs)
    ring_x.forward()
    arrive(head_a)
    head_a = links.spread(wqkv.at[zh, :, zl, core, a], here.zs)
    head_a += links.spread(wo.at[zh, zl, core, oa], here.zs)
    arrive(head_b)
    head_b = links.spread(wqkv.at[:, y, :, core, b], here.ys)
    head_b += links.spread(wo.at[:, :, core, ob, y_cols], here.ys)

    for copy in kept:
        copy.wait()
    arrive(small)
    mine = posb[y]
    mine = jnp.where(zh == 0, mine[0:4], mine[4:8]).astype(f32)
    lane = lax.broadcasted_iota(i32, (128, 128), 1)
    for c in range(4):
        column = jnp.broadcast_to(mine[c : c + 1], (128, 128)).T
        sine, cosine = sine_cosine(column * freq[0:1])
        cosb[pl.ds(c * 128, 128)] = cosine
        sinb[pl.ds(c * 128, 128)] = jnp.where(lane < 64, -sine, sine)

    ring_x.finish()
    ring_c = RingGather(links, here, lambda half: cot.at[half], cotf)
    cot_kept = links.keep(cot, cotf.at[:, lanes(x, 384)])

    def norm_rows(i, _):
        rows = pl.ds(pl.multiple_of(i * 64, 64), 64)
        value = xf[rows].astype(f32)
        inverse = lax.rsqrt(jnp.sum(value * value, axis=1, keepdims=True) * (1.0 / D) + epsilon)
        a1[rows] = (value * gn[0:1]).astype(bf16)
        stats[rows] = jnp.broadcast_to(inverse, (64, 128))
        return 0

    lax.fori_loop(0, 8, norm_rows, 0)

    arrive(head_a)
    arrive(head_b)
    core_qkv = links.spread(wqkv.at[:, :, :, core], [here.twin])
    core_o = links.spread(wo.at[:, :, core], [here.twin])

    for copy in swap_kept:
        copy.wait()
    arrive(swaps)
    hidden_a, hidden_b = [], []
    for ref in (wg, wu):
        hidden_a += links.spread(ref.at[:, zl, core, a, lanes(hid, 128)], here.ys)
        hidden_b += links.spread(ref.at[:, zl, core, b, lanes(hid, 128)], here.zs)
    da, db = pl.ds(0, 16), pl.ds(16, 16)
    hidden_a += links.spread(wd.at[zh, y, zl, core, da], here.ys)
    hidden_b += links.spread(wd.at[zh, y, zl, core, db], here.zs)

    arrive(core_qkv)

    def widen(i, _):
        rows = 4 * 96

        def block(j, _):
            w = wqkv[i, j].reshape(rows, 384)
            wpad[i, pl.ds(pl.multiple_of(j * rows, rows), rows)] = dot(w, perm[...]).astype(bf16)
            return 0

        lax.fori_loop(0, 4, block, 0)
        return 0

    lax.fori_loop(0, 2, widen, 0)

    def keys_values(g, _):
        pair = dot(a1[...], wpad[g, :, 256:512])
        inverse = stats[...]
        qkv[:, lanes(g * 4 + 2, 128)] = turn(pair[:, :128] * inverse, cosb[...], sinb[...]).astype(bf16)
        qkv[:, lanes(g * 4 + 3, 128)] = (pair[:, 128:] * inverse).astype(bf16)
        return 0

    lax.fori_loop(0, 2, keys_values, 0)
    over = [
        links.make(qkv.at[:, pl.ds(g * 512 + 256, 256)], kvr.at[g], here.zs[2]) for g in range(2)
    ]

    @pl.when(zh == 0)
    def _():
        for copy in over:
            copy.start()

    def queries(g, _):
        pair = dot(a1[...], wpad[g, :, 0:256])
        inverse = stats[...]
        for h in range(2):
            head = pair[:, h * 128 : h * 128 + 128] * inverse
            qkv[:, lanes(g * 4 + h, 128)] = turn(head, cosb[...], sinb[...]).astype(bf16)
        return 0

    lax.fori_loop(0, 2, queries, 0)
    ring_c.forward()

    def own_keys(i, _):
        g = i // 2
        for qb in range(2):
            rows, keys = pl.ds(qb * 256, 256), pl.ds(0, qb * 256 + 256)
            q = qkv[rows, lanes(g * 4 + i % 2, 128)]
            s = dot_t(q, qkv[keys, lanes(g * 4 + 2, 128)]) * score_scale
            index = lax.broadcasted_iota(i32, s.shape, 0) + qb * 256
            s = jnp.where(lax.broadcasted_iota(i32, s.shape, 1) <= index, s, masked_score)
            m = jnp.max(s, axis=1, keepdims=True)
            e = jnp.exp2(s - m)
            acc[i, rows] = dot(e.astype(bf16), qkv[keys, lanes(g * 4 + 3, 128)])
            top[i, rows] = jnp.broadcast_to(m, (256, 128))
            tot[i, rows] = jnp.broadcast_to(jnp.sum(e, axis=1, keepdims=True), (256, 128))
        return 0

    lax.fori_loop(0, 4, own_keys, 0)

    arrive(hidden_a)
    hidden_a = []
    for ref in (wg, wu):
        hidden_a += links.spread(ref.at[:, zl, core, a, lanes(zh, 512)], here.zs)
    hidden_a += links.spread(wd.at[zh, :, zl, core, da], here.zs)
    arrive(hidden_b)
    hidden_b = []
    for ref in (wg, wu):
        for other in range(2):
            hidden_b += links.spread(ref.at[:, :, core, b, lanes(other * 4 + y, 128)], here.ys)
    hidden_b += links.spread(wd.at[:, y, :, core, db], here.ys)

    @pl.when(zh == 1)
    def _():
        for copy in over:
            copy.wait_recv()

        def first_half(i, _):
            g = i // 2
            for qb in range(2):
                rows = pl.ds(qb * 256, 256)
                q = qkv[rows, lanes(g * 4 + i % 2, 128)]
                s = dot_t(q, kvr[g, :, 0:128]) * score_scale
                old = top[i, rows][:, 0:1]
                m = jnp.maximum(old, jnp.max(s, axis=1, keepdims=True))
                e = jnp.exp2(s - m)
                shrink = jnp.exp2(old - m)
                acc[i, rows] = acc[i, rows] * shrink + dot(e.astype(bf16), kvr[g, :, 128:256])
                tot[i, rows] = tot[i, rows] * shrink + jnp.sum(e, axis=1, keepdims=True)
                top[i, rows] = jnp.broadcast_to(m, (256, 128))
            return 0

        lax.fori_loop(0, 4, first_half, 0)

    @pl.when(zh == 0)
    def _():
        for copy in over:
            copy.wait_send()

    lane = lax.broadcasted_iota(i32, (512, 128), 1)
    for i in range(4):
        att[:, i * 128 : i * 128 + 128] = (acc[i] / tot[i]).astype(bf16)
        stats[...] = jnp.where(lane == i, top[i] + jnp.log2(tot[i]), stats[...])

    arrive(core_o)
    packed[...] = dot(att[...], permo[...]).astype(bf16)

    def project(block):
        w = wo[:, :, :, :, lanes(block, 384)].reshape(384, 384)
        return dot(packed[...], w)

    scatter = RingScatter(links, here, part, slots)
    part[here.across] = project(here.across).astype(bf16)
    scatter.send_far()
    part[here.ahead] = project(here.ahead).astype(bf16)
    part[here.behind] = project(here.behind).astype(bf16)
    scatter.send_near()
    middle[...] = project(x) + xf[:, lanes(x, 384)].astype(f32)
    scatter.forward()
    cot_kept.wait()
    ring_c.finish()
    scatter.finish()
    for half, rows in enumerate((H0, H1)):
        middle[rows] = middle[rows] + scatter.received(half)
    own = lanes(x, 384)
    mf[:, own] = middle[...].astype(bf16)
    ring_m = RingGather(links, here, lambda half: mf.at[half, own], mf)
    ring_m.forward()

    arrive(hidden_a)
    arrive(hidden_b)
    cores = [links.start(ref.at[:, :, core], ref.at[:, :, core], here.twin) for ref in (wg, wu)]
    cores.append(links.start(wd.at[:, :, :, core], wd.at[:, :, :, core], here.twin))
    ring_m.finish()
    arrive(cores)
    links.close()


def run_forward(tokens, pos, gains, qkvw, ow, gw, uw, dw, cot, consts):
    s = jax.ShapeDtypeStruct
    outs = [
        ("a1", (512, D), bf16, VM),
        ("stats", (512, 128), f32, VM),
        ("qkv", (512, 1024), bf16, VM),
        ("kvr", (2, 512, 256), bf16, VM),
        ("att", (512, 512), bf16, VM),
        ("cos", (512, 128), f32, VM),
        ("sin", (512, 128), f32, VM),
        ("middle", (512, 384), f32, VM),
        ("mf", (512, D), bf16, VM),
        ("cotf", (512, D), bf16, ANY),
        ("gn", (8, D), f32, VM),
        ("wqkv", (2, 4, 2, 2, 96, 384), bf16, VM),
        ("wo", (2, 2, 2, 48, D), bf16, VM),
        ("wg", (4, 2, 2, 96, 1024), bf16, ANY),
        ("wu", (4, 2, 2, 96, 1024), bf16, ANY),
        ("wd", (2, 4, 2, 2, 32, D), bf16, ANY),
    ]
    count = 128
    result = pl.pallas_call(
        forward_kernel,
        out_shape=[s(shape, dtype) for _, shape, dtype, _ in outs],
        in_specs=[ANY] * 9 + [VM] * 3,
        out_specs=[spec for _, _, _, spec in outs],
        scratch_shapes=[
            pltpu.VMEM((512, D), bf16),
            pltpu.VMEM((4, 8, 128), i32),
            pltpu.VMEM((2, D, 512), bf16),
            pltpu.VMEM((4, 512, 128), f32),
            pltpu.VMEM((4, 512, 128), f32),
            pltpu.VMEM((4, 512, 128), f32),
            pltpu.VMEM((512, 384), bf16),
            pltpu.VMEM((4, 512, 384), bf16),
            pltpu.VMEM((6, 256, 384), bf16),
            pltpu.SemaphoreType.DMA((count,)),
            pltpu.SemaphoreType.DMA((count,)),
            pltpu.SemaphoreType.DMA((16,)),
        ],
        compiler_params=pltpu.CompilerParams(
            collective_id=0, has_side_effects=True, vmem_limit_bytes=56 * 1024 * 1024
        ),
        name="forward",
    )(tokens, pos, gains, qkvw, ow, gw, uw, dw, cot, *consts)
    return {name: value for (name, _, _, _), value in zip(outs, result)}


def constants():
    half = HD // 2
    freq = np.zeros((8, 128), np.float32)
    rates = rope_base ** (-(np.arange(half) * 2.0 / HD))
    freq[:, :half] = rates
    freq[:, 64 : 64 + half] = rates
    perm = np.zeros((384, 512), np.float32)
    permo = np.zeros((512, 384), np.float32)
    for h in range(4):
        for d in range(HD):
            wide = d if (h == 3 or d < half) else d - half + 64
            perm[h * HD + d, h * 128 + wide] = 1
            permo[h * 128 + d, h * HD + d] = 1
    return jnp.asarray(freq), jnp.asarray(perm, bf16), jnp.asarray(permo, bf16)


def dot_first(a, b):
    return lax.dot_general(a, b, (((0,), (0,)), ((), ())), preferred_element_type=f32)


def column_to_rows(column, ref):
    for c in range(4):
        block = jnp.broadcast_to(column[c * 128 : c * 128 + 128], (128, 128)).T
        ref[c : c + 1] = block[0:1]


def rows_to_column(rows):
    return jnp.concatenate([jnp.broadcast_to(rows[c : c + 1], (128, 128)).T for c in range(4)], 0)


def backward_kernel(
    tokens, a1_in, stats, qkv, kvr, att, cosb, sinb, middle, mf_in, cotf, gn, wqkv_in, wo_in, wg_in, wu_in, wd_in,
    perm, permo,
    mixed, tgrad, dgain, fin_q, fin_o, fin_g, fin_u, fin_d,
    wqkv, wo, wg, wu, wd, a2, wide, hidden, dgate, dup, part, partd, slots, dzf, dmid, turned, datt, packed,
    dq, dkv, dkr, dks, dkin, dproj, small, sums, gains, rc_g, rc_u, rc_d, rc_q, rc_o,
    za_g, za_u, za_d, yb_g, yb_u, yb_d, ya_g, ya_u, ya_d, zb_g, zb_u, zb_d,
    za_q, za_o, yb_q, yb_o, ya_q, ya_o, zb_q, zb_o, send, recv, local,
):
    here = Place()
    links = Links(send, recv, local)
    x, y, zl, zh, core = here.x, here.y, here.zl, here.zh, here.core
    hid = zh * 4 + y
    own = lanes(x, 384)
    y_cols = lanes(y, 384)
    loads = [
        links.keep(src, dst)
        for src, dst in ((mf_in, a2), (wg_in, wg), (wu_in, wu), (wd_in, wd), (wo_in, wo), (wqkv_in, wqkv))
    ]
    dq[...] = jnp.zeros_like(dq)
    dkv[...] = jnp.zeros_like(dkv)
    here.enter()

    loads[0].wait()

    def norm_rows(i, _):
        rows = pl.ds(pl.multiple_of(i * 64, 64), 64)
        value = a2[rows].astype(f32)
        inverse = lax.rsqrt(jnp.sum(value * value, axis=1, keepdims=True) * (1.0 / D) + epsilon)
        a2[rows] = (value * inverse * gn[1:2]).astype(bf16)
        wide[rows] = jnp.broadcast_to(inverse, (64, 128))
        return 0

    lax.fori_loop(0, 8, norm_rows, 0)
    for copy in loads[1:4]:
        copy.wait()

    sums[...] = jnp.zeros_like(sums)

    def units(n, _):
        cols = lanes(n, 256)
        w_g = wg[:, :, :, :, cols].reshape(D, 256)
        w_u = wu[:, :, :, :, cols].reshape(D, 256)
        w_d = wd[n // 2, pl.ds((n % 2) * 2, 2)].reshape(256, D)
        for rows in (H0, H1):
            gate = dot(a2[rows], w_g)
            up = dot(a2[rows], w_u)
            dh = dot_t(cotf[rows], w_d)
            sg = 1.0 / (1.0 + jnp.exp(-gate))
            silu = gate * sg
            dg = (dh * up * (sg + silu * (1.0 - sg))).astype(bf16)
            du = (dh * silu).astype(bf16)
            hidden[rows, cols] = (silu * up).astype(bf16)
            dgate[rows, cols] = dg
            dup[rows, cols] = du
            inner = jnp.sum(dg.astype(f32) * gate + du.astype(f32) * up, axis=1, keepdims=True)
            sums[rows] = sums[rows] + inner
        return 0

    lax.fori_loop(0, 4, units, 0)

    def back_block(block):
        w_g = wg[block].reshape(384, 1024)
        w_u = wu[block].reshape(384, 1024)
        return dot_t(dgate[...], w_g) + dot_t(dup[...], w_u)

    scatter = RingScatter(links, here, part, slots.at[0])
    part[here.across] = back_block(here.across).astype(bf16)
    scatter.send_far()
    part[here.ahead] = back_block(here.ahead).astype(bf16)
    part[here.behind] = back_block(here.behind).astype(bf16)
    scatter.send_near()
    column_to_rows(sums[...], small.at[0, x])
    inner_sums = [links.start(small.at[0, x], small.at[0, x], p) for p in (here.right, here.left, here.far)]
    dmid[...] = back_block(x)
    scatter.forward()

    def down_block(block, _):
        cols = lanes(block, 384)
        partd[block] = dot(hidden[...], wd[:, :, :, :, :, cols].reshape(1024, 384)).astype(bf16)
        return 0

    lax.fori_loop(0, 4, down_block, 0)

    def down_grad(n, _):
        rows = hidden[:, lanes(n, 256)].T
        for c in range(3):
            cols = pl.ds(c * 512, 512)
            value = dot(rows, cotf[:, cols]).astype(bf16)
            wd[n // 2, pl.ds((n % 2) * 2, 2), :, :, :, cols] = value.reshape(2, 2, 2, 32, 512)
        return 0

    lax.fori_loop(0, 4, down_grad, 0)
    other = 1 - core
    cores = [links.start(wd.at[:, :, :, other], rc_d, here.twin)]

    def up_grads(block, _):
        rows = a2[:, lanes(block, 384)].T
        for source, target in ((dgate, wg), (dup, wu)):
            for c in range(2):
                cols = pl.ds(c * 512, 512)
                target[block, :, :, :, cols] = dot(rows, source[:, cols]).astype(bf16).reshape(2, 2, 96, 512)
        return 0

    lax.fori_loop(0, 4, up_grads, 0)
    cores += [
        links.start(wg.at[:, :, other], rc_g, here.twin),
        links.start(wu.at[:, :, other], rc_u, here.twin),
    ]
    load_a1 = links.keep(a1_in, a2)

    arrive(inner_sums)
    inner = rows_to_column(jnp.sum(small[0], axis=0)[0:4])[:, 0:1]
    scatter.finish()
    gains[...] = jnp.zeros_like(gains)
    for half, rows in enumerate((H0, H1)):
        da2 = dmid[rows] + scatter.received(half)
        m, inverse = middle[rows], wide[rows][:, 0:1]
        gains[1:2] = gains[1:2] + jnp.sum(da2 * m * inverse, axis=0, keepdims=True)
        factor = inner[half * 256 : half * 256 + 256] * inverse * inverse * (1.0 / D)
        value = cotf[rows, own].astype(f32) + inverse * gn[1:2, own] * da2 - m * factor
        dmid[rows] = value
        dzf[rows, own] = value.astype(bf16)
    ring_z = RingGather(links, here, lambda half: dzf.at[half, own], dzf)
    ring_z.forward()

    arrive(cores)

    def core_sum(i, _):
        for target, source in ((wg, rc_g), (wu, rc_u)):
            for j in range(2):
                target[i, j, core] = (target[i, j, core].astype(f32) + source[i, j].astype(f32)).astype(bf16)
        for k in range(2):
            for j in range(2):
                value = wd[k, i, j, core].astype(f32) + rc_d[k, i, j].astype(f32)
                wd[k, i, j, core] = value.astype(bf16)
        return 0

    lax.fori_loop(0, 4, core_sum, 0)
    a, b, da, db, oa, ob = pl.ds(0, 48), pl.ds(48, 48), pl.ds(0, 16), pl.ds(16, 16), pl.ds(0, 32), pl.ds(32, 16)
    z_places = [(1 - zl, zh), (1 - zl, 1 - zh), (zl, 1 - zh)]
    y_places = [(y + k) % 4 for k in (1, 3, 2)]
    round_a, round_b = [], []
    for j, (pzl, pzh) in enumerate(z_places):
        for ref, slot in ((wg, za_g), (wu, za_u)):
            round_a.append(links.start(ref.at[:, pzl, core, a, lanes(pzh, 512)], slot.at[j], here.zs[j]))
        round_a.append(links.start(wd.at[pzh, :, pzl, core, da], za_d.at[j], here.zs[j]))
    for j, py in enumerate(y_places):
        for ref, slot in ((wg, yb_g), (wu, yb_u)):
            for k in range(2):
                round_b.append(
                    links.start(ref.at[:, :, core, b, lanes(k * 4 + py, 128)], slot.at[j, k], here.ys[j])
                )
        round_b.append(links.start(wd.at[:, py, :, core, db], yb_d.at[j], here.ys[j]))

    ring_z.finish()

    scatter_d = RingScatter(links, here, partd, slots.at[1])
    scatter_d.send_far()
    scatter_d.send_near()

    loads[4].wait()
    packed[...] = dot_t(dzf[...], wo[...].reshape(384, D)).astype(bf16)
    datt[...] = dot_t(packed[...], permo[...]).astype(bf16)
    packed[...] = dot(att[...], permo[...]).astype(bf16)
    for c in range(3):
        cols = pl.ds(c * 512, 512)
        value = dot_first(packed[...], dzf[:, cols]).astype(bf16)
        wo[:, :, :, :, cols] = value.reshape(2, 2, 2, 48, 512)

    def pair(i, rows, k, v, visible):
        g = i // 2
        head = lanes(i, 128)
        q, grad = qkv[rows, lanes(g * 4 + i % 2, 128)], datt[rows, head]
        delta = jnp.sum(grad.astype(f32) * att[rows, head].astype(f32), axis=1, keepdims=True)
        lane = lax.broadcasted_iota(i32, (256, 128), 1)
        lse = jnp.sum(jnp.where(lane == i, stats[rows], 0.0), axis=1, keepdims=True)
        s = dot_t(q, k) * score_scale
        if visible is not None:
            s = jnp.where(visible(s.shape), s, masked_score)
        p = jnp.exp2(s - lse)
        ds = (p * (dot_t(grad, v) - delta) * (1.0 / math.sqrt(HD))).astype(bf16)
        dq[i, rows] = dq[i, rows] + dot(ds, k)
        return dot_first(ds, q), dot_first(p.astype(bf16), grad)

    give = [links.make(dks.at[g], dkin.at[g], here.zs[2]) for g in range(2)]

    @pl.when(zh == 1)
    def _():
        dkr[...] = jnp.zeros_like(dkr)

        def first_half(i, _):
            g = i // 2
            for qb in range(2):
                dk, dv = pair(i, pl.ds(qb * 256, 256), kvr[g, :, 0:128], kvr[g, :, 128:256], None)
                dkr[g, :, 0:128] = dkr[g, :, 0:128] + dk
                dkr[g, :, 128:256] = dkr[g, :, 128:256] + dv
            return 0

        for g in range(2):
            lax.fori_loop(2 * g, 2 * g + 2, first_half, 0)
            dks[g] = dkr[g].astype(bf16)
            give[g].start()

    scatter_d.forward()

    def own_keys(i, _):
        g = i // 2
        for qb in range(2):
            keys = pl.ds(0, qb * 256 + 256)

            def visible(shape):
                rows = lax.broadcasted_iota(i32, shape, 0) + qb * 256
                return lax.broadcasted_iota(i32, shape, 1) <= rows

            k, v = qkv[keys, lanes(g * 4 + 2, 128)], qkv[keys, lanes(g * 4 + 3, 128)]
            dk, dv = pair(i, pl.ds(qb * 256, 256), k, v, visible)
            dkv[g, keys, 0:128] = dkv[g, keys, 0:128] + dk
            dkv[g, keys, 128:256] = dkv[g, keys, 128:256] + dv
        return 0

    lax.fori_loop(0, 4, own_keys, 0)

    @pl.when(zh == 0)
    def _():
        for g in range(2):
            give[g].wait_recv()
            dkv[g] = dkv[g] + dkin[g].astype(f32)

    @pl.when(zh == 1)
    def _():
        for g in range(2):
            give[g].wait_send()

    arrive(round_a)
    for ref, slot in ((wg, za_g), (wu, za_u)):

        def add_z(i, _, ref=ref, slot=slot):
            cols = lanes(zh, 512)
            value = ref[i, zl, core, a, cols].astype(f32)
            for j in range(3):
                value = value + slot[j, i].astype(f32)
            ref[i, zl, core, a, cols] = value.astype(bf16)
            return 0

        lax.fori_loop(0, 4, add_z, 0)
    value = wd[zh, :, zl, core, da].astype(f32)
    for j in range(3):
        value = value + za_d[j].astype(f32)
    wd[zh, :, zl, core, da] = value.astype(bf16)
    round_a = []
    for j, py in enumerate(y_places):
        for ref, slot in ((wg, ya_g), (wu, ya_u)):
            round_a.append(
                links.start(ref.at[:, zl, core, a, lanes(zh * 4 + py, 128)], slot.at[j], here.ys[j])
            )
        round_a.append(links.start(wd.at[zh, py, zl, core, da], ya_d.at[j], here.ys[j]))
    arrive(round_b)
    for ref, slot in ((wg, yb_g), (wu, yb_u)):

        def add_y(i, _, ref=ref, slot=slot):
            for k in range(2):
                cols = lanes(k * 4 + y, 128)
                value = ref[i, :, core, b, cols].astype(f32)
                for j in range(3):
                    value = value + slot[j, k, i].astype(f32)
                ref[i, :, core, b, cols] = value.astype(bf16)
            return 0

        lax.fori_loop(0, 4, add_y, 0)
    value = wd[:, y, :, core, db].astype(f32)
    for j in range(3):
        value = value + yb_d[j].astype(f32)
    wd[:, y, :, core, db] = value.astype(bf16)
    round_b = []
    for j, (pzl, pzh) in enumerate(z_places):
        for ref, slot in ((wg, zb_g), (wu, zb_u)):
            round_b.append(
                links.start(ref.at[:, pzl, core, b, lanes(pzh * 4 + y, 128)], slot.at[j], here.zs[j])
            )
        round_b.append(links.start(wd.at[pzh, y, pzl, core, db], zb_d.at[j], here.zs[j]))

    sums[...] = jnp.zeros_like(sums)
    inverse = stats[:, 4:5]
    for i in range(4):
        q_cols = pl.ds((i // 2 * 4 + i % 2) * 128, 128)
        value = dq[i]
        sums[...] = sums[...] + jnp.sum(value * qkv[:, q_cols].astype(f32), axis=1, keepdims=True)
        turned[:, q_cols] = (turn(value, cosb[...], -sinb[...]) * inverse).astype(bf16)
    for g in range(2):
        kv_cols = pl.ds(g * 512 + 256, 256)
        value = dkv[g]
        sums[...] = sums[...] + jnp.sum(value * qkv[:, kv_cols].astype(f32), axis=1, keepdims=True)
        turned[:, g * 512 + 256 : g * 512 + 384] = (
            turn(value[:, :128], cosb[...], -sinb[...]) * inverse
        ).astype(bf16)
        turned[:, g * 512 + 384 : g * 512 + 512] = (value[:, 128:] * inverse).astype(bf16)
    column_to_rows(sums[...], small.at[1, x])
    inner_sums = [links.start(small.at[1, x], small.at[1, x], p) for p in (here.right, here.left, here.far)]
    for g in range(2):
        dproj[g] = dot_t(turned[:, g * 512 : g * 512 + 512], perm[...]).astype(bf16)
    loads[5].wait()

    def back_input(block):
        return sum(dot_t(dproj[g], wqkv[g, block].reshape(384, 384)) for g in range(2))

    scatter_d.finish()
    links.close()
    scatter = RingScatter(links, here, part, slots.at[2])
    part[here.across] = back_input(here.across).astype(bf16)
    scatter.send_far()
    part[here.ahead] = back_input(here.ahead).astype(bf16)
    part[here.behind] = back_input(here.behind).astype(bf16)
    scatter.send_near()
    tgrad[...] = back_input(x)

    load_a1.wait()

    def qkv_grads(block, _):
        rows = a2[:, lanes(block, 384)].T
        for g in range(2):
            wqkv[g, block] = dot(rows, dproj[g]).astype(bf16).reshape(2, 2, 96, 384)
        return 0

    lax.fori_loop(0, 4, qkv_grads, 0)
    cores = [
        links.start(wqkv.at[:, :, :, other], rc_q, here.twin),
        links.start(wo.at[:, :, other], rc_o, here.twin),
    ]
    scatter.forward()

    for half, rows in enumerate((H0, H1)):
        mixed[rows] = middle[rows] + partd[x, rows].astype(f32) + scatter_d.received(half)

    arrive(round_a)
    for ref, slot in ((wg, ya_g), (wu, ya_u)):
        cols = lanes(hid, 128)
        value = ref[:, zl, core, a, cols].astype(f32)
        for j in range(3):
            value = value + slot[j].astype(f32)
        ref[:, zl, core, a, cols] = value.astype(bf16)
    value = wd[zh, y, zl, core, da].astype(f32)
    for j in range(3):
        value = value + ya_d[j].astype(f32)
    wd[zh, y, zl, core, da] = value.astype(bf16)
    arrive(round_b)
    for ref, slot in ((wg, zb_g), (wu, zb_u)):
        cols = lanes(hid, 128)
        value = ref[:, zl, core, b, cols].astype(f32)
        for j in range(3):
            value = value + slot[j].astype(f32)
        ref[:, zl, core, b, cols] = value.astype(bf16)
    value = wd[zh, y, zl, core, db].astype(f32)
    for j in range(3):
        value = value + zb_d[j].astype(f32)
    wd[zh, y, zl, core, db] = value.astype(bf16)

    def hidden_blocks(target):
        return [
            (wg.at[target, zl, core, :, lanes(hid, 128)], fin_g.at[zl, core, :, lanes(x, 128)]),
            (wu.at[target, zl, core, :, lanes(hid, 128)], fin_u.at[zl, core, :, lanes(x, 128)]),
            (wd.at[zh, y, zl, core, :, lanes(target, 384)], fin_d.at[x, zl, core]),
        ]

    swaps = []
    for peer, target in ((here.right, here.ahead), (here.left, here.behind), (here.far, here.across)):
        swaps += [links.start(src, dst, peer) for src, dst in hidden_blocks(target)]
    swap_kept = [links.keep(src, dst) for src, dst in hidden_blocks(x)]

    arrive(cores)
    for g in range(2):

        def core_heads(i, _, g=g):
            for j in range(2):
                value = wqkv[g, i, j, core].astype(f32) + rc_q[g, i, j].astype(f32)
                wqkv[g, i, j, core] = value.astype(bf16)
            return 0

        lax.fori_loop(0, 4, core_heads, 0)
        for j in range(2):
            wo[g, j, core] = (wo[g, j, core].astype(f32) + rc_o[g, j].astype(f32)).astype(bf16)
    round_a, round_b = [], []
    for j, (pzl, pzh) in enumerate(z_places):
        round_a.append(links.start(wqkv.at[pzh, :, pzl, core, a], za_q.at[j], here.zs[j]))
        round_a.append(links.start(wo.at[pzh, pzl, core, oa], za_o.at[j], here.zs[j]))
    for j, py in enumerate(y_places):
        round_b.append(links.start(wqkv.at[:, py, :, core, b], yb_q.at[j], here.ys[j]))
        round_b.append(links.start(wo.at[:, :, core, ob, lanes(py, 384)], yb_o.at[j], here.ys[j]))

    arrive(inner_sums)
    inner = rows_to_column(jnp.sum(small[1], axis=0)[0:4])[:, 0:1]
    scatter.finish()
    for half, rows in enumerate((H0, H1)):
        da1 = tgrad[rows] + scatter.received(half)
        source, rinv = tokens[rows].astype(f32), stats[rows][:, 4:5]
        gains[0:1] = gains[0:1] + jnp.sum(da1 * source, axis=0, keepdims=True)
        factor = inner[half * 256 : half * 256 + 256] * rinv * rinv * (1.0 / D)
        tgrad[rows] = dmid[rows] + gn[0:1, own] * da1 - source * factor
    dgain[0] = gains[...]
    gain_y = [links.start(dgain.at[0], dgain.at[1 + j], here.ys[j]) for j in range(3)]

    for copy in swap_kept:
        copy.wait()
    arrive(swaps)
    fins = ((fin_g, 0), (fin_u, 0), (fin_d, 1))
    pick = lambda ref, lead, index: ref.at[(slice(None),) * lead + index]
    over = [pick(ref, lead, (zl, core)) for ref, lead in fins]
    across_zl = [links.start(v, v, here.zs[0]) for v in over]

    arrive(round_a)
    value = wqkv[zh, :, zl, core, a].astype(f32)
    value_o = wo[zh, zl, core, oa].astype(f32)
    for j in range(3):
        value = value + za_q[j].astype(f32)
        value_o = value_o + za_o[j].astype(f32)
    wqkv[zh, :, zl, core, a] = value.astype(bf16)
    wo[zh, zl, core, oa] = value_o.astype(bf16)
    round_a = []
    for j, py in enumerate(y_places):
        round_a.append(links.start(wqkv.at[zh, py, zl, core, a], ya_q.at[j], here.ys[j]))
        round_a.append(links.start(wo.at[zh, zl, core, oa, lanes(py, 384)], ya_o.at[j], here.ys[j]))
    arrive(round_b)
    value = wqkv[:, y, :, core, b].astype(f32)
    value_o = wo[:, :, core, ob, y_cols].astype(f32)
    for j in range(3):
        value = value + yb_q[j].astype(f32)
        value_o = value_o + yb_o[j].astype(f32)
    wqkv[:, y, :, core, b] = value.astype(bf16)
    wo[:, :, core, ob, y_cols] = value_o.astype(bf16)
    round_b = []
    for j, (pzl, pzh) in enumerate(z_places):
        round_b.append(links.start(wqkv.at[pzh, y, pzl, core, b], zb_q.at[j], here.zs[j]))
        round_b.append(links.start(wo.at[pzh, pzl, core, ob, y_cols], zb_o.at[j], here.zs[j]))

    arrive(gain_y)
    gains[...] = dgain[0] + dgain[1] + dgain[2] + dgain[3]
    dgain[4] = gains[...]
    gain_z = [links.start(dgain.at[4], dgain.at[5 + j], here.zs[j]) for j in range(3)]
    arrive(across_zl)
    both = [pick(ref, lead, (slice(None), core)) for ref, lead in fins]
    to_core = [links.start(v, v, here.twin) for v in both]

    arrive(round_a)
    value = wqkv[zh, y, zl, core, a].astype(f32)
    value_o = wo[zh, zl, core, oa, y_cols].astype(f32)
    for j in range(3):
        value = value + ya_q[j].astype(f32)
        value_o = value_o + ya_o[j].astype(f32)
    wqkv[zh, y, zl, core, a] = value.astype(bf16)
    wo[zh, zl, core, oa, y_cols] = value_o.astype(bf16)
    arrive(round_b)
    value = wqkv[zh, y, zl, core, b].astype(f32)
    value_o = wo[zh, zl, core, ob, y_cols].astype(f32)
    for j in range(3):
        value = value + zb_q[j].astype(f32)
        value_o = value_o + zb_o[j].astype(f32)
    wqkv[zh, y, zl, core, b] = value.astype(bf16)
    wo[zh, zl, core, ob, y_cols] = value_o.astype(bf16)
    src_q, src_o = wqkv.at[zh, y, zl, core], wo.at[zh, zl, core, :, y_cols]
    dst_q, dst_o = fin_q.at[zl, core], fin_o.at[zl, core]
    mirror = [links.make(src_q, dst_q, here.mirror), links.make(src_o, dst_o, here.mirror)]
    first = links.local_count
    stay = [pltpu.make_async_copy(src_q, dst_q, local.at[first]), pltpu.make_async_copy(src_o, dst_o, local.at[first + 1])]

    @pl.when(x != y)
    def _():
        for copy in mirror:
            copy.start()
        for copy in mirror:
            copy.wait()

    @pl.when(x == y)
    def _():
        for copy in stay:
            copy.start()
        for copy in stay:
            copy.wait()

    head_zl = [links.start(v, v, here.zs[0]) for v in (fin_q.at[zl, core], fin_o.at[zl, core])]
    arrive(gain_z)
    gains[...] = dgain[4] + dgain[5] + dgain[6] + dgain[7]
    dgain[8] = gains[...]
    gain_c = links.start(dgain.at[8], dgain.at[9], here.twin)
    arrive(head_zl)
    head_core = [links.start(v, v, here.twin) for v in (fin_q.at[:, core], fin_o.at[:, core])]
    arrive([gain_c])
    arrive(to_core)
    arrive(head_core)
    links.close()


def run_backward(tokens, k, consts):
    s = jax.ShapeDtypeStruct
    v = pltpu.VMEM
    _, perm, permo = consts
    outs = [
        s((512, 384), f32),
        s((512, 384), f32),
        s((10, 8, 384), f32),
        s((2, 2, 96, 384), bf16),
        s((2, 2, 48, 384), bf16),
        s((2, 2, 96, 512), bf16),
        s((2, 2, 96, 512), bf16),
        s((4, 2, 2, 32, 384), bf16),
    ]
    scratch = [
        v((2, 4, 2, 2, 96, 384), bf16),
        v((2, 2, 2, 48, D), bf16),
        v((4, 2, 2, 96, 1024), bf16),
        v((4, 2, 2, 96, 1024), bf16),
        v((2, 4, 2, 2, 32, D), bf16),
        v((512, D), bf16),
        v((512, 128), f32),
        v((512, 1024), bf16),
        v((512, 1024), bf16),
        v((512, 1024), bf16),
        v((4, 512, 384), bf16),
        v((4, 512, 384), bf16),
        v((3, 6, 256, 384), bf16),
        v((512, D), bf16),
        v((512, 384), f32),
        v((512, 1024), bf16),
        v((512, 512), bf16),
        v((512, 384), bf16),
        v((4, 512, 128), f32),
        v((2, 512, 256), f32),
        v((2, 512, 256), f32),
        v((2, 512, 256), bf16),
        v((2, 512, 256), bf16),
        v((2, 512, 384), bf16),
        v((2, 4, 8, 128), f32),
        v((512, 1), f32),
        v((8, 384), f32),
        v((4, 2, 96, 1024), bf16),
        v((4, 2, 96, 1024), bf16),
        v((2, 4, 2, 32, D), bf16),
        v((2, 4, 2, 96, 384), bf16),
        v((2, 2, 48, D), bf16),
        v((3, 4, 48, 512), bf16),
        v((3, 4, 48, 512), bf16),
        v((3, 4, 16, D), bf16),
        v((3, 2, 4, 2, 48, 128), bf16),
        v((3, 2, 4, 2, 48, 128), bf16),
        v((3, 2, 2, 16, D), bf16),
        v((3, 4, 48, 128), bf16),
        v((3, 4, 48, 128), bf16),
        v((3, 16, D), bf16),
        v((3, 4, 48, 128), bf16),
        v((3, 4, 48, 128), bf16),
        v((3, 16, D), bf16),
        v((3, 4, 48, 384), bf16),
        v((3, 32, D), bf16),
        v((3, 2, 2, 48, 384), bf16),
        v((3, 2, 2, 16, 384), bf16),
        v((3, 48, 384), bf16),
        v((3, 32, 384), bf16),
        v((3, 48, 384), bf16),
        v((3, 16, 384), bf16),
        pltpu.SemaphoreType.DMA((150,)),
        pltpu.SemaphoreType.DMA((150,)),
        pltpu.SemaphoreType.DMA((16,)),
    ]
    names = [
        ("a1", ANY), ("stats", VM), ("qkv", VM), ("kvr", VM), ("att", VM), ("cos", VM), ("sin", VM),
        ("middle", VM), ("mf", ANY), ("cotf", VM), ("gn", VM), ("wqkv", ANY), ("wo", ANY),
        ("wg", ANY), ("wu", ANY), ("wd", ANY),
    ]
    return pl.pallas_call(
        backward_kernel,
        out_shape=outs,
        in_specs=[VM] + [spec for _, spec in names] + [VM, VM],
        out_specs=[VM] * len(outs),
        scratch_shapes=scratch,
        compiler_params=pltpu.CompilerParams(
            collective_id=1, has_side_effects=True, vmem_limit_bytes=63 * 1024 * 1024
        ),
        name="backward",
    )(tokens, *[k[name] for name, _ in names], perm, permo)


def per_device(
    tokens,
    positions,
    attn_gain,
    qkv_weight,
    output_weight,
    ffn_gain,
    gate_weight,
    up_weight,
    down_weight,
    cotangent,
):
    consts = constants()
    gains = jnp.concatenate([attn_gain[None], ffn_gain[None], jnp.zeros((6, 384), f32)], 0)
    kept = run_forward(
        tokens, positions.reshape(8, 128), gains, qkv_weight, output_weight,
        gate_weight, up_weight, down_weight, cotangent, consts,
    )
    mixed, tgrad, dgain, g_q, g_o, g_g, g_u, g_d = run_backward(tokens, kept, consts)
    dgain = dgain[8] + dgain[9]
    return (
        mixed,
        tgrad,
        dgain[0],
        g_q.reshape(384, 384).astype(f32),
        g_o.reshape(192, 384).astype(f32),
        dgain[1],
        g_g.reshape(384, 512).astype(f32),
        g_u.reshape(384, 512).astype(f32),
        g_d.reshape(512, 384).astype(f32),
    )


def solution(mesh):
    finer = Mesh(mesh.devices.reshape(2, 2, 4, 2, 4), AXES)
    row = ("y", "zh")
    in_specs = (
        P(DP_ROW, "x"),
        P(("zl", "core", "x")),
        P("x"),
        P("x", row),
        P(row, "x"),
        P("x"),
        P("x", row),
        P("x", row),
        P(row, "x"),
        P(DP_ROW, "x"),
    )
    out_specs = (
        P(DP_ROW, "x"),
        P(DP_ROW, "x"),
        P("x"),
        P("x", row),
        P(row, "x"),
        P("x"),
        P("x", row),
        P("x", row),
        P(row, "x"),
    )
    return jax.shard_map(per_device, mesh=finer, in_specs=in_specs, out_specs=out_specs, check_vma=False)
```

time: 594 us -> 237 us (0.40)
  the two profiles are of different devices: /device:TPU:1 before, /device:TPU:25 now
where the time goes in v2:
time: 237 us
  Pallas kernels  224 us (95%)
  other arithmetic  8.4 us (4%)
  local copies, waits for them, and re-layouts  3.82 us (2%)
    pallas_call x1, Pallas kernels, run_backward(): pl.pallas_call(backward_kernel, out_shape=outs, in_specs=[VM] + [spec for...  139 us
    pallas_call x1, Pallas kernels, run_forward(): pl.pallas_call(forward_kernel, out_shape=[s(shape, dtype) for _, shape, d...  85.2 us

profile of v2, /device:TPU:25, one launch (start us, length us, event | category | flops | bytes accessed | tf_op | source)
XLA Modules:
  0.0 236.9 jit_solution(556679480918294934)
XLA Ops:
  0.7 0.1 pad.2.clone
  0.7 0.7 broadcast_in_dim.9
  1.4 0.7 broadcast_in_dim.10
  2.1 0.7 maximum_maximum_fusion.gains
  2.8 85.2 %forward.1 = (bf16[512,1536]{1,0:T(8,128)(2,1)}, f32[512,128]{1,0:T(8,128)}, bf16[512,1024]{1,0:T(8,128)(2,1)}, bf16[2,512,256]{2,1,0:T(8,128)(2,1)}, bf16[512,5...) custom-call(bf16[512,384]{1,0:T(8,128)(2,1)} %tokens.3, ...), custom_call_target="tpu_custom_call" | custom-call | tf_op jit(solution)/shard_map/forward/pallas_call | solution.py:462
  87.9 138.8 %backward.1 = (f32[512,384]{1,0:T(8,128)}, f32[512,384]{1,0:T(8,128)}, f32[10,8,384]{2,1,0:T(8,128)}, bf16[2,2,96,384]{3,2,1,0:T(8,128)(2,1)}, bf16[2,2,48,384]{...) custom-call(bf16[512,384]{1,0:T(8,128)(2,1)} %tokens.3, ...), custom_call_target="tpu_custom_call" | custom-call | tf_op jit(solution)/shard_map/backward/pallas_call | solution.py:1086
  226.8 0.0 copy-start.2
  226.8 0.0 copy-start.3
  226.8 0.8 slice_add_fusion
  227.6 0.6 slice_reduce_fusion
  228.2 0.0 copy-start.1
  228.2 1.7 bitcast_convert_fusion.4
  229.9 1.8 bitcast_convert_fusion.3
  231.7 0.0 copy-start
  231.7 2.0 bitcast_convert_fusion
  233.7 0.0 copy-done.2
  233.7 0.0 copy-done.3
  233.7 1.4 bitcast_convert_fusion.1
  235.1 0.0 copy-done.1
  235.1 0.9 copy.24
  236.0 0.0 copy-done
  236.0 0.9 copy.25
  (1 shorter events, 0.0 us)
Async XLA Ops:
  226.8 7.0 %copy-start.2 = (bf16[2,2,96,512]{3,2,1,0:T(8,128)(2,1)S(1)}, bf16[2,2,96,512]{3,2,1,0:T(8,128)(2,1)}, u32[]{:S(2)}) copy-start(bf16[2,2,96,512]{3,2,1,0:T(8,128)(2,1)} %get-tuple-element.54) | copy-start | bytes 1179652
  226.8 7.0 %copy-start.3 = (bf16[2,2,96,512]{3,2,1,0:T(8,128)(2,1)S(1)}, bf16[2,2,96,512]{3,2,1,0:T(8,128)(2,1)}, u32[]{:S(2)}) copy-start(bf16[2,2,96,512]{3,2,1,0:T(8,128)(2,1)} %get-tuple-element.55) | copy-start | bytes 1179652
  228.2 6.9 %copy-start.1 = (f32[512,384]{1,0:T(8,128)S(1)}, f32[512,384]{1,0:T(8,128)}, u32[]{:S(2)}) copy-start(f32[512,384]{1,0:T(8,128)} %get-tuple-element.70) | copy-start | bytes 2359300
  231.7 4.3 %copy-start = (f32[512,384]{1,0:T(8,128)S(1)}, f32[512,384]{1,0:T(8,128)}, u32[]{:S(2)}) copy-start(f32[512,384]{1,0:T(8,128)} %get-tuple-element.71) | copy-start | bytes 2359300

commit v3 on v1

v3 whole, which is shorter than its diff:
```python
import functools
import math

import jax
import jax.numpy as jnp
import numpy as np
from jax import lax
from jax.experimental import pallas as pl
from jax.experimental.pallas import tpu as pltpu
from jax.sharding import Mesh
from jax.sharding import PartitionSpec as P

D = 1536
HD = 96
AXES = ("zl", "core", "y", "zh", "x")
DP_ROW = ("zl", "core", "y", "zh")
bf16 = jnp.bfloat16
f32 = jnp.float32
i32 = jnp.int32
MESH = pl.DeviceIdType.MESH
VM = pl.BlockSpec(memory_space=pltpu.VMEM)
ANY = pl.BlockSpec(memory_space=pl.ANY)

epsilon = 1e-05
rope_base = 100000.0
masked_score = -1e30
score_scale = math.log2(math.e) / math.sqrt(HD)
H0, H1 = pl.ds(0, 256), pl.ds(256, 256)


def dot(a, b):
    return lax.dot_general(a, b, (((1,), (0,)), ((), ())), preferred_element_type=f32)


def dot_t(a, b):
    return lax.dot_general(a, b, (((1,), (1,)), ((), ())), preferred_element_type=f32)


def lanes(index, width):
    return pl.ds(pl.multiple_of(index * width, 128), width)


class Place:
    def __init__(self):
        self.x, self.y = lax.axis_index("x"), lax.axis_index("y")
        self.zl, self.zh, self.core = lax.axis_index("zl"), lax.axis_index("zh"), lax.axis_index("core")
        self.quarter = self.zl * 2 + self.core
        self.ahead, self.behind, self.across = [(self.x + k) % 4 for k in (1, 3, 2)]
        self.right, self.left, self.far = {"x": self.ahead}, {"x": self.behind}, {"x": self.across}
        self.ys = [{"y": (self.y + k) % 4} for k in (1, 3, 2)]
        self.zs = [{"zl": 1 - self.zl}, {"zl": 1 - self.zl, "zh": 1 - self.zh}, {"zh": 1 - self.zh}]
        self.twin = {"core": 1 - self.core}
        self.mirror = {"x": self.y, "y": self.x}
        y, zl, zh = self.y, self.zl, self.zh
        beside, opposite = y + 1 - y % 2 * 2, 3 - y
        self.cube = {
            "ya": ({"y": beside}, (beside, zl, zh)),
            "yb": ({"y": opposite}, (opposite, zl, zh)),
            "za": ({"zl": 1 - zl}, (y, 1 - zl, zh)),
            "zb": ({"zl": 1 - zl, "zh": 1 - zh}, (y, 1 - zl, 1 - zh)),
        }

    def across_link(self, name):
        return self.cube[name]

    def enter(self):
        barrier = pltpu.get_barrier_semaphore()
        peers = [self.right, self.left, self.far, *self.ys, *self.zs, self.twin]
        for peer in peers:
            pl.semaphore_signal(barrier, inc=1, device_id=peer, device_id_type=MESH)

        @pl.when(self.x != self.y)
        def _():
            pl.semaphore_signal(barrier, inc=1, device_id=self.mirror, device_id_type=MESH)
            pl.semaphore_wait(barrier, len(peers) + 1)

        @pl.when(self.x == self.y)
        def _():
            pl.semaphore_wait(barrier, len(peers))


class Links:
    def __init__(self, send, recv, local):
        self.send, self.recv, self.local, self.count, self.local_count = send, recv, local, 0, 0
        self.open = []

    def make(self, src, dst, device):
        i = self.count
        self.count += 1
        return pltpu.make_async_remote_copy(
            src, dst, self.send.at[i], self.recv.at[i], device_id=device, device_id_type=MESH
        )

    def start(self, src, dst, device):
        copy = self.make(src, dst, device)
        copy.start()
        self.open.append(copy)
        return copy

    def spread(self, ref, devices):
        return [self.start(ref, ref, device) for device in devices]

    def keep(self, src, dst):
        copy = pltpu.make_async_copy(src, dst, self.local.at[self.local_count])
        self.local_count += 1
        copy.start()
        return copy

    def settle(self, copies):
        for copy in copies:
            copy.wait_send()
        self.open = [copy for copy in self.open if all(copy is not done for done in copies)]

    def close(self):
        self.settle(list(self.open))


def arrive(copies):
    for copy in copies:
        copy.wait_recv()


class RingGather:
    def __init__(self, links, here, src, buf):
        cols = lanes(here.x, 384)
        self.links, self.here, self.buf = links, here, buf
        self.first = [
            links.start(src(H0), buf.at[H0, cols], here.right),
            links.start(src(H1), buf.at[H1, cols], here.left),
        ]
        self.second = [
            links.start(src(H1), buf.at[H1, cols], here.right),
            links.start(src(H0), buf.at[H0, cols], here.left),
        ]

    def forward(self):
        here, buf = self.here, self.buf
        self.first[0].wait_recv()
        a = buf.at[H0, lanes(here.behind, 384)]
        self.third = [self.links.start(a, a, here.right)]
        self.first[1].wait_recv()
        b = buf.at[H1, lanes(here.ahead, 384)]
        self.third += [self.links.start(b, b, here.left)]

    def finish(self):
        arrive(self.second)
        arrive(self.third)

    def settle(self):
        self.links.settle(self.first + self.second + self.third)


class RingScatter:
    def __init__(self, links, here, part, slots):
        self.links, self.here, self.part, self.slots = links, here, part, slots

    def send_far(self):
        h, p, s = self.here, self.part, self.slots
        self.r0 = self.links.start(p.at[h.across, H0], s.at[0], h.right)
        self.l0 = self.links.start(p.at[h.across, H1], s.at[1], h.left)

    def send_near(self):
        h, p, s = self.here, self.part, self.slots
        self.r1 = self.links.start(p.at[h.ahead, H1], s.at[2], h.right)
        self.l1 = self.links.start(p.at[h.behind, H0], s.at[3], h.left)

    def forward(self):
        h, p, s = self.here, self.part, self.slots
        self.r0.wait_recv()
        p[h.ahead, H0] = (p[h.ahead, H0].astype(f32) + s[0].astype(f32)).astype(bf16)
        self.r2 = self.links.start(p.at[h.ahead, H0], s.at[4], h.right)
        self.l0.wait_recv()
        p[h.behind, H1] = (p[h.behind, H1].astype(f32) + s[1].astype(f32)).astype(bf16)
        self.l2 = self.links.start(p.at[h.behind, H1], s.at[5], h.left)

    def finish(self):
        arrive([self.r1, self.l1, self.r2, self.l2])

    def settle(self):
        self.links.settle([self.r0, self.l0, self.r1, self.l1, self.r2, self.l2])

    def received(self, half):
        s = self.slots
        pair = (4, 3) if half == 0 else (2, 5)
        return s[pair[0]].astype(f32) + s[pair[1]].astype(f32)


ORDERS = (("ya", "yb", "za", "zb"), ("za", "zb", "ya", "yb"), ("yb", "ya", "zb", "za"), ("zb", "za", "yb", "ya"))


def part_of(order):
    y_state = {(): "own", ("ya",): "pair", ("yb",): "cross"}.get(tuple(d for d in order if d[0] == "y"), "all")
    z_state = {(): "own", ("za",): "low", ("zb",): "cross"}.get(tuple(d for d in order if d[0] == "z"), "all")
    return y_state, z_state


def y_cells(state, y):
    return {"own": [(y, 1)], "pair": [(y // 2 * 2, 2)], "cross": [(y, 1), (3 - y, 1)], "all": [(0, 4)]}[state]


def z_cells(state, zl, zh, joined):
    if state == "all" and not joined:
        return [(None, 0), (None, 1)]
    cells = {"own": [(zl, zh)], "low": [(None, zh)], "cross": [(zl, zh), (1 - zl, 1 - zh)], "all": [(None, None)]}
    return cells[state]


def either(index):
    return slice(None) if index is None else index


class UnitColumns:
    def __init__(self, core, start, size):
        self.core, self.start, self.size = core, start, size

    def cells(self, state, y, zl, zh):
        rows = pl.ds(self.start, self.size)
        return [
            (slice(None), either(l), self.core, rows, pl.ds(pl.multiple_of(h * 512 + first * 128, 128), count * 128))
            for l, h in z_cells(state[1], zl, zh, False)
            for first, count in y_cells(state[0], y)
        ]

    def shapes(self, state):
        return [
            (4,) + ((2,) if l is None else ()) + (self.size, count * 128)
            for l, _ in z_cells(state[1], 0, 0, False)
            for _, count in y_cells(state[0], 0)
        ]


class Blocks:
    def __init__(self, core, start, size, width):
        self.core, self.start, self.size, self.width = core, start, size, width

    def cells(self, state, y, zl, zh):
        rows = pl.ds(self.start, self.size)
        pick = lambda first, count: first if count == 1 else (slice(None) if count == 4 else pl.ds(first, count))
        return [
            (either(h), pick(first, count), either(l), self.core, rows)
            for l, h in z_cells(state[1], zl, zh, True)
            for first, count in y_cells(state[0], y)
        ]

    def shapes(self, state):
        return [
            ((2,) if h is None else ()) + ((count,) if count > 1 else ()) + ((2,) if l is None else ()) + (self.size, self.width)
            for l, h in z_cells(state[1], 0, 0, True)
            for _, count in y_cells(state[0], 0)
        ]


class OutputRows:
    def __init__(self, core, start, size, place):
        self.core, self.start, self.size, self.place = core, start, size, place

    def cells(self, state, y, zl, zh):
        rows = pl.ds(self.start, self.size)
        return [
            (either(h), self.place, either(l), self.core, rows, pl.ds(pl.multiple_of(first * 384, 128), count * 384))
            for l, h in z_cells(state[1], zl, zh, True)
            for first, count in y_cells(state[0], y)
        ]

    def shapes(self, state):
        return [
            ((2,) if h is None else ()) + ((2,) if l is None else ()) + (self.size, count * 384)
            for l, h in z_cells(state[1], 0, 0, True)
            for _, count in y_cells(state[0], 0)
        ]


class CubeGather:
    def __init__(self, links, here, ref, layout, order):
        self.links, self.here, self.ref, self.layout, self.order, self.step = links, here, ref, layout, order, 0
        self.launch()

    def launch(self):
        here, ref = self.here, self.ref
        device, _ = here.across_link(self.order[self.step])
        cells = self.layout.cells(part_of(self.order[: self.step]), here.y, here.zl, here.zh)
        self.copies = [self.links.start(ref.at[cell], ref.at[cell], device) for cell in cells]

    def advance(self):
        arrive(self.copies)
        self.step += 1
        if self.step < 4:
            self.launch()


class CubeReduce:
    def __init__(self, links, here, ref, layout, order, slots):
        self.links, self.here, self.ref, self.layout, self.order, self.step = links, here, ref, layout, order, 3
        self.slots = slots
        self.launch()

    def launch(self):
        here, ref = self.here, self.ref
        device, coordinates = here.across_link(self.order[self.step])
        cells = self.layout.cells(part_of(self.order[: self.step]), *coordinates)
        pairs = zip(cells, self.slots[self.step])
        self.copies = [self.links.start(ref.at[cell], slot, device) for cell, slot in pairs]

    def advance(self):
        here, ref = self.here, self.ref
        arrive(self.copies)
        cells = self.layout.cells(part_of(self.order[: self.step]), here.y, here.zl, here.zh)
        for cell, slot in zip(cells, self.slots[self.step]):
            ref[cell] = (ref[cell].astype(f32) + slot[...].astype(f32)).astype(bf16)
        self.step -= 1
        if self.step >= 0:
            self.launch()


def advance(cubes):
    for cube in cubes:
        cube.advance()


def grad_layouts(core, place):
    return [
        ("d", Blocks(core, 0, 16, D), 0),
        ("d", Blocks(core, 16, 16, D), 3),
        ("g", UnitColumns(core, 0, 48), 0),
        ("g", UnitColumns(core, 48, 48), 1),
        ("u", UnitColumns(core, 0, 48), 2),
        ("u", UnitColumns(core, 48, 48), 3),
        ("o", OutputRows(core, 0, 16, place), 1),
        ("o", OutputRows(core, 16, 16, place), 2),
        ("o", OutputRows(core, 32, 16, place), 3),
        ("q", Blocks(core, 0, 32, 384), 0),
        ("q", Blocks(core, 32, 32, 384), 1),
        ("q", Blocks(core, 64, 16, 384), 2),
        ("q", Blocks(core, 80, 16, 384), 3),
    ]


def slot_shapes():
    return [
        [layout.shapes(part_of(ORDERS[order][:step])) for step in range(4)] for _, layout, order in grad_layouts(0, 0)
    ]


def sine_cosine(angle):
    turns = jnp.floor(angle * (1.0 / (2.0 * math.pi)) + 0.5)
    r = angle - turns * 6.28125
    r = r - turns * 0.0019350051879882812
    r = r - turns * 3.0199159819185874e-07
    t = r * 0.5
    t2 = t * t
    s = 1.0 / 6227020800.0
    for c in (-1.0 / 39916800, 1.0 / 362880, -1.0 / 5040, 1.0 / 120, -1.0 / 6, 1.0):
        s = s * t2 + c
    s = s * t
    c_ = 1.0 / 479001600.0
    for c in (-1.0 / 3628800, 1.0 / 40320, -1.0 / 720, 1.0 / 24, -0.5, 1.0):
        c_ = c_ * t2 + c
    return 2.0 * s * c_, 1.0 - 2.0 * s * s


def turn(head, cosine, sine):
    return head * cosine + pltpu.roll(head, 64, 1) * sine


def dot_first(a, b):
    return lax.dot_general(a, b, (((0,), (0,)), ((), ())), preferred_element_type=f32)


def column_to_rows(column, ref):
    for c in range(4):
        block = jnp.broadcast_to(column[c * 128 : c * 128 + 128], (128, 128)).T
        ref[c : c + 1] = block[0:1]


def rows_to_column(rows):
    return jnp.concatenate([jnp.broadcast_to(rows[c : c + 1], (128, 128)).T for c in range(4)], 0)


def layer_kernel(
    tokens, pos, gain_a, gain_f, qkvw, ow, gw, uw, dw, cot, freq, perm, permo,
    mixed, tgrad, dgain, fin_q, fin_o, fin_g, fin_u, fin_d,
    xf, a1, a2, cotf, stats, qkv, kvr, att, cosb, sinb, middle, gn, posb, packed,
    wqkv, wo, wg, wu, wd, hdd, part, partd, slots, wide, dzf, dmid,
    dq, dkv, dkr, dkin, dproj, small, sums, gsum, rc_g, rc_u, rc_d, rc_q, rc_o,
    send, recv, local, *slot_refs,
):
    here = Place()
    links = Links(send, recv, local)
    x, y, zl, zh, core, quarter = here.x, here.y, here.zl, here.zh, here.core, here.quarter
    hid = zh * 4 + y
    other = 1 - core
    own, y_cols = lanes(x, 384), lanes(y, 384)
    a, b, da, db, oa, ob = pl.ds(0, 48), pl.ds(48, 48), pl.ds(0, 16), pl.ds(16, 16), pl.ds(0, 32), pl.ds(32, 16)
    refs = iter(slot_refs)
    layouts = [
        (name, layout, ORDERS[order], [[next(refs) for _ in shapes] for shapes in steps])
        for (name, layout, order), steps in zip(grad_layouts(core, x), slot_shapes())
    ]
    x_peers = (here.right, here.left, here.far)
    here.enter()

    own_qkv, src_qkv = wqkv.at[zh, x, zl, core], qkvw.at[pl.ds(quarter * 96, 96)]
    own_o, src_o = wo.at[zh, y, zl, core, :, own], ow.at[pl.ds(quarter * 48, 48)]
    mirror = [links.make(src_qkv, own_qkv, here.mirror)]
    stay = [pltpu.make_async_copy(src_qkv, own_qkv, local.at[0])]
    links.local_count = 2

    @pl.when(x != y)
    def _():
        for copy in mirror:
            copy.start()

    @pl.when(x == y)
    def _():
        for copy in stay:
            copy.start()

    def hidden_slices(target):
        rows = pl.ds(quarter * 96, 96)
        return [
            (gw.at[rows, lanes(target, 128)], wg.at[x, zl, core, :, lanes(hid, 128)]),
            (uw.at[rows, lanes(target, 128)], wu.at[x, zl, core, :, lanes(hid, 128)]),
            (dw.at[pl.ds(target * 128 + quarter * 32, 32)], wd.at[zh, y, zl, core, :, own]),
        ]

    swaps = []
    for peer, target in ((here.right, here.ahead), (here.left, here.behind), (here.far, here.across)):
        swaps += [links.start(src, dst, peer) for src, dst in hidden_slices(target)]
    swap_kept = [links.keep(src, dst) for src, dst in hidden_slices(x)]
    swaps_o = [links.start(src_o, own_o, peer) for peer in x_peers]
    swap_kept_o = links.keep(src_o, own_o)

    ring_x = RingGather(links, here, lambda half: tokens.at[half], xf)
    kept = [links.keep(tokens, xf.at[:, own])]
    small_sends = []
    for peer in x_peers:
        small_sends.append(links.start(pos, posb.at[x], peer))
        small_sends.append(links.start(gain_a, gn.at[0, :, own], peer))
        small_sends.append(links.start(gain_f, gn.at[1, :, own], peer))
    kept += [links.keep(pos, posb.at[x]), links.keep(gain_a, gn.at[0, :, own]), links.keep(gain_f, gn.at[1, :, own])]

    @pl.when(x != y)
    def _():
        for copy in mirror:
            copy.wait()

    @pl.when(x == y)
    def _():
        for copy in stay:
            copy.wait()

    pieces = ((0, 32), (32, 32), (64, 16), (80, 16))
    cube_q = [
        CubeGather(links, here, wqkv, Blocks(core, start, size, 384), ORDERS[k]) for k, (start, size) in enumerate(pieces)
    ]
    for copy in swap_kept:
        copy.wait()
    arrive(swaps)
    advance(cube_q)
    cube_g = [CubeGather(links, here, wg, UnitColumns(core, 48 * k, 48), ORDERS[k]) for k in range(2)]
    cube_u = [CubeGather(links, here, wu, UnitColumns(core, 48 * k, 48), ORDERS[2 + k]) for k in range(2)]
    cube_d = [CubeGather(links, here, wd, Blocks(core, 16 * k, 16, D), ORDERS[3 * k]) for k in range(2)]
    ring_x.forward()
    advance(cube_q)
    swap_kept_o.wait()
    arrive(swaps_o)
    cube_o = [CubeGather(links, here, wo, Blocks(core, 16 * k, 16, D), ORDERS[1 + k]) for k in range(3)]
    advance(cube_q)
    advance(cube_o)

    for copy in kept:
        copy.wait()
    arrive(small_sends)
    mine = posb[y]
    mine = jnp.where(zh == 0, mine[0:4], mine[4:8]).astype(f32)
    lane = lax.broadcasted_iota(i32, (128, 128), 1)
    for c in range(4):
        column = jnp.broadcast_to(mine[c : c + 1], (128, 128)).T
        sine, cosine = sine_cosine(column * freq[0:1])
        cosb[pl.ds(c * 128, 128)] = cosine
        sinb[pl.ds(c * 128, 128)] = jnp.where(lane < 64, -sine, sine)

    ring_x.finish()
    ring_c = RingGather(links, here, lambda half: cot.at[half], cotf)
    cot_kept = links.keep(cot, cotf.at[:, own])

    def norm_tokens(i, _):
        rows = pl.ds(pl.multiple_of(i * 64, 64), 64)
        value = xf[rows].astype(f32)
        inverse = lax.rsqrt(jnp.sum(value * value, axis=1, keepdims=True) * (1.0 / D) + epsilon)
        a1[rows] = (value * gn[0]).astype(bf16)
        stats[rows] = jnp.broadcast_to(inverse, (64, 128))
        return 0

    lax.fori_loop(0, 8, norm_tokens, 0)

    advance(cube_q)
    core_qkv = links.spread(wqkv.at[:, :, :, core], [here.twin])
    advance(cube_g)
    advance(cube_u)
    advance(cube_o)
    advance(cube_d)

    arrive(core_qkv)
    advance(cube_g)
    advance(cube_u)

    def widen(i, _):
        w = wqkv[i].reshape(D, 384)
        for j in range(3):
            hdd[j, :, lanes(i, 512)] = dot(w[j * 512 : j * 512 + 512], perm[...]).astype(bf16)
        return 0

    lax.fori_loop(0, 2, widen, 0)

    def keys_values(g, _):
        pair = dot(a1[...], hdd[:, :, lanes(g * 2 + 1, 256)].reshape(D, 256))
        inverse = stats[...]
        qkv[:, lanes(g * 4 + 2, 128)] = turn(pair[:, :128] * inverse, cosb[...], sinb[...]).astype(bf16)
        qkv[:, lanes(g * 4 + 3, 128)] = (pair[:, 128:] * inverse).astype(bf16)
        return 0

    lax.fori_loop(0, 2, keys_values, 0)
    over = [links.make(qkv.at[:, pl.ds(g * 512 + 256, 256)], kvr.at[g], here.zs[2]) for g in range(2)]

    @pl.when(zh == 0)
    def _():
        for copy in over:
            copy.start()

    def queries(g, _):
        pair = dot(a1[...], hdd[:, :, lanes(g * 2, 256)].reshape(D, 256))
        inverse = stats[...]
        for h in range(2):
            head = pair[:, h * 128 : h * 128 + 128] * inverse
            qkv[:, lanes(g * 4 + h, 128)] = turn(head, cosb[...], sinb[...]).astype(bf16)
        return 0

    lax.fori_loop(0, 2, queries, 0)
    ring_c.forward()
    advance(cube_o)
    advance(cube_d)
    advance(cube_g)

    def own_scores(i, _):
        g = i // 2
        for qb in range(2):
            rows, keys = pl.ds(qb * 256, 256), pl.ds(0, qb * 256 + 256)
            q = qkv[rows, lanes(g * 4 + i % 2, 128)]
            s = dot_t(q, qkv[keys, lanes(g * 4 + 2, 128)]) * score_scale
            index = lax.broadcasted_iota(i32, s.shape, 0) + qb * 256
            s = jnp.where(lax.broadcasted_iota(i32, s.shape, 1) <= index, s, masked_score)
            m = jnp.max(s, axis=1, keepdims=True)
            e = jnp.exp2(s - m)
            dq[i, rows] = dot(e.astype(bf16), qkv[keys, lanes(g * 4 + 3, 128)])
            dkv[i, rows] = jnp.broadcast_to(m, (256, 128))
            dkr[i, rows] = jnp.broadcast_to(jnp.sum(e, axis=1, keepdims=True), (256, 128))
        return 0

    lax.fori_loop(0, 4, own_scores, 0)
    advance(cube_u)
    advance(cube_o)
    core_o = links.spread(wo.at[:, :, :, core], [here.twin])
    advance(cube_d)

    @pl.when(zh == 1)
    def _():
        for copy in over:
            copy.wait_recv()

        def first_scores(i, _):
            g = i // 2
            for qb in range(2):
                rows = pl.ds(qb * 256, 256)
                q = qkv[rows, lanes(g * 4 + i % 2, 128)]
                s = dot_t(q, kvr[g, :, 0:128]) * score_scale
                old = dkv[i, rows][:, 0:1]
                m = jnp.maximum(old, jnp.max(s, axis=1, keepdims=True))
                e = jnp.exp2(s - m)
                shrink = jnp.exp2(old - m)
                dq[i, rows] = dq[i, rows] * shrink + dot(e.astype(bf16), kvr[g, :, 128:256])
                dkr[i, rows] = dkr[i, rows] * shrink + jnp.sum(e, axis=1, keepdims=True)
                dkv[i, rows] = jnp.broadcast_to(m, (256, 128))
            return 0

        lax.fori_loop(0, 4, first_scores, 0)

    @pl.when(zh == 0)
    def _():
        for copy in over:
            copy.wait_send()

    lane = lax.broadcasted_iota(i32, (512, 128), 1)
    for i in range(4):
        att[:, i * 128 : i * 128 + 128] = (dq[i] / dkr[i]).astype(bf16)
        stats[...] = jnp.where(lane == i, dkv[i] + jnp.log2(dkr[i]), stats[...])

    packed[...] = dot(att[...], permo[...]).astype(bf16)
    ring_a = RingGather(links, here, lambda half: packed.at[half], dzf)
    dzf[:, own] = packed[...]
    advance(cube_g)
    cores = [links.start(wg.at[:, :, core], wg.at[:, :, core], here.twin)]
    ring_a.forward()
    advance(cube_u)
    cores.append(links.start(wu.at[:, :, core], wu.at[:, :, core], here.twin))
    advance(cube_d)
    cores.append(links.start(wd.at[:, :, :, core], wd.at[:, :, :, core], here.twin))
    cot_kept.wait()
    ring_c.finish()
    arrive(core_o)
    ring_a.finish()
    sums[...] = jnp.zeros_like(sums)
    for rows in (H0, H1):
        for c in range(4):
            cols = pl.ds(c * 384, 384)
            value = xf[rows, cols].astype(f32)
            for k in range(4):
                value = value + dot(dzf[rows, k * 384 : k * 384 + 384], wo[:, k, :, :, :, cols].reshape(384, 384))
            a2[rows, cols] = value.astype(bf16)
            sums[rows] = sums[rows] + jnp.sum(value * value, axis=1, keepdims=True)

            @pl.when(x == c)
            def _(rows=rows, value=value):
                middle[rows] = value

    def norm_middle(i, _):
        rows = pl.ds(pl.multiple_of(i * 64, 64), 64)
        inverse = lax.rsqrt(sums[rows] * (1.0 / D) + epsilon)
        a2[rows] = (a2[rows].astype(f32) * inverse * gn[1]).astype(bf16)
        wide[rows] = jnp.broadcast_to(inverse, (64, 128))
        return 0

    lax.fori_loop(0, 8, norm_middle, 0)
    links.close()
    arrive(cores)

    sums[...] = jnp.zeros_like(sums)

    def units(n, _):
        cols = lanes(n, 256)
        w_g = wg[:, :, :, :, cols].reshape(D, 256)
        w_u = wu[:, :, :, :, cols].reshape(D, 256)
        w_d = wd[n // 2, pl.ds((n % 2) * 2, 2)].reshape(256, D)
        for rows in (H0, H1):
            gate = dot(a2[rows], w_g)
            up = dot(a2[rows], w_u)
            dh = dot_t(cotf[rows], w_d)
            sg = 1.0 / (1.0 + jnp.exp(-gate))
            silu = gate * sg
            dg = (dh * up * (sg + silu * (1.0 - sg))).astype(bf16)
            du = (dh * silu).astype(bf16)
            hdd[0, rows, cols] = (silu * up).astype(bf16)
            hdd[1, rows, cols] = dg
            hdd[2, rows, cols] = du
            inner = jnp.sum(dg.astype(f32) * gate + du.astype(f32) * up, axis=1, keepdims=True)
            sums[rows] = sums[rows] + inner
        return 0

    lax.fori_loop(0, 4, units, 0)

    def back_block(block):
        return dot_t(hdd[1], wg[block].reshape(384, 1024)) + dot_t(hdd[2], wu[block].reshape(384, 1024))

    scatter = RingScatter(links, here, part, slots.at[0])
    part[here.across] = back_block(here.across).astype(bf16)
    scatter.send_far()
    part[here.ahead] = back_block(here.ahead).astype(bf16)
    part[here.behind] = back_block(here.behind).astype(bf16)
    scatter.send_near()
    column_to_rows(sums[...], small.at[0, x])
    inner_sums = [links.start(small.at[0, x], small.at[0, x], p) for p in x_peers]
    dmid[...] = back_block(x)
    scatter.forward()

    def down_block(block, _):
        cols = lanes(block, 384)
        partd[block] = dot(hdd[0], wd[:, :, :, :, :, cols].reshape(1024, 384)).astype(bf16)
        return 0

    lax.fori_loop(0, 4, down_block, 0)

    def down_grad(n, _):
        rows = hdd[0, :, lanes(n, 256)].T
        for c in range(3):
            cols = pl.ds(c * 512, 512)
            value = dot(rows, cotf[:, cols]).astype(bf16)
            wd[n // 2, pl.ds((n % 2) * 2, 2), :, :, :, cols] = value.reshape(2, 2, 2, 32, 512)
        return 0

    lax.fori_loop(0, 4, down_grad, 0)
    cores = [links.start(wd.at[:, :, :, other], rc_d, here.twin)]

    def up_grads(block, _):
        rows = a2[:, lanes(block, 384)].T
        for source, target in ((1, wg), (2, wu)):
            for c in range(2):
                cols = pl.ds(c * 512, 512)
                target[block, :, :, :, cols] = dot(rows, hdd[source, :, cols]).astype(bf16).reshape(2, 2, 96, 512)
        return 0

    lax.fori_loop(0, 4, up_grads, 0)
    cores.append(links.start(wg.at[:, :, other], rc_g, here.twin))
    cores.append(links.start(wu.at[:, :, other], rc_u, here.twin))

    buffers = {"d": wd, "g": wg, "u": wu, "o": wo, "q": wqkv}
    reduces = {}

    def start_reduce(name):
        reduces[name] = [
            CubeReduce(links, here, buffers[name], layout, order, slots_)
            for piece, layout, order, slots_ in layouts
            if piece == name
        ]

    def core_sum_down(i, _):
        for k in range(2):
            for j in range(2):
                value = wd[k, i, j, core].astype(f32) + rc_d[k, i, j].astype(f32)
                wd[k, i, j, core] = value.astype(bf16)
        return 0

    arrive(cores[0:1])
    lax.fori_loop(0, 4, core_sum_down, 0)
    start_reduce("d")

    arrive(inner_sums)
    inner = rows_to_column(jnp.sum(small[0], axis=0)[0:4])[:, 0:1]
    scatter.finish()
    gsum[...] = jnp.zeros_like(gsum)
    for half, rows in enumerate((H0, H1)):
        da2 = dmid[rows] + scatter.received(half)
        m, inverse = middle[rows], wide[rows][:, 0:1]
        gsum[1:2] = gsum[1:2] + jnp.sum(da2 * m * inverse, axis=0, keepdims=True)
        factor = inner[half * 256 : half * 256 + 256] * inverse * inverse * (1.0 / D)
        value = cotf[rows, own].astype(f32) + inverse * gn[1, :, own] * da2 - m * factor
        dmid[rows] = value
        dzf[rows, own] = value.astype(bf16)
    ring_z = RingGather(links, here, lambda half: dzf.at[half, own], dzf)
    ring_z.forward()

    for matrix, (name, source) in enumerate((("g", rc_g), ("u", rc_u))):
        arrive(cores[matrix + 1 : matrix + 2])

        def core_sum(i, _, target=buffers[name], source=source):
            for j in range(2):
                target[i, j, core] = (target[i, j, core].astype(f32) + source[i, j].astype(f32)).astype(bf16)
            return 0

        lax.fori_loop(0, 4, core_sum, 0)
        start_reduce(name)

    ring_z.finish()

    scatter_d = RingScatter(links, here, partd, slots.at[1])
    scatter_d.send_far()
    scatter_d.send_near()

    packed[...] = dot_t(dzf[...], wo[:, x].reshape(384, D)).astype(bf16)
    hdd[1, :, 0:512] = dot_t(packed[...], permo[...]).astype(bf16)
    packed[...] = dot(att[...], permo[...]).astype(bf16)
    for c in range(3):
        cols = pl.ds(c * 512, 512)
        value = dot_first(packed[...], dzf[:, cols]).astype(bf16)
        wo[:, x, :, :, :, cols] = value.reshape(2, 2, 2, 48, 512)
    cores = [links.start(wo.at[:, x, :, other], rc_o, here.twin)]

    dq[...] = jnp.zeros_like(dq)
    dkv[...] = jnp.zeros_like(dkv)

    def pair(i, rows, k, v, visible):
        g = i // 2
        head = lanes(i, 128)
        q, grad = qkv[rows, lanes(g * 4 + i % 2, 128)], hdd[1, rows, head]
        delta = jnp.sum(grad.astype(f32) * att[rows, head].astype(f32), axis=1, keepdims=True)
        lane = lax.broadcasted_iota(i32, (256, 128), 1)
        lse = jnp.sum(jnp.where(lane == i, stats[rows], 0.0), axis=1, keepdims=True)
        s = dot_t(q, k) * score_scale
        if visible is not None:
            s = jnp.where(visible(s.shape), s, masked_score)
        p = jnp.exp2(s - lse)
        ds = (p * (dot_t(grad, v) - delta) * (1.0 / math.sqrt(HD))).astype(bf16)
        dq[i, rows] = dq[i, rows] + dot(ds, k)
        return dot_first(ds, q), dot_first(p.astype(bf16), grad)

    give = [links.make(kvr.at[g], dkin.at[g], here.zs[2]) for g in range(2)]

    @pl.when(zh == 1)
    def _():
        dkr[...] = jnp.zeros_like(dkr)

        def first_half(i, _):
            g = i // 2
            for qb in range(2):
                dk, dv = pair(i, pl.ds(qb * 256, 256), kvr[g, :, 0:128], kvr[g, :, 128:256], None)
                dkr[2 * g] = dkr[2 * g] + dk
                dkr[2 * g + 1] = dkr[2 * g + 1] + dv
            return 0

        for g in range(2):
            lax.fori_loop(2 * g, 2 * g + 2, first_half, 0)
            kvr[g, :, 0:128] = dkr[2 * g].astype(bf16)
            kvr[g, :, 128:256] = dkr[2 * g + 1].astype(bf16)
            give[g].start()

    scatter_d.forward()

    def own_keys(i, _):
        g = i // 2
        for qb in range(2):
            keys = pl.ds(0, qb * 256 + 256)

            def visible(shape):
                rows = lax.broadcasted_iota(i32, shape, 0) + qb * 256
                return lax.broadcasted_iota(i32, shape, 1) <= rows

            k, v = qkv[keys, lanes(g * 4 + 2, 128)], qkv[keys, lanes(g * 4 + 3, 128)]
            dk, dv = pair(i, pl.ds(qb * 256, 256), k, v, visible)
            dkv[2 * g, keys] = dkv[2 * g, keys] + dk
            dkv[2 * g + 1, keys] = dkv[2 * g + 1, keys] + dv
        return 0

    lax.fori_loop(0, 4, own_keys, 0)

    @pl.when(zh == 0)
    def _():
        for g in range(2):
            give[g].wait_recv()
            dkv[2 * g] = dkv[2 * g] + dkin[g, :, 0:128].astype(f32)
            dkv[2 * g + 1] = dkv[2 * g + 1] + dkin[g, :, 128:256].astype(f32)

    @pl.when(zh == 1)
    def _():
        for g in range(2):
            give[g].wait_send()

    arrive(cores)
    for g in range(2):
        for j in range(2):
            wo[g, x, j, core] = (wo[g, x, j, core].astype(f32) + rc_o[g, j].astype(f32)).astype(bf16)
    start_reduce("o")

    sums[...] = jnp.zeros_like(sums)
    inverse = stats[:, 4:5]
    for i in range(8):
        cols = pl.ds(i * 128, 128)
        g, place = i // 4, i % 4
        value = dq[2 * g + place] if place < 2 else dkv[2 * g + place - 2]
        sums[...] = sums[...] + jnp.sum(value * qkv[:, cols].astype(f32), axis=1, keepdims=True)
        if place < 3:
            value = turn(value, cosb[...], -sinb[...])
        hdd[0, :, cols] = (value * inverse).astype(bf16)
    column_to_rows(sums[...], small.at[1, x])
    inner_sums = [links.start(small.at[1, x], small.at[1, x], p) for p in x_peers]
    for g in range(2):
        dproj[g] = dot_t(hdd[0, :, g * 512 : g * 512 + 512], perm[...]).astype(bf16)

    def back_input(block):
        return sum(dot_t(dproj[g], wqkv[g, block].reshape(384, 384)) for g in range(2))

    scatter.settle()
    scatter = RingScatter(links, here, part, slots.at[2])
    part[here.across] = back_input(here.across).astype(bf16)
    scatter.send_far()
    part[here.ahead] = back_input(here.ahead).astype(bf16)
    part[here.behind] = back_input(here.behind).astype(bf16)
    scatter.send_near()
    tgrad[...] = back_input(x)

    def qkv_grads(block, _):
        rows = a1[:, lanes(block, 384)].T
        for g in range(2):
            wqkv[g, block] = dot(rows, dproj[g]).astype(bf16).reshape(2, 2, 96, 384)
        return 0

    lax.fori_loop(0, 4, qkv_grads, 0)
    cores.append(links.start(wqkv.at[:, :, :, other], rc_q, here.twin))
    scatter.forward()

    scatter_d.finish()
    for half, rows in enumerate((H0, H1)):
        mixed[rows] = middle[rows] + partd[x, rows].astype(f32) + scatter_d.received(half)

    advance(reduces["d"])
    advance(reduces["g"])
    advance(reduces["u"])

    arrive(cores[1:])
    for g in range(2):

        def core_heads(i, _, g=g):
            for j in range(2):
                value = wqkv[g, i, j, core].astype(f32) + rc_q[g, i, j].astype(f32)
                wqkv[g, i, j, core] = value.astype(bf16)
            return 0

        lax.fori_loop(0, 4, core_heads, 0)
    start_reduce("q")
    advance(reduces["o"])
    advance(reduces["d"])
    advance(reduces["g"])
    advance(reduces["u"])

    arrive(inner_sums)
    inner = rows_to_column(jnp.sum(small[1], axis=0)[0:4])[:, 0:1]
    scatter.finish()
    for half, rows in enumerate((H0, H1)):
        da1 = tgrad[rows] + scatter.received(half)
        source, rinv = xf[rows, own].astype(f32), stats[rows][:, 4:5]
        gsum[0:1] = gsum[0:1] + jnp.sum(da1 * source, axis=0, keepdims=True)
        factor = inner[half * 256 : half * 256 + 256] * rinv * rinv * (1.0 / D)
        tgrad[rows] = dmid[rows] + gn[0, :, own] * da1 - source * factor
    dgain[0] = gsum[...]
    gain_y = [links.start(dgain.at[0], dgain.at[1 + j], here.ys[j]) for j in range(3)]

    advance(reduces["q"])
    for _ in range(2):
        advance(reduces["d"])
        advance(reduces["g"])
        advance(reduces["u"])
    advance(reduces["o"])

    def hidden_blocks(target):
        return [
            (wg.at[target, zl, core, :, lanes(hid, 128)], fin_g.at[zl, core, :, lanes(x, 128)]),
            (wu.at[target, zl, core, :, lanes(hid, 128)], fin_u.at[zl, core, :, lanes(x, 128)]),
            (wd.at[zh, y, zl, core, :, lanes(target, 384)], fin_d.at[x, zl, core]),
        ]

    swaps = []
    for peer, target in ((here.right, here.ahead), (here.left, here.behind), (here.far, here.across)):
        swaps += [links.start(src, dst, peer) for src, dst in hidden_blocks(target)]
    swap_kept = [links.keep(src, dst) for src, dst in hidden_blocks(x)]

    advance(reduces["q"])
    advance(reduces["o"])

    for copy in swap_kept:
        copy.wait()
    arrive(swaps)
    fins = ((fin_g, 0), (fin_u, 0), (fin_d, 1))
    pick = lambda ref, lead, index: ref.at[(slice(None),) * lead + index]
    across_zl = [links.start(v, v, here.zs[0]) for v in (pick(ref, lead, (zl, core)) for ref, lead in fins)]

    arrive(gain_y)
    gsum[...] = dgain[0] + dgain[1] + dgain[2] + dgain[3]
    dgain[4] = gsum[...]
    gain_z = [links.start(dgain.at[4], dgain.at[5 + j], here.zs[j]) for j in range(3)]

    for _ in range(2):
        advance(reduces["q"])
    advance(reduces["o"])
    src_q, src_o = wqkv.at[zh, y, zl, core], wo.at[zh, x, zl, core, :, y_cols]
    dst_q, dst_o = fin_q.at[zl, core], fin_o.at[zl, core]
    mirror = [links.make(src_q, dst_q, here.mirror), links.make(src_o, dst_o, here.mirror)]
    first = links.local_count
    stay = [pltpu.make_async_copy(src_q, dst_q, local.at[first]), pltpu.make_async_copy(src_o, dst_o, local.at[first + 1])]

    @pl.when(x != y)
    def _():
        for copy in mirror:
            copy.start()
        for copy in mirror:
            copy.wait()

    @pl.when(x == y)
    def _():
        for copy in stay:
            copy.start()
        for copy in stay:
            copy.wait()

    head_zl = [links.start(v, v, here.zs[0]) for v in (fin_q.at[zl, core], fin_o.at[zl, core])]
    arrive(across_zl)
    to_core = [links.start(v, v, here.twin) for v in (pick(ref, lead, (slice(None), core)) for ref, lead in fins)]
    arrive(gain_z)
    gsum[...] = dgain[4] + dgain[5] + dgain[6] + dgain[7]
    dgain[8] = gsum[...]
    gain_c = links.start(dgain.at[8], dgain.at[9], here.twin)
    arrive(head_zl)
    head_core = [links.start(v, v, here.twin) for v in (fin_q.at[:, core], fin_o.at[:, core])]
    arrive([gain_c])
    arrive(to_core)
    arrive(head_core)
    links.close()


def run_layer(tokens, pos, gain_a, gain_f, qkvw, ow, gw, uw, dw, cot):
    s = jax.ShapeDtypeStruct
    v = pltpu.VMEM
    outs = [
        s((512, 384), f32),
        s((512, 384), f32),
        s((10, 8, 384), f32),
        s((2, 2, 96, 384), bf16),
        s((2, 2, 48, 384), bf16),
        s((2, 2, 96, 512), bf16),
        s((2, 2, 96, 512), bf16),
        s((4, 2, 2, 32, 384), bf16),
    ]
    scratch = [
        v((512, D), bf16),
        v((512, D), bf16),
        v((512, D), bf16),
        v((512, D), bf16),
        v((512, 128), f32),
        v((512, 1024), bf16),
        v((2, 512, 256), bf16),
        v((512, 512), bf16),
        v((512, 128), f32),
        v((512, 128), f32),
        v((512, 384), f32),
        v((2, 1, D), f32),
        v((4, 8, 128), i32),
        v((512, 384), bf16),
        v((2, 4, 2, 2, 96, 384), bf16),
        v((2, 4, 2, 2, 48, D), bf16),
        v((4, 2, 2, 96, 1024), bf16),
        v((4, 2, 2, 96, 1024), bf16),
        v((2, 4, 2, 2, 32, D), bf16),
        v((3, 512, 1024), bf16),
        v((4, 512, 384), bf16),
        v((4, 512, 384), bf16),
        v((3, 6, 256, 384), bf16),
        v((512, 128), f32),
        v((512, D), bf16),
        v((512, 384), f32),
        v((4, 512, 128), f32),
        v((4, 512, 128), f32),
        v((4, 512, 128), f32),
        v((2, 512, 256), bf16),
        v((2, 512, 384), bf16),
        v((2, 4, 8, 128), f32),
        v((512, 1), f32),
        v((8, 384), f32),
        v((4, 2, 96, 1024), bf16),
        v((4, 2, 96, 1024), bf16),
        v((2, 4, 2, 32, D), bf16),
        v((2, 4, 2, 96, 384), bf16),
        v((2, 2, 48, D), bf16),
        pltpu.SemaphoreType.DMA((270,)),
        pltpu.SemaphoreType.DMA((270,)),
        pltpu.SemaphoreType.DMA((20,)),
    ]
    scratch += [v(shape, bf16) for piece in slot_shapes() for step in piece for shape in step]
    return pl.pallas_call(
        layer_kernel,
        out_shape=outs,
        in_specs=[ANY] * 10 + [VM] * 3,
        out_specs=[VM] * len(outs),
        scratch_shapes=scratch,
        compiler_params=pltpu.CompilerParams(
            collective_id=0, has_side_effects=True, vmem_limit_bytes=63 * 1024 * 1024
        ),
        name="layer",
    )(tokens, pos, gain_a, gain_f, qkvw, ow, gw, uw, dw, cot, *constants())


def constants():
    half = HD // 2
    freq = np.zeros((8, 128), np.float32)
    rates = rope_base ** (-(np.arange(half) * 2.0 / HD))
    freq[:, :half] = rates
    freq[:, 64 : 64 + half] = rates
    perm = np.zeros((384, 512), np.float32)
    permo = np.zeros((512, 384), np.float32)
    for h in range(4):
        for d in range(HD):
            wide = d if (h == 3 or d < half) else d - half + 64
            perm[h * HD + d, h * 128 + wide] = 1
            permo[h * 128 + d, h * HD + d] = 1
    return jnp.asarray(freq), jnp.asarray(perm, bf16), jnp.asarray(permo, bf16)


def per_device(
    tokens,
    positions,
    attn_gain,
    qkv_weight,
    output_weight,
    ffn_gain,
    gate_weight,
    up_weight,
    down_weight,
    cotangent,
):
    mixed, tgrad, dgain, g_q, g_o, g_g, g_u, g_d = run_layer(
        tokens, positions.reshape(8, 128), attn_gain[None], ffn_gain[None], qkv_weight, output_weight,
        gate_weight, up_weight, down_weight, cotangent,
    )
    dgain = dgain[8] + dgain[9]
    return (
        mixed,
        tgrad,
        dgain[0],
        g_q.reshape(384, 384).astype(f32),
        g_o.reshape(192, 384).astype(f32),
        dgain[1],
        g_g.reshape(384, 512).astype(f32),
        g_u.reshape(384, 512).astype(f32),
        g_d.reshape(512, 384).astype(f32),
    )


def solution(mesh):
    finer = Mesh(mesh.devices.reshape(2, 2, 4, 2, 4), AXES)
    row = ("y", "zh")
    in_specs = (
        P(DP_ROW, "x"),
        P(("zl", "core", "x")),
        P("x"),
        P("x", row),
        P(row, "x"),
        P("x"),
        P("x", row),
        P("x", row),
        P(row, "x"),
        P(DP_ROW, "x"),
    )
    out_specs = (
        P(DP_ROW, "x"),
        P(DP_ROW, "x"),
        P("x"),
        P("x", row),
        P(row, "x"),
        P("x"),
        P("x", row),
        P("x", row),
        P(row, "x"),
    )
    return jax.shard_map(per_device, mesh=finer, in_specs=in_specs, out_specs=out_specs, check_vma=False)
```

time: 594 us -> 217 us (0.37)
  the two profiles are of different devices: /device:TPU:1 before, /device:TPU:25 now
where the time goes in v3:
time: 217 us
  Pallas kernels  206 us (95%)
  other arithmetic  5.85 us (3%)
  local copies, waits for them, and re-layouts  4.73 us (2%)
    pallas_call x1, Pallas kernels, run_layer(): pl.pallas_call(layer_kernel, out_shape=outs, in_specs=[ANY] * 10 + [VM] *...  206 us

profile of v3, /device:TPU:25, one launch (start us, length us, event | category | flops | bytes accessed | tf_op | source)
XLA Modules:
  0.0 217.0 jit_solution(339348793287524201)
XLA Ops:
  0.6 0.0 copy-start.5
  0.7 1.3 broadcast_in_dim.6.gain_a
  1.9 0.0 copy-done.5
  1.9 0.6 broadcast_in_dim.7.gain_f
  2.5 205.7 %layer.1 = (f32[512,384]{1,0:T(8,128)}, f32[512,384]{1,0:T(8,128)}, f32[10,8,384]{2,1,0:T(8,128)}, bf16[2,2,96,384]{3,2,1,0:T(8,128)(2,1)}, bf16[2,2,48,384]{3,2...) custom-call(bf16[512,384]{1,0:T(8,128)(2,1)} %tokens.1, ...), custom_call_target="tpu_custom_call" | custom-call | tf_op jit(solution)/shard_map/layer/pallas_call | solution.py:1045
  208.2 0.0 copy-start.2
  208.2 2.5 %bitcast_convert_fusion.1 = (f32[384,512]{1,0:T(8,128)}, f32[384,512]{1,0:T(8,128)}) fusion(bf16[2,2,96,512]{3,2,1,0:T(8,128)(2,1)} %get-tuple-element.23, bf16[2,2,96,512]{3,2,1,0:T(8,128)(2,1)} %get-tuple-element.22), kind=kLoop, calls=%fused_computation.1 | loop fusion | flops 393216 | bytes 2359296 | tf_op jit(solution)/shard_map/convert_element_type | solution.py:1099
  210.7 0.7 slice_add_fusion
  211.5 0.6 slice_reduce_fusion
  212.1 0.0 copy-done.2
  212.1 0.0 copy-start.3
  212.1 0.0 copy-start.4
  212.1 1.0 bitcast_convert_fusion
  213.0 0.0 copy-start.1
  213.0 0.0 copy-done.3
  213.0 0.9 bitcast_convert_fusion.3
  213.9 0.0 copy-done.4
  213.9 0.7 bitcast_convert_fusion.4
  214.7 0.0 copy-done.1
  214.7 0.0 copy-start
  214.7 0.9 copy.24
  215.6 0.5 copy-done
  216.1 0.9 copy.25
Async XLA Ops:
  0.6 1.3 copy-start.5
  208.2 3.9 %copy-start.2 = (bf16[4,2,2,32,384]{4,3,2,1,0:T(8,128)(2,1)S(1)}, bf16[4,2,2,32,384]{4,3,2,1,0:T(8,128)(2,1)}, u32[]{:S(2)}) copy-start(bf16[4,2,2,32,384]{4,3,2,1,0:T(8,128)(2,1)} %get-tuple-element.24) | copy-start | bytes 1179652
  212.1 1.0 copy-start.3
  212.1 1.9 copy-start.4
  213.0 1.6 copy-start.1
  214.7 1.4 copy-start

commit v4 on v3

--- a/solution.py
+++ b/solution.py
@@ -142,8 +142,10 @@
         b = buf.at[H1, lanes(here.ahead, 384)]
         self.third += [self.links.start(b, b, here.left)]
 
+    def near(self):
+        arrive(self.second)
+
     def finish(self):
-        arrive(self.second)
         arrive(self.third)
 
     def settle(self):
@@ -230,14 +232,15 @@
 
 
 class Blocks:
-    def __init__(self, core, start, size, width):
+    def __init__(self, core, start, size, width, left=None):
         self.core, self.start, self.size, self.width = core, start, size, width
+        self.columns = () if left is None else (pl.ds(left, width),)
 
     def cells(self, state, y, zl, zh):
         rows = pl.ds(self.start, self.size)
         pick = lambda first, count: first if count == 1 else (slice(None) if count == 4 else pl.ds(first, count))
         return [
-            (either(h), pick(first, count), either(l), self.core, rows)
+            (either(h), pick(first, count), either(l), self.core, rows, *self.columns)
             for l, h in z_cells(state[1], zl, zh, True)
             for first, count in y_cells(state[0], y)
         ]
@@ -319,8 +322,10 @@
 
 def grad_layouts(core, place):
     return [
-        ("d", Blocks(core, 0, 16, D), 0),
-        ("d", Blocks(core, 16, 16, D), 3),
+        ("d", Blocks(core, 0, 16, 768, 0), 0),
+        ("d", Blocks(core, 0, 16, 768, 768), 1),
+        ("d", Blocks(core, 16, 16, 768, 0), 2),
+        ("d", Blocks(core, 16, 16, 768, 768), 3),
         ("g", UnitColumns(core, 0, 48), 0),
         ("g", UnitColumns(core, 48, 48), 1),
         ("u", UnitColumns(core, 0, 48), 2),
@@ -356,6 +361,13 @@
     for c in (-1.0 / 3628800, 1.0 / 40320, -1.0 / 720, 1.0 / 24, -0.5, 1.0):
         c_ = c_ * t2 + c
     return 2.0 * s * c_, 1.0 - 2.0 * s * s
+
+
+def causal(scores):
+    last = scores[:, -256:]
+    seen = lax.broadcasted_iota(i32, (256, 256), 1) <= lax.broadcasted_iota(i32, (256, 256), 0)
+    last = jnp.where(seen, last, masked_score)
+    return last if scores.shape[1] == 256 else jnp.concatenate([scores[:, :-256], last], axis=1)
 
 
 def turn(head, cosine, sine):
@@ -415,6 +427,20 @@
         for copy in stay:
             copy.start()
 
+    @pl.when(x != y)
+    def _():
+        for copy in mirror:
+            copy.wait()
+
+    @pl.when(x == y)
+    def _():
+        for copy in stay:
+            copy.wait()
+
+    pieces = ((0, 32), (32, 32), (64, 16), (80, 16))
+    cube_q = [
+        CubeGather(links, here, wqkv, Blocks(core, start, size, 384), ORDERS[k]) for k, (start, size) in enumerate(pieces)
+    ]
     def hidden_slices(target):
         rows = pl.ds(quarter * 96, 96)
         return [
@@ -439,32 +465,23 @@
         small_sends.append(links.start(gain_f, gn.at[1, :, own], peer))
     kept += [links.keep(pos, posb.at[x]), links.keep(gain_a, gn.at[0, :, own]), links.keep(gain_f, gn.at[1, :, own])]
 
-    @pl.when(x != y)
-    def _():
-        for copy in mirror:
-            copy.wait()
-
-    @pl.when(x == y)
-    def _():
-        for copy in stay:
-            copy.wait()
-
-    pieces = ((0, 32), (32, 32), (64, 16), (80, 16))
-    cube_q = [
-        CubeGather(links, here, wqkv, Blocks(core, start, size, 384), ORDERS[k]) for k, (start, size) in enumerate(pieces)
-    ]
+    advance(cube_q)
     for copy in swap_kept:
         copy.wait()
     arrive(swaps)
-    advance(cube_q)
     cube_g = [CubeGather(links, here, wg, UnitColumns(core, 48 * k, 48), ORDERS[k]) for k in range(2)]
     cube_u = [CubeGather(links, here, wu, UnitColumns(core, 48 * k, 48), ORDERS[2 + k]) for k in range(2)]
-    cube_d = [CubeGather(links, here, wd, Blocks(core, 16 * k, 16, D), ORDERS[3 * k]) for k in range(2)]
+    cube_d = [
+        CubeGather(links, here, wd, Blocks(core, 16 * (k // 2), 16, 768, 768 * (k % 2)), ORDERS[k]) for k in range(4)
+    ]
     ring_x.forward()
     advance(cube_q)
     swap_kept_o.wait()
     arrive(swaps_o)
     cube_o = [CubeGather(links, here, wo, Blocks(core, 16 * k, 16, D), ORDERS[1 + k]) for k in range(3)]
+    advance(cube_g)
+    advance(cube_u)
+    advance(cube_d)
     advance(cube_q)
     advance(cube_o)
 
@@ -480,6 +497,7 @@
         cosb[pl.ds(c * 128, 128)] = cosine
         sinb[pl.ds(c * 128, 128)] = jnp.where(lane < 64, -sine, sine)
 
+    ring_x.near()
     ring_x.finish()
     ring_c = RingGather(links, here, lambda half: cot.at[half], cotf)
     cot_kept = links.keep(cot, cotf.at[:, own])
@@ -498,12 +516,10 @@
     core_qkv = links.spread(wqkv.at[:, :, :, core], [here.twin])
     advance(cube_g)
     advance(cube_u)
+    advance(cube_d)
     advance(cube_o)
-    advance(cube_d)
 
     arrive(core_qkv)
-    advance(cube_g)
-    advance(cube_u)
 
     def widen(i, _):
         w = wqkv[i].reshape(D, 384)
@@ -528,28 +544,28 @@
         for copy in over:
             copy.start()
 
+    advance(cube_g)
+    advance(cube_u)
+    advance(cube_d)
+    advance(cube_o)
+
     def queries(g, _):
         pair = dot(a1[...], hdd[:, :, lanes(g * 2, 256)].reshape(D, 256))
         inverse = stats[...]
         for h in range(2):
             head = pair[:, h * 128 : h * 128 + 128] * inverse
-            qkv[:, lanes(g * 4 + h, 128)] = turn(head, cosb[...], sinb[...]).astype(bf16)
+            qkv[:, lanes(g * 4 + h, 128)] = (turn(head, cosb[...], sinb[...]) * score_scale).astype(bf16)
         return 0
 
     lax.fori_loop(0, 2, queries, 0)
     ring_c.forward()
-    advance(cube_o)
-    advance(cube_d)
-    advance(cube_g)
 
     def own_scores(i, _):
         g = i // 2
         for qb in range(2):
             rows, keys = pl.ds(qb * 256, 256), pl.ds(0, qb * 256 + 256)
             q = qkv[rows, lanes(g * 4 + i % 2, 128)]
-            s = dot_t(q, qkv[keys, lanes(g * 4 + 2, 128)]) * score_scale
-            index = lax.broadcasted_iota(i32, s.shape, 0) + qb * 256
-            s = jnp.where(lax.broadcasted_iota(i32, s.shape, 1) <= index, s, masked_score)
+            s = causal(dot_t(q, qkv[keys, lanes(g * 4 + 2, 128)]))
             m = jnp.max(s, axis=1, keepdims=True)
             e = jnp.exp2(s - m)
             dq[i, rows] = dot(e.astype(bf16), qkv[keys, lanes(g * 4 + 3, 128)])
@@ -558,10 +574,6 @@
         return 0
 
     lax.fori_loop(0, 4, own_scores, 0)
-    advance(cube_u)
-    advance(cube_o)
-    core_o = links.spread(wo.at[:, :, :, core], [here.twin])
-    advance(cube_d)
 
     @pl.when(zh == 1)
     def _():
@@ -573,7 +585,7 @@
             for qb in range(2):
                 rows = pl.ds(qb * 256, 256)
                 q = qkv[rows, lanes(g * 4 + i % 2, 128)]
-                s = dot_t(q, kvr[g, :, 0:128]) * score_scale
+                s = dot_t(q, kvr[g, :, 0:128])
                 old = dkv[i, rows][:, 0:1]
                 m = jnp.maximum(old, jnp.max(s, axis=1, keepdims=True))
                 e = jnp.exp2(s - m)
@@ -590,6 +602,8 @@
         for copy in over:
             copy.wait_send()
 
+    advance(cube_o)
+    core_o = links.spread(wo.at[:, :, :, core], [here.twin])
     lane = lax.broadcasted_iota(i32, (512, 128), 1)
     for i in range(4):
         att[:, i * 128 : i * 128 + 128] = (dq[i] / dkr[i]).astype(bf16)
@@ -598,39 +612,52 @@
     packed[...] = dot(att[...], permo[...]).astype(bf16)
     ring_a = RingGather(links, here, lambda half: packed.at[half], dzf)
     dzf[:, own] = packed[...]
+    thirds = (dq, dkv, dkr)
+
+    def output_part(block, c):
+        return dot(dzf[:, lanes(block, 384)], wo[:, block, :, :, :, lanes(c, 384)].reshape(384, 384))
+
+    def output_first(c, _):
+        value = xf[:, lanes(c, 384)].astype(f32) + output_part(x, c)
+        for k, ref in enumerate(thirds):
+            ref[c] = value[:, k * 128 : k * 128 + 128]
+        return 0
+
+    def output_near(c, _):
+        value = output_part(here.ahead, c) + output_part(here.behind, c)
+        for k, ref in enumerate(thirds):
+            ref[c] = ref[c] + value[:, k * 128 : k * 128 + 128]
+        return 0
+
+    def output_last(c, _):
+        value = output_part(here.across, c)
+        for k, ref in enumerate(thirds):
+            m = ref[c] + value[:, k * 128 : k * 128 + 128]
+            ref[c] = m
+            a2[:, lanes(c * 3 + k, 128)] = (m * gn[1, :, lanes(c * 3 + k, 128)]).astype(bf16)
+            sums[...] = sums[...] + jnp.sum(m * m, axis=1, keepdims=True)
+        return 0
+
+    arrive(core_o)
+    lax.fori_loop(0, 4, output_first, 0)
+    ring_a.forward()
     advance(cube_g)
     cores = [links.start(wg.at[:, :, core], wg.at[:, :, core], here.twin)]
-    ring_a.forward()
     advance(cube_u)
     cores.append(links.start(wu.at[:, :, core], wu.at[:, :, core], here.twin))
     advance(cube_d)
     cores.append(links.start(wd.at[:, :, :, core], wd.at[:, :, :, core], here.twin))
+    ring_a.near()
+    lax.fori_loop(0, 4, output_near, 0)
     cot_kept.wait()
+    ring_c.near()
     ring_c.finish()
-    arrive(core_o)
+    sums[...] = jnp.zeros_like(sums)
     ring_a.finish()
-    sums[...] = jnp.zeros_like(sums)
-    for rows in (H0, H1):
-        for c in range(4):
-            cols = pl.ds(c * 384, 384)
-            value = xf[rows, cols].astype(f32)
-            for k in range(4):
-                value = value + dot(dzf[rows, k * 384 : k * 384 + 384], wo[:, k, :, :, :, cols].reshape(384, 384))
-            a2[rows, cols] = value.astype(bf16)
-            sums[rows] = sums[rows] + jnp.sum(value * value, axis=1, keepdims=True)
-
-            @pl.when(x == c)
-            def _(rows=rows, value=value):
-                middle[rows] = value
-
-    def norm_middle(i, _):
-        rows = pl.ds(pl.multiple_of(i * 64, 64), 64)
-        inverse = lax.rsqrt(sums[rows] * (1.0 / D) + epsilon)
-        a2[rows] = (a2[rows].astype(f32) * inverse * gn[1]).astype(bf16)
-        wide[rows] = jnp.broadcast_to(inverse, (64, 128))
-        return 0
-
-    lax.fori_loop(0, 8, norm_middle, 0)
+    lax.fori_loop(0, 4, output_last, 0)
+    wide[...] = jnp.broadcast_to(lax.rsqrt(sums[...] * (1.0 / D) + epsilon), (512, 128))
+    for k, ref in enumerate(thirds):
+        middle[:, k * 128 : k * 128 + 128] = ref[x]
     links.close()
     arrive(cores)
 
@@ -642,17 +669,18 @@
         w_u = wu[:, :, :, :, cols].reshape(D, 256)
         w_d = wd[n // 2, pl.ds((n % 2) * 2, 2)].reshape(256, D)
         for rows in (H0, H1):
-            gate = dot(a2[rows], w_g)
-            up = dot(a2[rows], w_u)
+            inverse = wide[rows][:, 0:1]
+            gate = dot(a2[rows], w_g) * inverse
+            up = dot(a2[rows], w_u) * inverse
             dh = dot_t(cotf[rows], w_d)
             sg = 1.0 / (1.0 + jnp.exp(-gate))
             silu = gate * sg
-            dg = (dh * up * (sg + silu * (1.0 - sg))).astype(bf16)
-            du = (dh * silu).astype(bf16)
+            dg = dh * up * (sg + silu * (1.0 - sg))
+            du = dh * silu
             hdd[0, rows, cols] = (silu * up).astype(bf16)
-            hdd[1, rows, cols] = dg
-            hdd[2, rows, cols] = du
-            inner = jnp.sum(dg.astype(f32) * gate + du.astype(f32) * up, axis=1, keepdims=True)
+            hdd[1, rows, cols] = (dg * inverse).astype(bf16)
+            hdd[2, rows, cols] = (du * inverse).astype(bf16)
+            inner = jnp.sum(dg * gate + du * up, axis=1, keepdims=True)
             sums[rows] = sums[rows] + inner
         return 0
 
@@ -730,9 +758,9 @@
     for half, rows in enumerate((H0, H1)):
         da2 = dmid[rows] + scatter.received(half)
         m, inverse = middle[rows], wide[rows][:, 0:1]
-        gsum[1:2] = gsum[1:2] + jnp.sum(da2 * m * inverse, axis=0, keepdims=True)
+        gsum[1:2] = gsum[1:2] + jnp.sum(da2 * m, axis=0, keepdims=True)
         factor = inner[half * 256 : half * 256 + 256] * inverse * inverse * (1.0 / D)
-        value = cotf[rows, own].astype(f32) + inverse * gn[1, :, own] * da2 - m * factor
+        value = cotf[rows, own].astype(f32) + gn[1, :, own] * da2 - m * factor
         dmid[rows] = value
         dzf[rows, own] = value.astype(bf16)
     ring_z = RingGather(links, here, lambda half: dzf.at[half, own], dzf)
@@ -749,6 +777,7 @@
         lax.fori_loop(0, 4, core_sum, 0)
         start_reduce(name)
 
+    ring_z.near()
     ring_z.finish()
 
     scatter_d = RingScatter(links, here, partd, slots.at[1])
@@ -767,18 +796,18 @@
     dq[...] = jnp.zeros_like(dq)
     dkv[...] = jnp.zeros_like(dkv)
 
-    def pair(i, rows, k, v, visible):
+    def pair(i, rows, k, v, masked):
         g = i // 2
         head = lanes(i, 128)
         q, grad = qkv[rows, lanes(g * 4 + i % 2, 128)], hdd[1, rows, head]
         delta = jnp.sum(grad.astype(f32) * att[rows, head].astype(f32), axis=1, keepdims=True)
         lane = lax.broadcasted_iota(i32, (256, 128), 1)
         lse = jnp.sum(jnp.where(lane == i, stats[rows], 0.0), axis=1, keepdims=True)
-        s = dot_t(q, k) * score_scale
-        if visible is not None:
-            s = jnp.where(visible(s.shape), s, masked_score)
+        s = dot_t(q, k)
+        if masked:
+            s = causal(s)
         p = jnp.exp2(s - lse)
-        ds = (p * (dot_t(grad, v) - delta) * (1.0 / math.sqrt(HD))).astype(bf16)
+        ds = (p * (dot_t(grad, v) - delta)).astype(bf16)
         dq[i, rows] = dq[i, rows] + dot(ds, k)
         return dot_first(ds, q), dot_first(p.astype(bf16), grad)
 
@@ -791,7 +820,7 @@
         def first_half(i, _):
             g = i // 2
             for qb in range(2):
-                dk, dv = pair(i, pl.ds(qb * 256, 256), kvr[g, :, 0:128], kvr[g, :, 128:256], None)
+                dk, dv = pair(i, pl.ds(qb * 256, 256), kvr[g, :, 0:128], kvr[g, :, 128:256], False)
                 dkr[2 * g] = dkr[2 * g] + dk
                 dkr[2 * g + 1] = dkr[2 * g + 1] + dv
             return 0
@@ -808,13 +837,8 @@
         g = i // 2
         for qb in range(2):
             keys = pl.ds(0, qb * 256 + 256)
-
-            def visible(shape):
-                rows = lax.broadcasted_iota(i32, shape, 0) + qb * 256
-                return lax.broadcasted_iota(i32, shape, 1) <= rows
-
             k, v = qkv[keys, lanes(g * 4 + 2, 128)], qkv[keys, lanes(g * 4 + 3, 128)]
-            dk, dv = pair(i, pl.ds(qb * 256, 256), k, v, visible)
+            dk, dv = pair(i, pl.ds(qb * 256, 256), k, v, True)
             dkv[2 * g, keys] = dkv[2 * g, keys] + dk
             dkv[2 * g + 1, keys] = dkv[2 * g + 1, keys] + dv
         return 0
@@ -833,6 +857,8 @@
         for g in range(2):
             give[g].wait_send()
 
+    for name in "dgu":
+        advance(reduces[name])
     arrive(cores)
     for g in range(2):
         for j in range(2):
@@ -845,7 +871,13 @@
         cols = pl.ds(i * 128, 128)
         g, place = i // 4, i % 4
         value = dq[2 * g + place] if place < 2 else dkv[2 * g + place - 2]
-        sums[...] = sums[...] + jnp.sum(value * qkv[:, cols].astype(f32), axis=1, keepdims=True)
+        if place == 2:
+            value = value * math.log(2.0)
+        inside = jnp.sum(value * qkv[:, cols].astype(f32), axis=1, keepdims=True)
+        if place < 2:
+            inside = inside * math.log(2.0)
+            value = value * (1.0 / math.sqrt(HD))
+        sums[...] = sums[...] + inside
         if place < 3:
             value = turn(value, cosb[...], -sinb[...])
         hdd[0, :, cols] = (value * inverse).astype(bf16)
@@ -876,13 +908,12 @@
     cores.append(links.start(wqkv.at[:, :, :, other], rc_q, here.twin))
     scatter.forward()
 
+    for name in "dgu":
+        advance(reduces[name])
+
     scatter_d.finish()
     for half, rows in enumerate((H0, H1)):
         mixed[rows] = middle[rows] + partd[x, rows].astype(f32) + scatter_d.received(half)
-
-    advance(reduces["d"])
-    advance(reduces["g"])
-    advance(reduces["u"])
 
     arrive(cores[1:])
     for g in range(2):
@@ -896,9 +927,8 @@
         lax.fori_loop(0, 4, core_heads, 0)
     start_reduce("q")
     advance(reduces["o"])
-    advance(reduces["d"])
-    advance(reduces["g"])
-    advance(reduces["u"])
+    for name in "dgu":
+        advance(reduces[name])
 
     arrive(inner_sums)
     inner = rows_to_column(jnp.sum(small[1], axis=0)[0:4])[:, 0:1]
@@ -912,12 +942,8 @@
     dgain[0] = gsum[...]
     gain_y = [links.start(dgain.at[0], dgain.at[1 + j], here.ys[j]) for j in range(3)]
 
-    advance(reduces["q"])
-    for _ in range(2):
-        advance(reduces["d"])
-        advance(reduces["g"])
-        advance(reduces["u"])
-    advance(reduces["o"])
+    for name in "dgu":
+        advance(reduces[name])
 
     def hidden_blocks(target):
         return [
@@ -931,8 +957,9 @@
         swaps += [links.start(src, dst, peer) for src, dst in hidden_blocks(target)]
     swap_kept = [links.keep(src, dst) for src, dst in hidden_blocks(x)]
 
-    advance(reduces["q"])
-    advance(reduces["o"])
+    for _ in range(2):
+        advance(reduces["q"])
+        advance(reduces["o"])
 
     for copy in swap_kept:
         copy.wait()
@@ -982,6 +1009,16 @@
     arrive(to_core)
     arrive(head_core)
     links.close()
+
+
+def outputs_kernel(mixed, tgrad, dgain, g_q, g_o, g_g, g_u, g_d, *outs):
+    gains = dgain[8] + dgain[9]
+    outs[0][...] = mixed[...]
+    outs[1][...] = tgrad[...]
+    outs[2][...] = gains[0:1]
+    outs[5][...] = gains[1:2]
+    for out, source in zip((outs[3], outs[4], outs[6], outs[7], outs[8]), (g_q, g_o, g_g, g_u, g_d)):
+        out[...] = source[...].reshape(out.shape).astype(f32)
 
 
 def run_layer(tokens, pos, gain_a, gain_f, qkvw, ow, gw, uw, dw, cot):
@@ -1037,8 +1074,8 @@
         v((2, 4, 2, 32, D), bf16),
         v((2, 4, 2, 96, 384), bf16),
         v((2, 2, 48, D), bf16),
-        pltpu.SemaphoreType.DMA((270,)),
-        pltpu.SemaphoreType.DMA((270,)),
+        pltpu.SemaphoreType.DMA((340,)),
+        pltpu.SemaphoreType.DMA((340,)),
         pltpu.SemaphoreType.DMA((20,)),
     ]
     scratch += [v(shape, bf16) for piece in slot_shapes() for step in piece for shape in step]
@@ -1083,22 +1120,21 @@
     down_weight,
     cotangent,
 ):
-    mixed, tgrad, dgain, g_q, g_o, g_g, g_u, g_d = run_layer(
+    parts = run_layer(
         tokens, positions.reshape(8, 128), attn_gain[None], ffn_gain[None], qkv_weight, output_weight,
         gate_weight, up_weight, down_weight, cotangent,
     )
-    dgain = dgain[8] + dgain[9]
-    return (
-        mixed,
-        tgrad,
-        dgain[0],
-        g_q.reshape(384, 384).astype(f32),
-        g_o.reshape(192, 384).astype(f32),
-        dgain[1],
-        g_g.reshape(384, 512).astype(f32),
-        g_u.reshape(384, 512).astype(f32),
-        g_d.reshape(512, 384).astype(f32),
-    )
+    s = jax.ShapeDtypeStruct
+    shapes = [(512, 384), (512, 384), (1, 384), (384, 384), (192, 384), (1, 384), (384, 512), (384, 512), (512, 384)]
+    outs = pl.pallas_call(
+        outputs_kernel,
+        out_shape=[s(shape, f32) for shape in shapes],
+        in_specs=[VM] * 8,
+        out_specs=[VM] * 9,
+        compiler_params=pltpu.CompilerParams(vmem_limit_bytes=32 * 1024 * 1024),
+        name="outputs",
+    )(*parts)
+    return tuple(out.reshape(384) if out.shape == (1, 384) else out for out in outs)
 
 
 def solution(mesh):

time: 217 us -> 219 us (level)
  local copies, waits for them, and re-layouts: 4.73 us -> 9.83 us
  other arithmetic: 5.85 us -> 1.19 us
    unnamed x14 -> x18, local copies, waits for them, and re-layouts: 2.31 us -> 8.02 us
    convert_element_type x4 -> x0, other arithmetic: 5.12 us -> none  [the longest x1 2.52 us: per_device(): g_u.reshape(384, 512).astype(f32)]
    pallas_call x1, Pallas kernels: 206 us -> 203 us  [run_layer(): pl.pallas_call(layer_kernel, out_shape=outs, in_specs=[ANY] * 10 + [VM] *...]
    pallas_call x0 -> x1, Pallas kernels: none -> 2.33 us  [per_device(): pl.pallas_call(outputs_kernel, out_shape=[s(shape, f32) for shape in shap...]
where the time goes in v4:
time: 219 us; the launch traced here: 217 us
  Pallas kernels  206 us (94%)
  local copies, waits for them, and re-layouts  9.83 us (4%)
    pallas_call x1, Pallas kernels, run_layer(): pl.pallas_call(layer_kernel, out_shape=outs, in_specs=[ANY] * 10 + [VM] *...  203 us
    unnamed x18, local copies, waits for them, and re-layouts  8.02 us

profile of v4, /device:TPU:25, one launch (start us, length us, event | category | flops | bytes accessed | tf_op | source)
XLA Modules:
  0.0 217.2 jit_solution(7154792038122782829)
XLA Ops:
  0.6 0.0 copy-start.8
  0.7 1.3 broadcast_in_dim.6.gain_a
  1.9 0.0 copy-done.8
  1.9 0.6 broadcast_in_dim.7.gain_f
  2.5 203.2 %layer.1 = (f32[512,384]{1,0:T(8,128)}, f32[512,384]{1,0:T(8,128)}, f32[10,8,384]{2,1,0:T(8,128)}, bf16[2,2,96,384]{3,2,1,0:T(8,128)(2,1)}, bf16[2,2,48,384]{3,2...) custom-call(bf16[512,384]{1,0:T(8,128)(2,1)} %tokens.1, ...), custom_call_target="tpu_custom_call" | custom-call | tf_op jit(solution)/shard_map/layer/pallas_call | solution.py:1082
  205.7 0.0 copy-start
  205.7 1.1 copy-done
  206.8 0.0 copy-start.1
  206.8 1.1 copy-done.1
  207.9 0.0 copy-start.2
  207.9 1.0 copy-done.2
  208.9 0.0 copy-start.3
  208.9 1.0 copy-done.3
  209.9 0.0 copy-start.4
  209.9 1.0 copy-done.4
  210.9 0.0 copy-start.5
  210.9 1.0 copy-done.5
  211.9 0.0 copy-start.6
  211.9 0.9 copy-done.6
  212.8 0.0 copy-start.7
  212.8 0.9 copy-done.7
  213.7 2.3 %outputs.1 = (f32[512,384]{1,0:T(8,128)}, f32[512,384]{1,0:T(8,128)}, f32[1,384]{1,0:T(1,128)S(1)}, f32[384,384]{1,0:T(8,128)}, f32[192,384]{1,0:T(8,128)}, /*in...) custom-call(f32[512,384]{1,0:T(8,128)S(1)} %copy-done, ...), custom_call_target="tpu_custom_call" | custom-call | tf_op jit(solution)/shard_map/outputs/pallas_call | solution.py:1129
  216.0 0.6 reduce
  216.6 0.6 reduce.1
Async XLA Ops:
  0.6 1.3 copy-start.8
  205.7 1.1 copy-start
  206.8 1.1 copy-start.1
  207.9 1.0 copy-start.2
  208.9 1.0 copy-start.3
  209.9 1.0 copy-start.4
  210.9 1.0 copy-start.5
  211.9 0.9 copy-start.6
  212.8 0.9 copy-start.7

commit v5 on v4

--- a/solution.py
+++ b/solution.py
@@ -232,15 +232,14 @@
 
 
 class Blocks:
-    def __init__(self, core, start, size, width, left=None):
+    def __init__(self, core, start, size, width):
         self.core, self.start, self.size, self.width = core, start, size, width
-        self.columns = () if left is None else (pl.ds(left, width),)
 
     def cells(self, state, y, zl, zh):
         rows = pl.ds(self.start, self.size)
         pick = lambda first, count: first if count == 1 else (slice(None) if count == 4 else pl.ds(first, count))
         return [
-            (either(h), pick(first, count), either(l), self.core, rows, *self.columns)
+            (either(h), pick(first, count), either(l), self.core, rows)
             for l, h in z_cells(state[1], zl, zh, True)
             for first, count in y_cells(state[0], y)
         ]
@@ -322,10 +321,8 @@
 
 def grad_layouts(core, place):
     return [
-        ("d", Blocks(core, 0, 16, 768, 0), 0),
-        ("d", Blocks(core, 0, 16, 768, 768), 1),
-        ("d", Blocks(core, 16, 16, 768, 0), 2),
-        ("d", Blocks(core, 16, 16, 768, 768), 3),
+        ("d", Blocks(core, 0, 16, D), 0),
+        ("d", Blocks(core, 16, 16, D), 3),
         ("g", UnitColumns(core, 0, 48), 0),
         ("g", UnitColumns(core, 48, 48), 1),
         ("u", UnitColumns(core, 0, 48), 2),
@@ -427,20 +424,6 @@
         for copy in stay:
             copy.start()
 
-    @pl.when(x != y)
-    def _():
-        for copy in mirror:
-            copy.wait()
-
-    @pl.when(x == y)
-    def _():
-        for copy in stay:
-            copy.wait()
-
-    pieces = ((0, 32), (32, 32), (64, 16), (80, 16))
-    cube_q = [
-        CubeGather(links, here, wqkv, Blocks(core, start, size, 384), ORDERS[k]) for k, (start, size) in enumerate(pieces)
-    ]
     def hidden_slices(target):
         rows = pl.ds(quarter * 96, 96)
         return [
@@ -465,15 +448,27 @@
         small_sends.append(links.start(gain_f, gn.at[1, :, own], peer))
     kept += [links.keep(pos, posb.at[x]), links.keep(gain_a, gn.at[0, :, own]), links.keep(gain_f, gn.at[1, :, own])]
 
+    @pl.when(x != y)
+    def _():
+        for copy in mirror:
+            copy.wait()
+
+    @pl.when(x == y)
+    def _():
+        for copy in stay:
+            copy.wait()
+
+    pieces = ((0, 32), (32, 32), (64, 16), (80, 16))
+    cube_q = [
+        CubeGather(links, here, wqkv, Blocks(core, start, size, 384), ORDERS[k]) for k, (start, size) in enumerate(pieces)
+    ]
     advance(cube_q)
     for copy in swap_kept:
         copy.wait()
     arrive(swaps)
     cube_g = [CubeGather(links, here, wg, UnitColumns(core, 48 * k, 48), ORDERS[k]) for k in range(2)]
     cube_u = [CubeGather(links, here, wu, UnitColumns(core, 48 * k, 48), ORDERS[2 + k]) for k in range(2)]
-    cube_d = [
-        CubeGather(links, here, wd, Blocks(core, 16 * (k // 2), 16, 768, 768 * (k % 2)), ORDERS[k]) for k in range(4)
-    ]
+    cube_d = [CubeGather(links, here, wd, Blocks(core, 16 * k, 16, D), ORDERS[3 * k]) for k in range(2)]
     ring_x.forward()
     advance(cube_q)
     swap_kept_o.wait()
@@ -1074,8 +1069,8 @@
         v((2, 4, 2, 32, D), bf16),
         v((2, 4, 2, 96, 384), bf16),
         v((2, 2, 48, D), bf16),
-        pltpu.SemaphoreType.DMA((340,)),
-        pltpu.SemaphoreType.DMA((340,)),
+        pltpu.SemaphoreType.DMA((270,)),
+        pltpu.SemaphoreType.DMA((270,)),
         pltpu.SemaphoreType.DMA((20,)),
     ]
     scratch += [v(shape, bf16) for piece in slot_shapes() for step in piece for shape in step]

time: 219 us -> 213 us (0.973)
  Pallas kernels: 206 us -> 198 us
    pallas_call x1, Pallas kernels: 203 us -> 196 us  [run_layer(): pl.pallas_call(layer_kernel, out_shape=outs, in_specs=[ANY] * 10 + [VM] *...]
where the time goes in v5:
time: 213 us; the launch traced here: 210 us
  Pallas kernels  198 us (93%)
  local copies, waits for them, and re-layouts  9.83 us (5%)
    pallas_call x1, Pallas kernels, run_layer(): pl.pallas_call(layer_kernel, out_shape=outs, in_specs=[ANY] * 10 + [VM] *...  196 us
    unnamed x18, local copies, waits for them, and re-layouts  8.02 us

profile of v5, /device:TPU:25, one launch (start us, length us, event | category | flops | bytes accessed | tf_op | source)
XLA Modules:
  0.0 209.6 jit_solution(4785081432796699220)
XLA Ops:
  0.6 0.0 copy-start.8
  0.7 1.3 broadcast_in_dim.6.gain_a
  1.9 0.0 copy-done.8
  1.9 0.6 broadcast_in_dim.7.gain_f
  2.5 195.6 %layer.1 = (f32[512,384]{1,0:T(8,128)}, f32[512,384]{1,0:T(8,128)}, f32[10,8,384]{2,1,0:T(8,128)}, bf16[2,2,96,384]{3,2,1,0:T(8,128)(2,1)}, bf16[2,2,48,384]{3,2...) custom-call(bf16[512,384]{1,0:T(8,128)(2,1)} %tokens.1, ...), custom_call_target="tpu_custom_call" | custom-call | tf_op jit(solution)/shard_map/layer/pallas_call | solution.py:1077
  198.0 0.0 copy-start
  198.1 1.1 copy-done
  199.2 0.0 copy-start.1
  199.2 1.1 copy-done.1
  200.3 0.0 copy-start.2
  200.3 1.0 copy-done.2
  201.3 0.0 copy-start.3
  201.3 1.0 copy-done.3
  202.3 0.0 copy-start.4
  202.3 1.0 copy-done.4
  203.3 0.0 copy-start.5
  203.3 1.0 copy-done.5
  204.3 0.0 copy-start.6
  204.3 0.9 copy-done.6
  205.2 0.0 copy-start.7
  205.2 0.9 copy-done.7
  206.1 2.3 %outputs.1 = (f32[512,384]{1,0:T(8,128)}, f32[512,384]{1,0:T(8,128)}, f32[1,384]{1,0:T(1,128)S(1)}, f32[384,384]{1,0:T(8,128)}, f32[192,384]{1,0:T(8,128)}, /*in...) custom-call(f32[512,384]{1,0:T(8,128)S(1)} %copy-done, ...), custom_call_target="tpu_custom_call" | custom-call | tf_op jit(solution)/shard_map/outputs/pallas_call | solution.py:1124
  208.4 0.6 reduce
  209.0 0.6 reduce.1
Async XLA Ops:
  0.6 1.3 copy-start.8
  198.0 1.1 copy-start
  199.2 1.1 copy-start.1
  200.3 1.0 copy-start.2
  201.3 1.0 copy-start.3
  202.3 1.0 copy-start.4
  203.3 1.0 copy-start.5
  204.3 0.9 copy-start.6
  205.2 0.9 copy-start.7

commit v6 on v5

--- a/solution.py
+++ b/solution.py
@@ -1010,8 +1010,8 @@
     gains = dgain[8] + dgain[9]
     outs[0][...] = mixed[...]
     outs[1][...] = tgrad[...]
-    outs[2][...] = gains[0:1]
-    outs[5][...] = gains[1:2]
+    outs[2][...] = gains[0]
+    outs[5][...] = gains[1]
     for out, source in zip((outs[3], outs[4], outs[6], outs[7], outs[8]), (g_q, g_o, g_g, g_u, g_d)):
         out[...] = source[...].reshape(out.shape).astype(f32)
 
@@ -1120,16 +1120,16 @@
         gate_weight, up_weight, down_weight, cotangent,
     )
     s = jax.ShapeDtypeStruct
-    shapes = [(512, 384), (512, 384), (1, 384), (384, 384), (192, 384), (1, 384), (384, 512), (384, 512), (512, 384)]
+    shapes = [(512, 384), (512, 384), (384,), (384, 384), (192, 384), (384,), (384, 512), (384, 512), (512, 384)]
     outs = pl.pallas_call(
         outputs_kernel,
         out_shape=[s(shape, f32) for shape in shapes],
         in_specs=[VM] * 8,
         out_specs=[VM] * 9,
-        compiler_params=pltpu.CompilerParams(vmem_limit_bytes=32 * 1024 * 1024),
+        compiler_params=pltpu.CompilerParams(vmem_limit_bytes=63 * 1024 * 1024),
         name="outputs",
     )(*parts)
-    return tuple(out.reshape(384) if out.shape == (1, 384) else out for out in outs)
+    return tuple(outs)
 
 
 def solution(mesh):

time: 213 us -> 206 us (0.967)
  local copies, waits for them, and re-layouts: 9.83 us -> 1.82 us
    unnamed x18 -> x2, local copies, waits for them, and re-layouts: 8.02 us -> 0.01 us
where the time goes in v6:
time: 206 us; the launch traced here: 202 us
  Pallas kernels  200 us (97%)
    pallas_call x1, Pallas kernels, run_layer(): pl.pallas_call(layer_kernel, out_shape=outs, in_specs=[ANY] * 10 + [VM] *...  196 us
    pallas_call x1, Pallas kernels, per_device(): pl.pallas_call(outputs_kernel, out_shape=[s(shape, f32) for shape in shap...  4.15 us

profile of v6, /device:TPU:25, one launch (start us, length us, event | category | flops | bytes accessed | tf_op | source)
XLA Modules:
  0.0 202.2 jit_solution(18319648611745420100)
XLA Ops:
  0.6 0.0 copy-start
  0.7 1.3 broadcast_in_dim.6.gain_a
  1.9 0.0 copy-done
  1.9 0.6 broadcast_in_dim.7.gain_f
  2.5 195.5 %layer.1 = (f32[512,384]{1,0:T(8,128)}, f32[512,384]{1,0:T(8,128)}, f32[10,8,384]{2,1,0:T(8,128)}, bf16[2,2,96,384]{3,2,1,0:T(8,128)(2,1)}, bf16[2,2,48,384]{3,2...) custom-call(bf16[512,384]{1,0:T(8,128)(2,1)} %tokens.1, ...), custom_call_target="tpu_custom_call" | custom-call | tf_op jit(solution)/shard_map/layer/pallas_call | solution.py:1077
  198.0 4.2 %outputs.1 = (f32[512,384]{1,0:T(8,128)}, f32[512,384]{1,0:T(8,128)}, f32[384]{0:T(512)}, f32[384,384]{1,0:T(8,128)}, f32[192,384]{1,0:T(8,128)}, /*index=5*/f32...) custom-call(f32[512,384]{1,0:T(8,128)} %get-tuple-element.17.mixed, ...), custom_call_target="tpu_custom_call" | custom-call | tf_op jit(solution)/shard_map/outputs/pallas_call | solution.py:1124
Async XLA Ops:
  0.6 1.3 copy-start

commit v7 on v6

--- a/solution.py
+++ b/solution.py
@@ -406,6 +406,8 @@
         for (name, layout, order), steps in zip(grad_layouts(core, x), slot_shapes())
     ]
     x_peers = (here.right, here.left, here.far)
+    gn[0, :, own] = gain_a[...].reshape(1, 384)
+    gn[1, :, own] = gain_f[...].reshape(1, 384)
     here.enter()
 
     own_qkv, src_qkv = wqkv.at[zh, x, zl, core], qkvw.at[pl.ds(quarter * 96, 96)]
@@ -444,9 +446,9 @@
     small_sends = []
     for peer in x_peers:
         small_sends.append(links.start(pos, posb.at[x], peer))
-        small_sends.append(links.start(gain_a, gn.at[0, :, own], peer))
-        small_sends.append(links.start(gain_f, gn.at[1, :, own], peer))
-    kept += [links.keep(pos, posb.at[x]), links.keep(gain_a, gn.at[0, :, own]), links.keep(gain_f, gn.at[1, :, own])]
+        small_sends.append(links.start(gn.at[0, :, own], gn.at[0, :, own], peer))
+        small_sends.append(links.start(gn.at[1, :, own], gn.at[1, :, own], peer))
+    kept += [links.keep(pos, posb.at[x])]
 
     @pl.when(x != y)
     def _():
@@ -1077,7 +1079,7 @@
     return pl.pallas_call(
         layer_kernel,
         out_shape=outs,
-        in_specs=[ANY] * 10 + [VM] * 3,
+        in_specs=[ANY] * 2 + [VM] * 2 + [ANY] * 6 + [VM] * 3,
         out_specs=[VM] * len(outs),
         scratch_shapes=scratch,
         compiler_params=pltpu.CompilerParams(
@@ -1116,7 +1118,7 @@
     cotangent,
 ):
     parts = run_layer(
-        tokens, positions.reshape(8, 128), attn_gain[None], ffn_gain[None], qkv_weight, output_weight,
+        tokens, positions.reshape(8, 128), attn_gain, ffn_gain, qkv_weight, output_weight,
         gate_weight, up_weight, down_weight, cotangent,
     )
     s = jax.ShapeDtypeStruct

time: 206 us -> 204 us (level)
  no operation moved by 1% of the time
where the time goes in v7:
time: 204 us; the launch traced here: 201 us
  Pallas kernels  200 us (98%)
    pallas_call x1, Pallas kernels, run_layer(): pl.pallas_call(layer_kernel, out_shape=outs, in_specs=[ANY] * 2 + [VM] *...  196 us
    pallas_call x1, Pallas kernels, per_device(): pl.pallas_call(outputs_kernel, out_shape=[s(shape, f32) for shape in shap...  4.15 us

profile of v7, /device:TPU:25, one launch (start us, length us, event | category | flops | bytes accessed | tf_op | source)
XLA Modules:
  0.0 200.5 jit_solution(15349448479363472158)
XLA Ops:
  0.6 195.7 %layer.1 = (f32[512,384]{1,0:T(8,128)}, f32[512,384]{1,0:T(8,128)}, f32[10,8,384]{2,1,0:T(8,128)}, bf16[2,2,96,384]{3,2,1,0:T(8,128)(2,1)}, bf16[2,2,48,384]{3,2...) custom-call(bf16[512,384]{1,0:T(8,128)(2,1)} %tokens.1, ...), custom_call_target="tpu_custom_call" | custom-call | tf_op jit(solution)/shard_map/layer/pallas_call | solution.py:1079
  196.4 4.2 %outputs.1 = (f32[512,384]{1,0:T(8,128)}, f32[512,384]{1,0:T(8,128)}, f32[384]{0:T(512)}, f32[384,384]{1,0:T(8,128)}, f32[192,384]{1,0:T(8,128)}, /*index=5*/f32...) custom-call(f32[512,384]{1,0:T(8,128)} %get-tuple-element.17.mixed, ...), custom_call_target="tpu_custom_call" | custom-call | tf_op jit(solution)/shard_map/outputs/pallas_call | solution.py:1126
